TPU v7x, 256 devices: a whole 4x4x8 slice. The times are simulated.
256 devices in a mesh: lat: 32 (over x, z_lo, core), layer: 8 (over z_hi, y).
Axes of the slice: x: 4, y: 4, z: 8 (z_hi: 2, z_lo: 4; z = z_hi * 4 + z_lo), core: 2. Of those that a mesh axis runs over, the one named last changes fastest.
Arguments:
- streams: bfloat16 [256, 8, 1792], P(None, 'layer'), may hold values from -8 to 8
- enc_weight: bfloat16 [8, 1792, 16384], P('layer', None, 'lat'), may hold values from -0.046875 to 0.046875
- enc_bias: float32 [16384], P('lat'), may hold values from -3 to 3
- dec_weight: bfloat16 [16384, 8, 1792], P('lat', 'layer'), may hold values from -0.125 to 0.125
- dec_bias: float32 [8, 1792], P('layer'), may hold values from -3 to 3
- active: int32 [256, 16384], P(None, 'lat'), may hold values 0 or 1
- bounds: int32 [5], replicated, may hold values from 1 to 16384, as said below
- first_moment: bfloat16 [8, 1792, 16384], P('layer', None, 'lat'), may hold values from -3 to 3
- second_moment: bfloat16 [8, 1792, 16384], P('layer', None, 'lat'), may hold values from 0.049804688 to 2
Outputs:
- new_first: bfloat16 [8, 1792, 16384], P('layer', None, 'lat')
- new_second: bfloat16 [8, 1792, 16384], P('layer', None, 'lat')
- loss_value: float32 [], replicated
- grad_norm: float32 [], replicated
Inputs may be any that keep to these rules, and one draw needn't show every extreme that they name: Strictly increasing, the last equal to 16384; latent j lies in prefix k when j < bounds[k].
All inputs are finite; a program needn't handle non-finite values. No bound on the sum of `active` on one device may be relied on, other than what follows from the above.
Results may differ from a plain program's by a relative error of at most 0.002.
Values may be sent and summed in bfloat16 or wider, within the bound.
No kernel may reach another device: no remote copies, remote signals or barrier semaphores. Data moves between devices by JAX's collectives and lax.ppermute only.
A program may use at most 128 MiB of HBM per device.

v0:
```python
import math

import jax
import jax.numpy as jnp
from jax import lax
from jax.sharding import PartitionSpec as P


def on_device(
    streams, enc_weight, enc_bias, dec_weight, dec_bias, active, bounds, first_moment, second_moment
):
    lat_count = lax.axis_size("lat")
    layer_count = lax.axis_size("layer")
    tokens_here = streams.shape[0]
    width = streams.shape[2]
    feats_here = enc_weight.shape[2]
    groups = bounds.shape[0]
    layer_in = streams[:, 0, :]
    enc_local = enc_weight[0]
    dec_local = dec_weight[:, 0, :]
    latent_ids = lax.axis_index("lat") * feats_here + lax.iota(jnp.int32, feats_here)
    prefix_mask = (latent_ids[None, :] < bounds[:, None]).astype(jnp.float32)
    gate_mask = active.astype(jnp.float32)
    partial_pre = jnp.dot(layer_in, enc_local, preferred_element_type=jnp.float32)
    pre_acts = lax.psum(partial_pre, "layer") + enc_bias
    features = (pre_acts * gate_mask).astype(jnp.bfloat16)
    total_rows = groups * tokens_here
    masked = (features[None, :, :] * prefix_mask[:, None, :].astype(jnp.bfloat16)).reshape(
        total_rows, feats_here
    )
    inputs_wide = layer_in.astype(jnp.float32)
    partial_recon = jnp.dot(masked, dec_local, preferred_element_type=jnp.float32)
    recon = lax.psum(partial_recon, "lat")
    residuals = recon.reshape(groups, tokens_here, width) + dec_bias[0] - inputs_wide[None]
    first_lat = (lax.axis_index("lat") == 0).astype(jnp.float32)
    loss_term = jnp.sum(residuals * residuals) * first_lat
    grad_err = (2.0 * residuals).astype(jnp.bfloat16).reshape(total_rows, width)
    back = lax.dot_general(
        grad_err, dec_local, (((1,), (1,)), ((), ())), preferred_element_type=jnp.float32
    )
    partial_dfeat = jnp.sum(
        back.reshape(groups, tokens_here, feats_here) * prefix_mask[:, None, :], axis=0
    )
    dfeat = lax.psum(partial_dfeat, "layer")
    dpre = (dfeat * gate_mask).astype(jnp.bfloat16)
    grad_enc = lax.dot_general(
        layer_in, dpre, (((0,), (0,)), ((), ())), preferred_element_type=jnp.float32
    )
    grad_dec = lax.dot_general(
        masked, grad_err, (((0,), (0,)), ((), ())), preferred_element_type=jnp.float32
    )
    squares = jnp.sum(grad_enc * grad_enc) + jnp.sum(grad_dec * grad_dec)
    loss_total = lax.psum(loss_term, ("lat", "layer"))
    norm_total = lax.psum(squares, ("lat", "layer"))
    grad_norm = jnp.sqrt(norm_total)
    limit = math.sqrt(2.0 * layer_count * width * feats_here * lat_count)
    factor = limit / jnp.maximum(grad_norm, limit)
    clipped = factor * grad_enc[None]
    new_first = (0.9 * first_moment.astype(jnp.float32) + 0.1 * clipped).astype(jnp.bfloat16)
    new_second = (0.95 * second_moment.astype(jnp.float32) + 0.05 * clipped * clipped).astype(
        jnp.bfloat16
    )
    loss_value = loss_total / (tokens_here * layer_count * width)
    return (new_first, new_second, loss_value, grad_norm)


def solution(mesh):
    in_specs = (
        P(None, "layer", None),
        P("layer", None, "lat"),
        P("lat"),
        P("lat", "layer", None),
        P("layer", None),
        P(None, "lat"),
        P(),
        P("layer", None, "lat"),
        P("layer", None, "lat"),
    )
    out_specs = (P("layer", None, "lat"), P("layer", None, "lat"), P(), P())
    return jax.shard_map(
        on_device, mesh=mesh, in_specs=in_specs, out_specs=out_specs, check_vma=False
    )
```

profile of v0, /device:TPU:1, one launch (start us, length us, event | category | flops | bytes accessed | tf_op | source)
XLA Modules:
  0.0 666.7 jit_solution(1373607043527091749)
XLA Ops:
  7.2 0.0 copy-start
  7.2 0.0 copy-start.5
  7.2 0.0 copy-start.4
  7.2 0.0 copy-start.2
  7.2 0.0 all-reduce.5.cloned.1.call-start
  7.3 3.4 fusion.13
  10.6 0.0 all-reduce.5.cloned.1.call-update
  10.6 0.0 all-reduce.7.cloned.1.call-start
  10.7 0.0 copy-done.5
  10.7 0.7 fusion.20
  11.4 107.1 %all-reduce.5.cloned.1.call-done = f32[256,512]{1,0:T(8,128)} async-done(((f32[256,512]{1,0:T(8,128)}), f32[256,512]{1,0:T(8,128)}) %all-reduce.5.cloned.1.call-update) | async-done | bytes 524304 | tf_op jit(solution)/shard_map/psum | solution.py:25
  118.5 0.0 copy-done.4
  118.5 0.0 copy-done.2
  118.5 1.2 multiply_convert_fusion.6
  119.7 0.1 broadcast_multiply_fusion
  119.8 0.0 copy-done
  119.8 6.1 fusion.11
  125.9 0.0 all-reduce.7.cloned.1.call-update
  126.0 0.0 copy-start.1
  126.0 0.2 all-reduce.9.cloned.1.call-start
  126.2 3.8 copy.23
  130.0 0.7 reduce.2
  130.8 0.0 copy-done.1
  130.8 1.3 bitcast_convert_fusion
  132.1 308.9 %all-reduce.7.cloned.1.call-done = f32[1280,1792]{1,0:T(8,128)} async-done(((f32[1280,1792]{1,0:T(8,128)}), f32[1280,1792]{1,0:T(8,128)}) %all-reduce.7.cloned.1.call-update) | async-done | bytes 9175056 | tf_op jit(solution)/shard_map/psum | solution.py:33
  441.1 0.0 copy-start.3
  441.1 7.3 %multiply_reduce_fusion = (f32[]{:T(128)}, bf16[1280,1792]{1,0:T(8,128)(2,1)S(1)}) fusion(f32[1280,1792]{1,0:T(8,128)} %all-reduce.7.cloned.1.call-done, f32[256,1792]{1,0:T(8,128)} %bitcast_convert_fusion, f32[1792]{0:T(1024)S(1)} %reduce.2), kind=kLoop, calls=%fused_computation.1 | loop fusion | flops 13762559 | bytes 15604740 | tf_op jit(solution)/shard_map/reduce_sum | solution.py:36
  448.4 0.0 copy-done.3
  448.4 3.4 multiply_reduce_fusion.2
  451.7 0.0 all-reduce.9.cloned.1.call-update
  452.4 7.9 %fusion.8 = f32[]{:T(128)} fusion(f32[5,256,1792]{2,1,0:T(8,128)} %bitcast.49, f32[1792]{0:T(1024)S(1)} %reduce.2, f32[256,1792]{1,0:T(8,128)} %bitcast_convert_fusion, bf16[5,512]{1,0:T(8,128)(2,1)S(1)} %get-tuple-element.22, bf16[256,512]{1,0:T(8,128)(2,1)S(1)} %multiply_convert_fusion.6), kind=kOutput, calls=%fused_computation.16 | convolution fusion | flops 2360475648 | bytes 11284484 | tf_op jit(solution)/shard_map/dot_general | solution.py:49
  460.3 94.1 %all-reduce.9.cloned.1.call-done = f32[256,512]{1,0:T(8,128)} async-done(((f32[256,512]{1,0:T(8,128)}), f32[256,512]{1,0:T(8,128)}) %all-reduce.9.cloned.1.call-update) | async-done | bytes 524304 | tf_op jit(solution)/shard_map/psum | solution.py:44
  554.4 4.1 multiply_reduce_fusion.1
  559.8 3.8 copy.25
  563.6 79.0 %all-reduce = (f32[]{:T(128)}, f32[]{:T(128)}) all-reduce(f32[]{:T(128)S(6)} %add.62, f32[]{:T(128)S(6)} %mul.139), channel_id=1, replica_groups=mesh['lat'=32,'layer'=8] {'lat','layer'}, use_global_device_ids=true, to_apply=%region_6.0 | all-reduce | flops 2 | bytes 16 | tf_op jit(solution)/shard_map/psum | solution.py:54
  643.3 6.4 fusion.6
  649.7 3.8 copy.26
  653.5 3.8 copy.27
  (1 shorter events, 0.0 us)
Async XLA Ops:
  7.2 112.6 %copy-start = (bf16[512,1,1792]{2,0,1:T(8,128)(2,1)S(1)}, bf16[512,1,1792]{2,0,1:T(8,128)(2,1)}, u32[]{:S(2)}) copy-start(bf16[512,1,1792]{2,0,1:T(8,128)(2,1)} %param.12) | copy-start | bytes 5505028
  7.2 3.5 copy-start.5
  7.2 111.3 %copy-start.4 = (f32[512]{0:T(512)S(1)}, f32[512]{0:T(512)}, u32[]{:S(2)}) copy-start(f32[512]{0:T(512)} %param.11) | copy-start | bytes 6148
  7.2 111.3 %copy-start.2 = (s32[256,512]{1,0:T(8,128)S(1)}, s32[256,512]{1,0:T(8,128)}, u32[]{:S(2)}) copy-start(s32[256,512]{1,0:T(8,128)} %param.14) | copy-start | bytes 1572868
  7.2 111.3 %all-reduce.5.cloned.1.call-start = ((), (), s32[]{:S(2)}) async-start(), calls=%async_computation | async-start | bytes 1048576 | tf_op jit(solution)/shard_map/psum | solution.py:25
  10.6 430.4 %all-reduce.7.cloned.1.call-start = ((), (), s32[]{:S(2)}) async-start(), calls=%async_computation.1 | async-start | bytes 18350080 | tf_op jit(solution)/shard_map/psum | solution.py:33
  126.0 4.8 copy-start.1
  126.0 428.4 %all-reduce.9.cloned.1.call-start = ((), (), s32[]{:S(2)}) async-start(), calls=%async_computation.2 | async-start | bytes 1048576 | tf_op jit(solution)/shard_map/psum | solution.py:44
  441.1 7.3 %copy-start.3 = (f32[5,512]{1,0:T(8,128)S(1)}, f32[5,512]{1,0:T(8,128)}, u32[]{:S(2)}) copy-start(f32[5,512]{1,0:T(8,128)} %get-tuple-element.23) | copy-start | bytes 30724
Sparse Core Ops, SparseCore 0:
  11.2 107.2 all-reduce.4
  126.1 314.9 all-reduce.6
  451.9 102.4 all-reduce.8
where the time goes:
time: 667 us
  waiting for transfers between devices  510 us (76%)
  blocking collectives  79 us (12%)
  matrix products  24.9 us (4%)
  between operations  19.3 us (3%)
  other arithmetic  17.6 us (3%)
  local copies, waits for them, and re-layouts  15.3 us (2%)
    psum x1, waiting for transfers between devices, on_device(): recon = lax.psum(partial_recon, 'lat')  309 us
    psum x1, waiting for transfers between devices, on_device(): pre_acts = lax.psum(partial_pre, 'layer') + enc_bias  107 us
    psum x1, waiting for transfers between devices, on_device(): dfeat = lax.psum(partial_dfeat, 'layer')  94.1 us
    psum x1, blocking collectives, on_device(): norm_total = lax.psum(squares, ('lat', 'layer'))  79 us
    unnamed x16, local copies, waits for them, and re-layouts  15.3 us
  transfers between devices with their start and end apart: 3, of which 3 were waited for; matrix products, arithmetic and copies ran while one was open for 2% of the time, Pallas kernels for 0%

commit v1 on v0

v1 whole, which is shorter than its diff:
```python
import math

import jax
import jax.numpy as jnp
from jax import lax
from jax.sharding import PartitionSpec as P

BF16 = jnp.bfloat16
F32 = jnp.float32

NX, NZ, NCORE, NHI, NY = 4, 4, 2, 2, 4
X_SETS = [
    [(x * NZ + z) * NCORE + c for x in range(NX)] for z in range(NZ) for c in range(NCORE)
]
Z_SETS = [
    [(x * NZ + z) * NCORE + c for z in range(NZ)] for x in range(NX) for c in range(NCORE)
]
Y_SETS = [[h * NY + y for y in range(NY)] for h in range(NHI)]
CORE_SWAP = [(i, i ^ 1) for i in range(NX * NZ * NCORE)]
HI_SWAP = [(i, i ^ NY) for i in range(NHI * NY)]


def swap_blocks(blocks, axis, sets):
    return lax.all_to_all(blocks, axis, 0, 0, axis_index_groups=sets)


def gather_blocks(block, axis, sets):
    copies = jnp.broadcast_to(block[None], (len(sets[0]), *block.shape))
    return swap_blocks(copies, axis, sets)


def sum_over_layers(partial):
    rows, feats = partial.shape
    parts = partial.astype(BF16).reshape(NY, rows // NY, feats)
    mine = jnp.sum(swap_blocks(parts, "layer", Y_SETS).astype(F32), axis=0)
    return mine + lax.ppermute(mine, "layer", HI_SWAP)


def on_device(
    streams, enc_weight, enc_bias, dec_weight, dec_bias, active, bounds, first_moment, second_moment
):
    lat_count = lax.axis_size("lat")
    layer_count = lax.axis_size("layer")
    lat = lax.axis_index("lat")
    layer = lax.axis_index("layer")
    tokens = streams.shape[0]
    width = streams.shape[2]
    feats_here = enc_weight.shape[2]
    groups = bounds.shape[0]
    core, zlo, xpos = lat % NCORE, (lat // NCORE) % NZ, lat // (NCORE * NZ)
    ypos = layer % NY
    half = tokens // NCORE
    per_x = half // NX
    per_z = per_x // NZ
    quarter = tokens // NY
    layer_in = streams[:, 0, :]
    enc_local = enc_weight[0]
    dec_local = dec_weight[:, 0, :]

    own_in = lax.dynamic_slice_in_dim(layer_in, core * half, half, 0)
    other_in = lax.dynamic_slice_in_dim(layer_in, (1 - core) * half, half, 0)
    turned_in = jnp.concatenate([own_in, other_in], axis=0)
    gate_start = (ypos * quarter + core * half) % tokens
    gate_mask = lax.dynamic_slice_in_dim(active, gate_start, quarter, 0).astype(F32)

    latent_ids = lat * feats_here + lax.iota(jnp.int32, feats_here)
    seg = jnp.sum((bounds[:, None] <= latent_ids[None, :]).astype(jnp.int32), axis=0)
    chip_feats = NCORE * feats_here
    chip_starts = lax.iota(jnp.int32, lat_count // NCORE) * chip_feats
    chip_first = jnp.sum((bounds[:, None] <= chip_starts[None, :]).astype(jnp.int32), axis=0)
    chip_last = jnp.sum(
        (bounds[:, None] <= chip_starts[None, :] + (chip_feats - 1)).astype(jnp.int32), axis=0
    )
    slots_needed = jnp.max(chip_last - chip_first) + 1
    first_here = lax.dynamic_index_in_dim(chip_first, lat // NCORE, 0, keepdims=False)
    first_by_x = lax.dynamic_index_in_dim(chip_first.reshape(NX, NZ), zlo, 1, keepdims=False)

    partial_pre = jnp.dot(turned_in, enc_local, preferred_element_type=F32)
    pre_acts = sum_over_layers(partial_pre) + enc_bias
    features_mine = (pre_acts * gate_mask).astype(BF16)
    features = gather_blocks(features_mine, "layer", Y_SETS).reshape(tokens, feats_here)

    token_start = core * half + xpos * per_x + zlo * per_z
    stream_rows = lax.dynamic_slice_in_dim(layer_in, token_start, per_z, 0).astype(F32)

    def middle(slots, features, dec_local):
        slot_ids = lax.iota(jnp.int32, slots)
        slot_mask = (seg - first_here)[None, :] == slot_ids[:, None]

        def by_slot(rows):
            spread = rows.reshape(NX, 1, per_x, feats_here)
            kept = jnp.where(slot_mask[None, :, None, :], spread, jnp.zeros((), BF16))
            return kept.reshape(NX * slots * per_x, feats_here)

        own_rows = by_slot(features[:half])
        other_rows = by_slot(features[half:])
        theirs = jnp.dot(other_rows, dec_local, preferred_element_type=F32)
        got = lax.ppermute(theirs, "lat", CORE_SWAP)
        ours = jnp.dot(own_rows, dec_local, preferred_element_type=F32)
        chip_sum = (ours + got).astype(BF16).reshape(NX, slots * per_x, width)
        by_x = swap_blocks(chip_sum, "lat", X_SETS).reshape(NX, slots, per_x, width)
        slot_seg = first_by_x[:, None] + slot_ids[None, :]
        sums = []
        for k in range(groups):
            inside = (slot_seg <= k)[:, :, None, None]
            sums.append(jnp.sum(jnp.where(inside, by_x.astype(F32), 0.0), axis=(0, 1)))
        x_sum = jnp.stack(sums).astype(BF16).reshape(groups, NZ, per_z, width)
        by_z = swap_blocks(x_sum.transpose(1, 0, 2, 3), "lat", Z_SETS)
        recon = jnp.sum(by_z.astype(F32), axis=0)
        residuals = recon + dec_bias[0] - stream_rows[None]
        loss = jnp.sum(residuals * residuals)
        grad_err = (2.0 * residuals).astype(BF16).astype(F32)
        suffix = [grad_err[groups - 1]]
        for k in range(groups - 2, -1, -1):
            suffix.append(suffix[-1] + grad_err[k])
        err_sums = jnp.stack(suffix[::-1]).astype(BF16)

        z_rows = gather_blocks(err_sums, "lat", Z_SETS)
        wanted = jnp.minimum(slot_seg, groups - 1)[:, :, None, None, None]
        picked = jnp.broadcast_to(z_rows[None, None, :, 0], (NX, slots, NZ, per_z, width))
        for k in range(1, groups):
            picked = jnp.where(wanted == k, z_rows[None, None, :, k], picked)
        own_err = swap_blocks(picked.reshape(NX, slots * per_x, width), "lat", X_SETS)
        own_err = own_err.reshape(NX * slots * per_x, width)
        other_err = lax.ppermute(own_err, "lat", CORE_SWAP)

        def back(err):
            out = lax.dot_general(
                err, dec_local, (((1,), (1,)), ((), ())), preferred_element_type=F32
            ).reshape(NX, slots, per_x, feats_here)
            return jnp.sum(
                jnp.where(slot_mask[None, :, None, :], out, 0.0), axis=1
            ).reshape(half, feats_here)

        partial_dfeat = jnp.concatenate([back(own_err), back(other_err)], axis=0)
        dfeat = sum_over_layers(partial_dfeat)
        dpre_mine = (dfeat * gate_mask).astype(BF16)
        grad_dec = lax.dot_general(
            jnp.concatenate([own_rows, other_rows], axis=0),
            jnp.concatenate([own_err, other_err], axis=0),
            (((0,), (0,)), ((), ())),
            preferred_element_type=F32,
        )
        return dpre_mine, loss, jnp.sum(grad_dec * grad_dec)

    choices = sorted({min(2, groups), min(3, groups), groups})
    which = sum((slots_needed > c).astype(jnp.int32) for c in choices[:-1])
    dpre_mine, loss_part, dec_squares = lax.switch(
        which,
        [lambda f, d, s=s: middle(s, f, d) for s in choices],
        features,
        dec_local,
    )

    dpre = gather_blocks(dpre_mine, "layer", Y_SETS).reshape(tokens, feats_here)
    grad_enc = lax.dot_general(
        turned_in, dpre, (((0,), (0,)), ((), ())), preferred_element_type=F32
    )
    squares = jnp.sum(grad_enc * grad_enc) + dec_squares
    lanes = lax.iota(jnp.int32, 128)
    row = jnp.where(lanes == 0, squares, jnp.where(lanes == 1, loss_part, 0.0))
    rows = jnp.broadcast_to(row[None], (lat_count * layer_count, 128))
    totals = jnp.sum(lax.all_to_all(rows, ("lat", "layer"), 0, 0), axis=0)
    norm_total, loss_total = totals[0], totals[1]
    grad_norm = jnp.sqrt(norm_total)
    limit = math.sqrt(2.0 * layer_count * width * feats_here * lat_count)
    factor = limit / jnp.maximum(grad_norm, limit)
    clipped = factor * grad_enc[None]
    new_first = (0.9 * first_moment.astype(F32) + 0.1 * clipped).astype(BF16)
    new_second = (0.95 * second_moment.astype(F32) + 0.05 * clipped * clipped).astype(BF16)
    loss_value = loss_total / (tokens * layer_count * width)
    return (new_first, new_second, loss_value, grad_norm)


def solution(mesh):
    in_specs = (
        P(None, "layer", None),
        P("layer", None, "lat"),
        P("lat"),
        P("lat", "layer", None),
        P("layer", None),
        P(None, "lat"),
        P(),
        P("layer", None, "lat"),
        P("layer", None, "lat"),
    )
    out_specs = (P("layer", None, "lat"), P("layer", None, "lat"), P(), P())
    return jax.shard_map(
        on_device, mesh=mesh, in_specs=in_specs, out_specs=out_specs, check_vma=False
    )
```

time: 667 us -> 221 us (0.33)
  waiting for transfers between devices: 510 us -> 63.8 us
  starting transfers between devices: 0.3 us -> 40 us
  blocking collectives: 79 us -> 61.1 us
  between operations: 19.3 us -> 6.28 us
  matrix products: 24.9 us -> 12.9 us
    psum x3 -> x0, waiting for transfers between devices: 510 us -> none  [the longest x1 309 us: on_device(): recon = lax.psum(partial_recon, 'lat')]
    psum x1 -> x0, blocking collectives: 79 us -> none  [on_device(): norm_total = lax.psum(squares, ('lat', 'layer'))]
    all_to_all x0 -> x4, blocking collectives: none -> 61.1 us  [the longest x3 36.4 us: swap_blocks(): return lax.all_to_all(blocks, axis, 0, 0, axis_index_groups=sets)]
    all_to_all x0 -> x5, waiting for transfers between devices: none -> 56 us  [swap_blocks(): return lax.all_to_all(blocks, axis, 0, 0, axis_index_groups=sets)]
    all_to_all x0 -> x5, starting transfers between devices: none -> 20.8 us  [swap_blocks(): return lax.all_to_all(blocks, axis, 0, 0, axis_index_groups=sets)]
    ppermute x0 -> x4, starting transfers between devices: none -> 19.1 us  [the longest x2 11.9 us: sum_over_layers(): return mine + lax.ppermute(mine, 'layer', HI_SWAP)]
    unnamed x16 -> x18, local copies, waits for them, and re-layouts: 15.3 us -> 1.03 us
    dot_general x5 -> x7, matrix products: 24.9 us -> 12.9 us  [the longest x1 4.22 us: on_device(): lax.dot_general(turned_in, dpre, (((0,), (0,)), ((), ())), preferred_elem...]
  transfers between devices with their start and end apart: 3 -> 9, of which waited for: 3 -> 9; matrix products, arithmetic and copies ran while one was open for 2% -> 3% of each run, Pallas kernels for 0% -> 0%
where the time goes in v1:
time: 221 us; the launch traced here: 219 us
  waiting for transfers between devices  63.8 us (29%)
  blocking collectives  61.1 us (28%)
  starting transfers between devices  40 us (18%)
  other arithmetic  20.6 us (9%)
  local copies, waits for them, and re-layouts  13.1 us (6%)
  matrix products  12.9 us (6%)
  between operations  6.28 us (3%)
    all_to_all x5, waiting for transfers between devices, swap_blocks(): return lax.all_to_all(blocks, axis, 0, 0, axis_index_groups=sets)  56 us
    all_to_all x3, blocking collectives, swap_blocks(): return lax.all_to_all(blocks, axis, 0, 0, axis_index_groups=sets)  36.4 us
    all_to_all x1, blocking collectives, on_device(): totals = jnp.sum(lax.all_to_all(rows, ('lat', 'layer'), 0, 0), axis=0)  24.6 us
    all_to_all x5, starting transfers between devices, swap_blocks(): return lax.all_to_all(blocks, axis, 0, 0, axis_index_groups=sets)  20.8 us
    ppermute x2, starting transfers between devices, sum_over_layers(): return mine + lax.ppermute(mine, 'layer', HI_SWAP)  11.9 us
    reduce_sum x6, other arithmetic, middle(): sums.append(jnp.sum(jnp.where(inside, by_x.astype(F32), 0.0), axis=(0, 1)))  8.37 us
    convert_element_type x1, other arithmetic, on_device(): (0.95 * second_moment.astype(F32) + 0.05 * clipped * clipped).astype(BF16)  6.46 us
    ppermute x1, starting transfers between devices, middle(): got = lax.ppermute(theirs, 'lat', CORE_SWAP)  4.87 us
  transfers between devices with their start and end apart: 9, of which 9 were waited for; matrix products, arithmetic and copies ran while one was open for 3% of the time, Pallas kernels for 0%

profile of v1, /device:TPU:1, one launch (start us, length us, event | category | flops | bytes accessed | tf_op | source)
XLA Modules:
  0.0 218.6 jit_solution(18291955904238265668)
XLA Ops:
  0.7 1.4 dynamic-slice_bitcast_fusion.1
  2.4 1.3 fusion.125
  3.8 5.2 %all-to-all-start.15 = ((bf16[4,64,512]{2,1,0:T(8,128)(2,1)}), bf16[4,64,512]{2,1,0:T(8,128)(2,1)S(1)}, u32[]{:S(2)}, u32[]{:S(2)}) async-start(bf16[4,64,512]{2,1,0:T(8,128)(2,1)} %bitcast.121), calls=%async_computation.15 | async-start | bytes 524288 | tf_op jit(solution)/shard_map/all_to_all | solution.py:24
  9.7 4.8 %all-to-all-done.15 = bf16[4,64,512]{2,1,0:T(8,128)(2,1)S(1)} async-done(((bf16[4,64,512]{2,1,0:T(8,128)(2,1)}), bf16[4,64,512]{2,1,0:T(8,128)(2,1)S(1)}, u32[]{:S(2)}, u32[]{:S(2)}) %all-to-all-start.15) | async-done | bytes 262176 | tf_op jit(solution)/shard_map/all_to_all | solution.py:24
  14.5 7.0 %collective-permute-start.9 = (f32[64,512]{1,0:T(8,128)S(1)}, f32[64,512]{1,0:T(8,128)S(1)}, u32[]{:S(2)}, u32[]{:S(2)}) collective-permute-start(f32[64,512]{1,0:T(8,128)S(1)} %convert_reduce_fusion.6), channel_id=1, source_target_pairs={{0,4},{1,5},{2,6},{3,7},{4,0},{5,1},{6,2},{7,3},{8,12},{9,13},{10,... | collective-permute-start | bytes 393224 | tf_op jit(solution)/shard_map/ppermute | solution.py:36
  23.1 0.9 collective-permute-done.9
  24.0 0.9 multiply_convert_fusion.3
  24.9 0.7 broadcast_in_dim.701
  25.7 3.4 %all-to-all-start.16 = ((bf16[4,64,512]{2,1,0:T(8,128)(2,1)}), bf16[4,64,512]{2,1,0:T(8,128)(2,1)S(1)}, u32[]{:S(2)}, u32[]{:S(2)}) async-start(bf16[4,64,512]{2,1,0:T(8,128)(2,1)} %broadcast_in_dim.701), calls=%async_computation.16 | async-start | bytes 524288 | tf_op jit(solution)/shard_map/all_to_all | solution.py:24
  29.1 0.8 bitcast_convert_fusion
  29.8 4.7 %all-to-all-done.16 = bf16[4,64,512]{2,1,0:T(8,128)(2,1)S(1)} async-done(((bf16[4,64,512]{2,1,0:T(8,128)(2,1)}), bf16[4,64,512]{2,1,0:T(8,128)(2,1)S(1)}, u32[]{:S(2)}, u32[]{:S(2)}) %all-to-all-start.16) | async-done | bytes 262176 | tf_op jit(solution)/shard_map/all_to_all | solution.py:24
  34.6 133.0 %conditional.2 = (bf16[64,512]{1,0:T(8,128)(2,1)S(1)}, f32[]{:T(128)}, f32[]{:T(128)}) conditional(s32[]{:T(128)} %clamp.3, (s32[]{:T(128)}, s32[512]{0:T(512)S(1)}, s32[4]{0:T(128)S(1)}, bf16[256,512]{1,0:T(8,128)(2,1)S(1)}, bf16[512,1792]{1,0:T(8,128)(2,1)S(1)}, /*index=5*/f32[1,1792]{1,0:T(1,128)S(1)}, ...), branch_computations={%region_5.22_spmd, %region_22.39_spmd, %region_39.0_spmd} | conditional | flops 7083123712 | bytes 120340808
  34.6 0.7 broadcast_subtract_fusion.1
  35.4 0.9 fusion.137
  36.3 4.9 %collective-permute-start.3 = (f32[384,1792]{1,0:T(8,128)S(1)}, f32[384,1792]{1,0:T(8,128)S(1)}, u32[]{:S(2)}, u32[]{:S(2)}) collective-permute-start(f32[384,1792]{1,0:T(8,128)S(1)} %fusion.137), channel_id=1, source_target_pairs={{0,8},{8,0},{16,24},{24,16},{32,40},{40,32},{48,56},{56,48},{64,72... | collective-permute-start | bytes 8257544 | tf_op jit(solution)/shard_map/cond/branch_1_fun/ppermute | solution.py:98
  41.2 4.7 %collective-permute-done.3 = f32[384,1792]{1,0:T(8,128)S(1)} collective-permute-done((f32[384,1792]{1,0:T(8,128)S(1)}, f32[384,1792]{1,0:T(8,128)S(1)}, u32[]{:S(2)}, u32[]{:S(2)}) %collective-permute-start.3) | collective-permute-done | bytes 2752544 | tf_op jit(solution)/shard_map/cond/branch_1_fun/ppermute | solution.py:98
  45.9 2.0 fusion.38
  47.9 4.0 %all-to-all-start.5 = ((bf16[4,96,1792]{2,1,0:T(8,128)(2,1)}), bf16[4,96,1792]{2,1,0:T(8,128)(2,1)S(1)}, u32[]{:S(2)}, u32[]{:S(2)}) async-start(bf16[4,96,1792]{2,1,0:T(8,128)(2,1)} %bitcast.239), calls=%async_computation.5 | async-start | bytes 2752512 | tf_op jit(solution)/shard_map/cond/branch_1_fun/all_to_all | solution.py:24
  52.8 17.1 %all-to-all-done.5 = bf16[4,96,1792]{2,1,0:T(8,128)(2,1)S(1)} async-done(((bf16[4,96,1792]{2,1,0:T(8,128)(2,1)}), bf16[4,96,1792]{2,1,0:T(8,128)(2,1)S(1)}, u32[]{:S(2)}, u32[]{:S(2)}) %all-to-all-start.5) | async-done | bytes 1376288 | tf_op jit(solution)/shard_map/cond/branch_1_fun/all_to_all | solution.py:24
  69.9 3.4 %fusion.43 = (f32[96,1792]{1,0:T(8,128)}, f32[96,1792]{1,0:T(8,128)}, f32[96,1792]{1,0:T(8,128)}, f32[96,1792]{1,0:T(8,128)}, f32[96,1792]{1,0:T(8,128)}) fusion(bf16[4,96,1792]{2,1,0:T(8,128)(2,1)S(1)} %all-to-all-done.5, pred[4,96]{1,0:T(4,128)(4,1)S(1)} %broadcast_in_dim.606, pred[4,96]{1,0:T(4,128)(4,1)S(1)} %broadcast_in_dim.597, ...), kind=kLoop, calls=%fused_computation.83 | loop fusion | flops 6709248 | bytes 4818816 | tf_op jit(solution)/shard_map/cond/branch_1_fun/reduce_sum | solution.py:106
  73.3 1.2 reduce_sum.344
  74.6 0.7 bitcast_dynamic-update-slice_fusion.9
  75.3 1.8 reduce_sum.350
  77.1 1.8 reduce_sum.356
  79.0 1.6 bitcast_dynamic-update-slice_fusion.8
  80.5 1.5 bitcast_dynamic-update-slice_fusion.7
  82.1 0.7 bitcast_dynamic-update-slice_fusion.6
  82.7 0.7 bitcast_dynamic-update-slice_fusion.5
  83.4 4.8 %all-to-all-start.6 = ((bf16[4,5,8,1792]{3,2,1,0:T(8,128)(2,1)}), bf16[4,5,8,1792]{3,2,1,0:T(8,128)(2,1)S(1)}, u32[]{:S(2)}, u32[]{:S(2)}) async-start(bf16[4,5,8,1792]{3,2,1,0:T(8,128)(2,1)} %bitcast.300), calls=%async_computation.6 | async-start | bytes 1146880 | tf_op jit(solution)/shard_map/cond/branch_1_fun/all_to_all | solution.py:24
  88.2 15.0 %all-to-all-done.6 = bf16[4,5,8,1792]{3,2,1,0:T(8,128)(2,1)S(1)} async-done(((bf16[4,5,8,1792]{3,2,1,0:T(8,128)(2,1)}), bf16[4,5,8,1792]{3,2,1,0:T(8,128)(2,1)S(1)}, u32[]{:S(2)}, u32[]{:S(2)}) %all-to-all-start.6) | async-done | bytes 573472 | tf_op jit(solution)/shard_map/cond/branch_1_fun/all_to_all | solution.py:24
  103.3 0.7 multiply_reduce_fusion.1
  104.1 0.8 broadcast_in_dim.608
  105.0 3.5 %all-to-all-start.7 = ((bf16[4,5,8,1792]{3,2,1,0:T(8,128)(2,1)}), bf16[4,5,8,1792]{3,2,1,0:T(8,128)(2,1)S(1)}, u32[]{:S(2)}, u32[]{:S(2)}) async-start(bf16[4,5,8,1792]{3,2,1,0:T(8,128)(2,1)} %broadcast_in_dim.608), calls=%async_computation.7 | async-start | bytes 1146880 | tf_op jit(solution)/shard_map/cond/branch_1_fun/all_to_all | solution.py:24
  109.2 14.3 %all-to-all-done.7 = bf16[4,5,8,1792]{3,2,1,0:T(8,128)(2,1)S(1)} async-done(((bf16[4,5,8,1792]{3,2,1,0:T(8,128)(2,1)}), bf16[4,5,8,1792]{3,2,1,0:T(8,128)(2,1)S(1)}, u32[]{:S(2)}, u32[]{:S(2)}) %all-to-all-start.7) | async-done | bytes 573472 | tf_op jit(solution)/shard_map/cond/branch_1_fun/all_to_all | solution.py:24
  123.6 0.7 select_select_fusion.1
  124.3 19.6 %all_to_all.83 = bf16[4,96,1792]{2,1,0:T(8,128)(2,1)S(1)} all-to-all(bf16[4,96,1792]{2,1,0:T(8,128)(2,1)S(1)} %select_select_fusion.1), channel_id=1, replica_groups={{0,64,128,192},{8,72,136,200},{16,80,144,208},{24,88,152,216},{32,96,16..., dimensions={0} | all-to-all | bytes 2752512 | tf_op jit(solution)/shard_map/cond/branch_1_fun/all_to_all | solution.py:24
  143.9 2.4 %collective-permute-start.4 = (bf16[384,1792]{1,0:T(8,128)(2,1)S(1)}, bf16[384,1792]{1,0:T(8,128)(2,1)S(1)}, u32[]{:S(2)}, u32[]{:S(2)}) collective-permute-start(bf16[384,1792]{1,0:T(8,128)(2,1)S(1)} %bitcast.275), channel_id=1, source_target_pairs={{0,8},{8,0},{16,24},{24,16},{32,40},{40,32},{48,56},{56,48},{64,72... | collective-permute-start | bytes 4128776 | tf_op jit(solution)/shard_map/cond/branch_1_fun/ppermute | solution.py:125
  146.3 0.9 fusion.52
  147.2 1.8 collective-permute-done.4
  149.1 0.9 fusion.138
  150.1 8.9 %all_to_all.84 = bf16[4,64,512]{2,1,0:T(8,128)(2,1)S(1)} all-to-all(bf16[4,64,512]{2,1,0:T(8,128)(2,1)S(1)} %bitcast.287), channel_id=1, replica_groups={{0,1,2,3},{4,5,6,7},{8,9,10,11},{12,13,14,15},{16,17,18,19},{20,21,22,2..., dimensions={0} | all-to-all | bytes 524288 | tf_op jit(solution)/shard_map/cond/branch_1_fun/all_to_all | solution.py:24
  159.1 4.8 %collective-permute-start.5 = (f32[64,512]{1,0:T(8,128)S(1)}, f32[64,512]{1,0:T(8,128)S(1)}, u32[]{:S(2)}, u32[]{:S(2)}) collective-permute-start(f32[64,512]{1,0:T(8,128)S(1)} %convert_reduce_fusion.3), channel_id=1, source_target_pairs={{0,4},{1,5},{2,6},{3,7},{4,0},{5,1},{6,2},{7,3},{8,12},{9,13},{10,... | collective-permute-start | bytes 393224 | tf_op jit(solution)/shard_map/cond/branch_1_fun/ppermute | solution.py:36
  163.9 2.7 %fusion.55 = f32[]{:T(128)} fusion(bf16[384,1792]{1,0:T(8,128)(2,1)S(1)} %collective-permute-done.4, bf16[384,1792]{1,0:T(8,128)(2,1)S(1)} %bitcast.277, bf16[384,512]{1,0:T(8,128)(2,1)S(1)} %bitcast.266, bf16[384,512]{1,0:T(8,128)(2,1)S(1)} %bitcast.274), kind=kOutput, calls=%fused_computation.93 | convolution fusion | flops 1418199040 | bytes 3538948 | tf_op jit(solution)/shard_map/cond/branch_1_fun/dot_general | solution.py:138
  168.2 0.9 broadcast_in_dim.702
  169.1 7.9 %all_to_all.87 = bf16[4,64,512]{2,1,0:T(8,128)(2,1)S(1)} all-to-all(bf16[4,64,512]{2,1,0:T(8,128)(2,1)S(1)} %broadcast_in_dim.702), channel_id=1, replica_groups={{0,1,2,3},{4,5,6,7},{8,9,10,11},{12,13,14,15},{16,17,18,19},{20,21,22,2..., dimensions={0} | all-to-all | bytes 524288 | tf_op jit(solution)/shard_map/all_to_all | solution.py:24
  177.0 4.2 %multiply_reduce_fusion.3 = (f32[]{:T(128)}, f32[1792,512]{1,0:T(8,128)}) fusion(bf16[256,512]{1,0:T(8,128)(2,1)S(1)} %bitcast.313, bf16[128,1792]{1,0:T(8,128)(2,1)} %copy-done.23, bf16[128,1792]{1,0:T(8,128)(2,1)} %copy-done.22), kind=kOutput, calls=%fused_computation.219 | convolution fusion | flops 473432064 | bytes 4849668 | tf_op jit(solution)/shard_map/dot_general | solution.py:156
  183.2 24.6 %all_to_all.88 = f32[256,1,128]{2,1,0:T(1,128)S(1)} all-to-all(f32[256,1,128]{2,1,0:T(1,128)S(1)} %broadcast_in_dim.706), channel_id=1, replica_groups=mesh['lat'=32,'layer'=8] {'lat','layer'}, dimensions={0} | all-to-all | bytes 262144 | tf_op jit(solution)/shard_map/all_to_all | solution.py:163
  209.8 6.5 %fusion.121 = (bf16[1,1792,512]{2,1,0:T(8,128)(2,1)}, bf16[1,1792,512]{2,1,0:T(8,128)(2,1)}) fusion(bf16[1,1792,512]{2,1,0:T(8,128)(2,1)} %param.20, f32[1792,512]{1,0:T(8,128)} %get-tuple-element.178, f32[]{:T(128)S(6)} %div.30, bf16[1,1792,512]{2,1,0:T(8,128)(2,1)} %param.19), kind=kLoop, calls=%fused_computation.216 | loop fusion | flops 11010048 | bytes 11010052 | tf_op jit(solution)/shard_map/convert_element_type | solution.py:170
  (89 shorter events, 6.8 us)
Async XLA Ops:
  0.6 1.8 copy-start
  2.0 1.7 copy-start.22
  2.0 1.7 copy-start.23
  2.4 6.5 %copy-start.27 = (s32[5]{0:T(128)S(1)}, s32[5]{0:T(128)}, u32[]{:S(2)}) copy-start(s32[5]{0:T(128)} %param.18) | copy-start | bytes 64
  2.4 21.6 %copy-start.26 = (f32[512]{0:T(512)S(1)}, f32[512]{0:T(512)}, u32[]{:S(2)}) copy-start(f32[512]{0:T(512)} %param.14) | copy-start | bytes 6148
  3.8 30.8 %copy-start.2 = (bf16[512,1,1792]{2,0,1:T(8,128)(2,1)S(1)}, bf16[512,1,1792]{2,0,1:T(8,128)(2,1)}, u32[]{:S(2)}) copy-start(bf16[512,1,1792]{2,0,1:T(8,128)(2,1)} %param.15) | copy-start | bytes 5505028
  3.8 30.8 %copy-start.25 = (f32[1,1792]{1,0:T(1,128)S(1)}, f32[1,1792]{1,0:T(1,128)}, u32[]{:S(2)}) copy-start(f32[1,1792]{1,0:T(1,128)} %param.16) | copy-start | bytes 21508
  3.8 10.7 %all-to-all-start.15 = ((bf16[4,64,512]{2,1,0:T(8,128)(2,1)}), bf16[4,64,512]{2,1,0:T(8,128)(2,1)S(1)}, u32[]{:S(2)}, u32[]{:S(2)}) async-start(bf16[4,64,512]{2,1,0:T(8,128)(2,1)} %bitcast.121), calls=%async_computation.15 | async-start | bytes 524288 | tf_op jit(solution)/shard_map/all_to_all | solution.py:24
  14.5 9.5 %collective-permute-start.9 = (f32[64,512]{1,0:T(8,128)S(1)}, f32[64,512]{1,0:T(8,128)S(1)}, u32[]{:S(2)}, u32[]{:S(2)}) collective-permute-start(f32[64,512]{1,0:T(8,128)S(1)} %convert_reduce_fusion.6), channel_id=1, source_target_pairs={{0,4},{1,5},{2,6},{3,7},{4,0},{5,1},{6,2},{7,3},{8,12},{9,13},{10,... | collective-permute-start | bytes 393224 | tf_op jit(solution)/shard_map/ppermute | solution.py:36
  25.7 8.9 %all-to-all-start.16 = ((bf16[4,64,512]{2,1,0:T(8,128)(2,1)}), bf16[4,64,512]{2,1,0:T(8,128)(2,1)S(1)}, u32[]{:S(2)}, u32[]{:S(2)}) async-start(bf16[4,64,512]{2,1,0:T(8,128)(2,1)} %broadcast_in_dim.701), calls=%async_computation.16 | async-start | bytes 524288 | tf_op jit(solution)/shard_map/all_to_all | solution.py:24
  34.6 1.7 copy-start.11
  35.4 0.9 copy-start.9
  35.4 10.5 %copy-start.16 = (bf16[4,3,32,512]{3,2,1,0:T(8,128)(2,1)}, bf16[4,3,32,512]{3,2,1,0:T(8,128)(2,1)S(1)}, u32[]{:S(2)}) copy-start(bf16[4,3,32,512]{3,2,1,0:T(8,128)(2,1)S(1)} %get-tuple-element.140) | copy-start | bytes 1179652 | tf_op jit(solution)/shard_map/conditional
  36.3 9.6 %collective-permute-start.3 = (f32[384,1792]{1,0:T(8,128)S(1)}, f32[384,1792]{1,0:T(8,128)S(1)}, u32[]{:S(2)}, u32[]{:S(2)}) collective-permute-start(f32[384,1792]{1,0:T(8,128)S(1)} %fusion.137), channel_id=1, source_target_pairs={{0,8},{8,0},{16,24},{24,16},{32,40},{40,32},{48,56},{56,48},{64,72... | collective-permute-start | bytes 8257544 | tf_op jit(solution)/shard_map/cond/branch_1_fun/ppermute | solution.py:98
  47.9 22.1 %all-to-all-start.5 = ((bf16[4,96,1792]{2,1,0:T(8,128)(2,1)}), bf16[4,96,1792]{2,1,0:T(8,128)(2,1)S(1)}, u32[]{:S(2)}, u32[]{:S(2)}) async-start(bf16[4,96,1792]{2,1,0:T(8,128)(2,1)} %bitcast.239), calls=%async_computation.5 | async-start | bytes 2752512 | tf_op jit(solution)/shard_map/cond/branch_1_fun/all_to_all | solution.py:24
  73.3 5.6 %copy-start.6 = (f32[96,1792]{1,0:T(8,128)S(1)}, f32[96,1792]{1,0:T(8,128)}, u32[]{:S(2)}) copy-start(f32[96,1792]{1,0:T(8,128)} %get-tuple-element.94) | copy-start | bytes 2064388 | tf_op jit(solution)/shard_map/conditional
  73.3 5.6 %copy-start.5 = (f32[96,1792]{1,0:T(8,128)S(1)}, f32[96,1792]{1,0:T(8,128)}, u32[]{:S(2)}) copy-start(f32[96,1792]{1,0:T(8,128)} %get-tuple-element.91) | copy-start | bytes 2064388 | tf_op jit(solution)/shard_map/conditional
  83.4 19.8 %all-to-all-start.6 = ((bf16[4,5,8,1792]{3,2,1,0:T(8,128)(2,1)}), bf16[4,5,8,1792]{3,2,1,0:T(8,128)(2,1)S(1)}, u32[]{:S(2)}, u32[]{:S(2)}) async-start(bf16[4,5,8,1792]{3,2,1,0:T(8,128)(2,1)} %bitcast.300), calls=%async_computation.6 | async-start | bytes 1146880 | tf_op jit(solution)/shard_map/cond/branch_1_fun/all_to_all | solution.py:24
  105.0 18.5 %all-to-all-start.7 = ((bf16[4,5,8,1792]{3,2,1,0:T(8,128)(2,1)}), bf16[4,5,8,1792]{3,2,1,0:T(8,128)(2,1)S(1)}, u32[]{:S(2)}, u32[]{:S(2)}) async-start(bf16[4,5,8,1792]{3,2,1,0:T(8,128)(2,1)} %broadcast_in_dim.608), calls=%async_computation.7 | async-start | bytes 1146880 | tf_op jit(solution)/shard_map/cond/branch_1_fun/all_to_all | solution.py:24
  143.9 5.1 %collective-permute-start.4 = (bf16[384,1792]{1,0:T(8,128)(2,1)S(1)}, bf16[384,1792]{1,0:T(8,128)(2,1)S(1)}, u32[]{:S(2)}, u32[]{:S(2)}) collective-permute-start(bf16[384,1792]{1,0:T(8,128)(2,1)S(1)} %bitcast.275), channel_id=1, source_target_pairs={{0,8},{8,0},{16,24},{24,16},{32,40},{40,32},{48,56},{56,48},{64,72... | collective-permute-start | bytes 4128776 | tf_op jit(solution)/shard_map/cond/branch_1_fun/ppermute | solution.py:125
  150.0 14.0 %copy-start.10 = (bf16[4,3,32,512]{3,2,1,0:T(8,128)(2,1)S(1)}, bf16[4,3,32,512]{3,2,1,0:T(8,128)(2,1)}, u32[]{:S(2)}) copy-start(bf16[4,3,32,512]{3,2,1,0:T(8,128)(2,1)} %copy-done.9) | copy-start | bytes 1179652 | tf_op jit(solution)/shard_map/conditional
  150.0 13.9 %copy-start.17 = (bf16[4,3,32,512]{3,2,1,0:T(8,128)(2,1)S(1)}, bf16[4,3,32,512]{3,2,1,0:T(8,128)(2,1)}, u32[]{:S(2)}) copy-start(bf16[4,3,32,512]{3,2,1,0:T(8,128)(2,1)} %copy-done.16) | copy-start | bytes 1179652 | tf_op jit(solution)/shard_map/conditional
  159.1 7.9 %copy-start.12 = (f32[64,512]{1,0:T(8,128)S(1)}, f32[64,512]{1,0:T(8,128)}, u32[]{:S(2)}) copy-start(f32[64,512]{1,0:T(8,128)} %copy-done.11) | copy-start | bytes 393220 | tf_op jit(solution)/shard_map/conditional
  159.1 7.9 %collective-permute-start.5 = (f32[64,512]{1,0:T(8,128)S(1)}, f32[64,512]{1,0:T(8,128)S(1)}, u32[]{:S(2)}, u32[]{:S(2)}) collective-permute-start(f32[64,512]{1,0:T(8,128)S(1)} %convert_reduce_fusion.3), channel_id=1, source_target_pairs={{0,4},{1,5},{2,6},{3,7},{4,0},{5,1},{6,2},{7,3},{8,12},{9,13},{10,... | collective-permute-start | bytes 393224 | tf_op jit(solution)/shard_map/cond/branch_1_fun/ppermute | solution.py:36
  167.6 0.6 copy-start.24
  209.8 6.5 %copy-start.1 = (bf16[1,1792,512]{2,1,0:T(8,128)(2,1)S(1)}, bf16[1,1792,512]{2,1,0:T(8,128)(2,1)}, u32[]{:S(2)}) copy-start(bf16[1,1792,512]{2,1,0:T(8,128)(2,1)} %param.13) | copy-start | bytes 5505028

commit v2 on v1

v2 whole, which is shorter than its diff:
```python
import functools
import math

import jax
import jax.numpy as jnp
from jax import lax
from jax.experimental import pallas as pl
from jax.experimental.pallas import tpu as pltpu
from jax.sharding import PartitionSpec as P

BF16 = jnp.bfloat16
F32 = jnp.float32

NX, NZ, NCORE, NHI, NY = 4, 4, 2, 2, 4
CHIPS = NX * NZ
PLANE_SETS = [[chip * NCORE + c for chip in range(CHIPS)] for c in range(NCORE)]
Y_SETS = [[h * NY + y for y in range(NY)] for h in range(NHI)]
CORE_SWAP = [(i, i ^ 1) for i in range(NX * NZ * NCORE)]
HI_SWAP = [(i, i ^ NY) for i in range(NHI * NY)]


def swap_blocks(blocks, axis, sets):
    return lax.all_to_all(blocks, axis, 0, 0, axis_index_groups=sets)


def gather_blocks(block, axis, sets):
    copies = jnp.broadcast_to(block[None], (len(sets[0]), *block.shape))
    return swap_blocks(copies, axis, sets)


def sum_over_layers(partial):
    rows, feats = partial.shape
    parts = partial.astype(BF16).reshape(NY, rows // NY, feats)
    mine = jnp.sum(swap_blocks(parts, "layer", Y_SETS).astype(F32), axis=0)
    return mine + lax.ppermute(mine, "layer", HI_SWAP)


def owner_kernel(slots, groups, seg_ref, got_ref, rows_ref, bias_ref, out_ref, loss_ref, sums, errs):
    sums[...] = jnp.zeros_like(sums)
    for c in range(CHIPS):
        for e in range(slots):
            s = seg_ref[c, e]
            sums[s] += got_ref[c, e].astype(F32)
    recon = jnp.zeros_like(rows_ref)
    loss = jnp.zeros_like(rows_ref)
    grad_err = []
    for k in range(groups):
        recon += sums[k]
        residual = recon + bias_ref[...] - rows_ref[...]
        loss += residual * residual
        grad_err.append((2.0 * residual).astype(BF16).astype(F32))
    total = jnp.zeros_like(rows_ref)
    for k in range(groups - 1, -1, -1):
        total += grad_err[k]
        errs[k] = total.astype(BF16)
    loss_ref[0, 0] = jnp.sum(loss)
    for c in range(CHIPS):
        for e in range(slots):
            out_ref[c, e] = errs[seg_ref[c, e]]


def owner_step(slot_seg, got, rows, bias, groups):
    chips, slots, per, width = got.shape
    vmem = pl.BlockSpec(memory_space=pltpu.VMEM)
    smem = pl.BlockSpec(memory_space=pltpu.SMEM)
    return pl.pallas_call(
        functools.partial(owner_kernel, slots, groups),
        out_shape=(
            jax.ShapeDtypeStruct(got.shape, BF16),
            jax.ShapeDtypeStruct((1, 1), F32),
        ),
        in_specs=[smem, vmem, vmem, vmem],
        out_specs=(vmem, smem),
        scratch_shapes=[
            pltpu.VMEM((groups, per, width), F32),
            pltpu.VMEM((groups, per, width), BF16),
        ],
        compiler_params=pltpu.CompilerParams(vmem_limit_bytes=24 * 2**20),
    )(slot_seg, got, rows, bias)


def update_kernel(factor_ref, in_ref, dpre_ref, first_ref, second_ref, new_first_ref, new_second_ref):
    grad = lax.dot_general(
        in_ref[...], dpre_ref[...], (((0,), (0,)), ((), ())), preferred_element_type=F32
    )
    clipped = factor_ref[0, 0] * grad
    new_first_ref[...] = (0.9 * first_ref[...].astype(F32) + 0.1 * clipped).astype(BF16)
    new_second_ref[...] = (
        0.95 * second_ref[...].astype(F32) + 0.05 * clipped * clipped
    ).astype(BF16)


def update(factor, layer_in, dpre, first, second):
    tokens, width = layer_in.shape
    feats = dpre.shape[1]
    tile = 256
    tiles = pl.BlockSpec((tile, feats), lambda i: (i, 0))
    return pl.pallas_call(
        update_kernel,
        grid=(width // tile,),
        out_shape=(jax.ShapeDtypeStruct((width, feats), BF16),) * 2,
        in_specs=[
            pl.BlockSpec(memory_space=pltpu.SMEM),
            pl.BlockSpec((tokens, tile), lambda i: (0, i)),
            pl.BlockSpec((tokens, feats), lambda i: (0, 0)),
            tiles,
            tiles,
        ],
        out_specs=(tiles, tiles),
        compiler_params=pltpu.CompilerParams(vmem_limit_bytes=24 * 2**20),
    )(factor, layer_in, dpre, first, second)


def on_device(
    streams, enc_weight, enc_bias, dec_weight, dec_bias, active, bounds, first_moment, second_moment
):
    lat_count = lax.axis_size("lat")
    layer_count = lax.axis_size("layer")
    lat = lax.axis_index("lat")
    layer = lax.axis_index("layer")
    tokens = streams.shape[0]
    width = streams.shape[2]
    feats_here = enc_weight.shape[2]
    groups = bounds.shape[0]
    core, chip = lat % NCORE, lat // NCORE
    ypos = layer % NY
    half = tokens // NCORE
    per = half // CHIPS
    quarter = tokens // NY
    layer_in = streams[:, 0, :]
    enc_local = enc_weight[0]
    dec_local = dec_weight[:, 0, :]

    own_start, other_start = core * half, (1 - core) * half
    own_in = lax.dynamic_slice_in_dim(layer_in, own_start, half, 0)
    other_in = lax.dynamic_slice_in_dim(layer_in, other_start, half, 0)
    turned_in = jnp.concatenate([own_in, other_in], axis=0)
    gate_mask = lax.dynamic_slice_in_dim(active, ypos * quarter, quarter, 0).astype(F32)
    turned_start = (ypos * quarter + own_start) % tokens
    turned_gate = lax.dynamic_slice_in_dim(active, turned_start, quarter, 0).astype(F32)

    latent_ids = lat * feats_here + lax.iota(jnp.int32, feats_here)
    seg = jnp.sum((bounds[:, None] <= latent_ids[None, :]).astype(jnp.int32), axis=0)
    chip_feats = NCORE * feats_here
    chip_starts = lax.iota(jnp.int32, CHIPS) * chip_feats
    chip_first = jnp.sum((bounds[None, :] <= chip_starts[:, None]).astype(jnp.int32), axis=1)
    chip_last = jnp.sum(
        (bounds[None, :] <= chip_starts[:, None] + (chip_feats - 1)).astype(jnp.int32), axis=1
    )
    slots_needed = jnp.max(chip_last - chip_first) + 1
    first_here = lax.dynamic_index_in_dim(chip_first, chip, 0, keepdims=False)

    partial_pre = jnp.dot(layer_in, enc_local, preferred_element_type=F32)
    pre_acts = sum_over_layers(partial_pre) + enc_bias
    features_mine = (pre_acts * gate_mask).astype(BF16)
    features = gather_blocks(features_mine, "layer", Y_SETS).reshape(tokens, feats_here)

    token_start = own_start + chip * per
    stream_rows = lax.dynamic_slice_in_dim(layer_in, token_start, per, 0).astype(F32)
    own_gram = lax.dot_general(
        turned_in, turned_in, (((1,), (1,)), ((), ())), preferred_element_type=F32
    )

    def middle(slots, features, dec_local):
        slot_ids = lax.iota(jnp.int32, slots)
        slot_mask = (seg - first_here)[None, :] == slot_ids[:, None]

        def by_slot(rows):
            spread = rows.reshape(CHIPS, 1, per, feats_here)
            kept = jnp.where(slot_mask[None, :, None, :], spread, jnp.zeros((), BF16))
            return kept.reshape(CHIPS * slots * per, feats_here)

        own_rows = by_slot(lax.dynamic_slice_in_dim(features, own_start, half, 0))
        other_rows = by_slot(lax.dynamic_slice_in_dim(features, other_start, half, 0))
        theirs = jnp.dot(other_rows, dec_local, preferred_element_type=F32)
        got = lax.ppermute(theirs, "lat", CORE_SWAP)
        ours = jnp.dot(own_rows, dec_local, preferred_element_type=F32)
        chip_sum = (ours + got).astype(BF16).reshape(CHIPS, slots, per, width)
        by_chip = swap_blocks(chip_sum, "lat", PLANE_SETS)
        slot_seg = jnp.minimum(chip_first[:, None] + slot_ids[None, :], groups - 1)
        wanted, loss = owner_step(slot_seg, by_chip, stream_rows, dec_bias, groups)
        own_err = swap_blocks(wanted, "lat", PLANE_SETS).reshape(CHIPS * slots * per, width)
        other_err = lax.ppermute(own_err, "lat", CORE_SWAP)

        def back(err):
            out = lax.dot_general(
                err, dec_local, (((1,), (1,)), ((), ())), preferred_element_type=F32
            ).reshape(CHIPS, slots, per, feats_here)
            return jnp.sum(
                jnp.where(slot_mask[None, :, None, :], out, 0.0), axis=1
            ).reshape(half, feats_here)

        partial_dfeat = jnp.concatenate([back(own_err), back(other_err)], axis=0)
        dfeat = sum_over_layers(partial_dfeat)
        dpre_mine = (dfeat * turned_gate).astype(BF16)
        grad_dec = lax.dot_general(
            jnp.concatenate([own_rows, other_rows], axis=0),
            jnp.concatenate([own_err, other_err], axis=0),
            (((0,), (0,)), ((), ())),
            preferred_element_type=F32,
        )
        return dpre_mine, loss[0, 0], jnp.sum(grad_dec * grad_dec)

    choices = sorted({min(2, groups), min(3, groups), groups})
    which = sum((slots_needed > c).astype(jnp.int32) for c in choices[:-1])
    dpre_mine, loss_part, dec_squares = lax.switch(
        which,
        [lambda f, d, s=s: middle(s, f, d) for s in choices],
        features,
        dec_local,
    )

    dpre = gather_blocks(dpre_mine, "layer", Y_SETS).reshape(tokens, feats_here)
    dpre_gram = lax.dot_general(dpre, dpre, (((1,), (1,)), ((), ())), preferred_element_type=F32)
    squares = jnp.sum(own_gram * dpre_gram) + dec_squares
    lanes = lax.iota(jnp.int32, 128)
    row = jnp.where(lanes == 0, squares, jnp.where(lanes == 1, loss_part, 0.0))
    rows = jnp.broadcast_to(row[None], (lat_count * layer_count, 128))
    totals = jnp.sum(lax.all_to_all(rows, ("lat", "layer"), 0, 0), axis=0)
    norm_total, loss_total = totals[0], totals[1]
    grad_norm = jnp.sqrt(norm_total)
    limit = math.sqrt(2.0 * layer_count * width * feats_here * lat_count)
    factor = limit / jnp.maximum(grad_norm, limit)
    new_first, new_second = update(
        factor.reshape(1, 1), turned_in, dpre, first_moment[0], second_moment[0]
    )
    loss_value = loss_total / (tokens * layer_count * width)
    return (new_first[None], new_second[None], loss_value, grad_norm)


def solution(mesh):
    in_specs = (
        P(None, "layer", None),
        P("layer", None, "lat"),
        P("lat"),
        P("lat", "layer", None),
        P("layer", None),
        P(None, "lat"),
        P(),
        P("layer", None, "lat"),
        P("layer", None, "lat"),
    )
    out_specs = (P("layer", None, "lat"), P("layer", None, "lat"), P(), P())
    return jax.shard_map(
        on_device, mesh=mesh, in_specs=in_specs, out_specs=out_specs, check_vma=False
    )
```

time: 221 us -> 182 us (0.82)
  blocking collectives: 61.1 us -> 37 us
  other arithmetic: 20.6 us -> 5.16 us
  starting transfers between devices: 40 us -> 49.4 us
  waiting for transfers between devices: 63.8 us -> 57.2 us
  Pallas kernels: 0 us -> 6.22 us
  matrix products: 12.9 us -> 9.55 us
  local copies, waits for them, and re-layouts: 13.1 us -> 9.77 us
    all_to_all x1 -> x0, blocking collectives: 24.6 us -> none  [on_device(): totals = jnp.sum(lax.all_to_all(rows, ('lat', 'layer'), 0, 0), axis=0)]
    all_to_all x5 -> x4, waiting for transfers between devices: 56 us -> 38 us  [swap_blocks(): return lax.all_to_all(blocks, axis, 0, 0, axis_index_groups=sets)]
    all_to_all x0 -> x1, waiting for transfers between devices: none -> 12.7 us  [on_device(): totals = jnp.sum(lax.all_to_all(rows, ('lat', 'layer'), 0, 0), axis=0)]
    all_to_all x0 -> x1, starting transfers between devices: none -> 12.6 us  [on_device(): totals = jnp.sum(lax.all_to_all(rows, ('lat', 'layer'), 0, 0), axis=0)]
    reduce_sum x9 -> x1, other arithmetic: 9.22 us -> 0.09 us  [on_device(): jnp.sum((bounds[None, :] <= chip_starts[:, None]).astype(jnp.int32), axis=1)]
    pallas_call x0 -> x2, Pallas kernels: none -> 6.22 us  [the longest x1 4.57 us: update(): pl.pallas_call(update_kernel, grid=(width // tile,), out_shape=(jax.Shape...]
    convert_element_type x2, other arithmetic: 7.22 us -> 1.67 us  [the longest x1 0.91 us: on_device(): lax.dynamic_slice_in_dim(active, turned_start, quarter, 0).astype(F32)]
    another operation x22 -> x4, local copies, waits for them, and re-layouts: 5.14 us -> 0.5 us
  transfers between devices with their start and end apart: 9 -> 9, of which waited for: 9 -> 8; matrix products, arithmetic and copies ran while one was open for 3% -> 4% of each run, Pallas kernels for 0% -> 0%
where the time goes in v2:
time: 182 us; the launch traced here: 181 us
  waiting for transfers between devices  57.2 us (31%)
  starting transfers between devices  49.4 us (27%)
  blocking collectives  37 us (20%)
  local copies, waits for them, and re-layouts  9.77 us (5%)
  matrix products  9.55 us (5%)
  between operations  6.43 us (4%)
  Pallas kernels  6.22 us (3%)
  other arithmetic  5.16 us (3%)
    all_to_all x4, waiting for transfers between devices, swap_blocks(): return lax.all_to_all(blocks, axis, 0, 0, axis_index_groups=sets)  38 us
    all_to_all x2, blocking collectives, swap_blocks(): return lax.all_to_all(blocks, axis, 0, 0, axis_index_groups=sets)  37 us
    all_to_all x4, starting transfers between devices, swap_blocks(): return lax.all_to_all(blocks, axis, 0, 0, axis_index_groups=sets)  19.4 us
    all_to_all x1, waiting for transfers between devices, on_device(): totals = jnp.sum(lax.all_to_all(rows, ('lat', 'layer'), 0, 0), axis=0)  12.7 us
    all_to_all x1, starting transfers between devices, on_device(): totals = jnp.sum(lax.all_to_all(rows, ('lat', 'layer'), 0, 0), axis=0)  12.6 us
    ppermute x2, starting transfers between devices, sum_over_layers(): return mine + lax.ppermute(mine, 'layer', HI_SWAP)  11.2 us
    unnamed x16, local copies, waits for them, and re-layouts  4.63 us
    pallas_call x1, Pallas kernels, update(): pl.pallas_call(update_kernel, grid=(width // tile,), out_shape=(jax.Shape...  4.57 us
  transfers between devices with their start and end apart: 9, of which 8 were waited for; matrix products, arithmetic and copies ran while one was open for 4% of the time, Pallas kernels for 0%

profile of v2, /device:TPU:1, one launch (start us, length us, event | category | flops | bytes accessed | tf_op | source)
XLA Modules:
  0.0 181.0 jit_solution(9964686665415345083)
XLA Ops:
  0.7 1.5 copy-done
  2.1 2.5 %fusion.64 = bf16[256,512]{1,0:T(8,128)(2,1)} fusion(bf16[1,1792,512]{2,1,0:T(8,128)(2,1)S(1)} %copy-done, bf16[256,1,1792]{2,0,1:T(8,128)(2,1)} %param.12), kind=kOutput, calls=%fused_computation.86 | convolution fusion | flops 469893120 | bytes 3014656 | tf_op jit(solution)/shard_map/dot_general | solution.py:153
  4.7 5.1 %all-to-all-start.9 = ((bf16[4,64,512]{2,1,0:T(8,128)(2,1)}), bf16[4,64,512]{2,1,0:T(8,128)(2,1)S(1)}, u32[]{:S(2)}, u32[]{:S(2)}) async-start(bf16[4,64,512]{2,1,0:T(8,128)(2,1)} %bitcast.44), calls=%async_computation.9 | async-start | bytes 524288 | tf_op jit(solution)/shard_map/all_to_all | solution.py:23
  9.8 0.1 convert_reduce_fusion.5
  9.9 0.1 convert_reduce_fusion.4
  10.0 5.3 %all-to-all-done.9 = bf16[4,64,512]{2,1,0:T(8,128)(2,1)S(1)} async-done(((bf16[4,64,512]{2,1,0:T(8,128)(2,1)}), bf16[4,64,512]{2,1,0:T(8,128)(2,1)S(1)}, u32[]{:S(2)}, u32[]{:S(2)}) %all-to-all-start.9) | async-done | bytes 262176 | tf_op jit(solution)/shard_map/all_to_all | solution.py:23
  15.4 7.0 %collective-permute-start.9 = (f32[64,512]{1,0:T(8,128)S(1)}, f32[64,512]{1,0:T(8,128)S(1)}, u32[]{:S(2)}, u32[]{:S(2)}) collective-permute-start(f32[64,512]{1,0:T(8,128)S(1)} %convert_reduce_fusion.3), channel_id=1, source_target_pairs={{0,4},{1,5},{2,6},{3,7},{4,0},{5,1},{6,2},{7,3},{8,12},{9,13},{10,... | collective-permute-start | bytes 393224 | tf_op jit(solution)/shard_map/ppermute | solution.py:35
  22.4 0.6 subtract_reduce_fusion
  23.7 0.6 dynamic_slice.45
  24.3 0.9 dynamic-slice_convert_fusion
  25.3 0.9 multiply_convert_fusion
  26.2 0.7 broadcast_in_dim.208
  26.9 3.4 %all-to-all-start.10 = ((bf16[4,64,512]{2,1,0:T(8,128)(2,1)}), bf16[4,64,512]{2,1,0:T(8,128)(2,1)S(1)}, u32[]{:S(2)}, u32[]{:S(2)}) async-start(bf16[4,64,512]{2,1,0:T(8,128)(2,1)} %broadcast_in_dim.208), calls=%async_computation.10 | async-start | bytes 524288 | tf_op jit(solution)/shard_map/all_to_all | solution.py:23
  30.4 0.8 bitcast_convert_fusion
  31.1 4.7 %all-to-all-done.10 = bf16[4,64,512]{2,1,0:T(8,128)(2,1)S(1)} async-done(((bf16[4,64,512]{2,1,0:T(8,128)(2,1)}), bf16[4,64,512]{2,1,0:T(8,128)(2,1)S(1)}, u32[]{:S(2)}, u32[]{:S(2)}) %all-to-all-start.10) | async-done | bytes 262176 | tf_op jit(solution)/shard_map/all_to_all | solution.py:23
  35.9 94.6 %conditional.2 = (bf16[64,512]{1,0:T(8,128)(2,1)S(1)}, f32[]{:T(128)}, f32[]{:T(128)}) conditional(s32[]{:T(128)} %clamp.3, (s32[]{:T(128)}, s32[512]{0:T(512)S(1)}, s32[16]{0:T(128)S(1)}, s32[]{:T(128)}, bf16[256,512]{1,0:T(8,128)(2,1)S(1)}, /*index=5*/bf16[512,1792]{1,0:T(8,128)(2,1)S(1)}, s32[]{:T(128)}, ...), branch_computations={%region_5.10_spmd, %region_10.15_spmd, %region_15.20_spmd} | conditional | flops 7065046016 | bytes 103237032
  35.9 0.5 copy-done.20
  36.4 0.6 broadcast_subtract_fusion
  37.2 0.6 fusion.71
  37.8 4.5 %collective-permute-start = (f32[256,1792]{1,0:T(8,128)S(1)}, f32[256,1792]{1,0:T(8,128)S(1)}, u32[]{:S(2)}, u32[]{:S(2)}) collective-permute-start(f32[256,1792]{1,0:T(8,128)S(1)} %fusion.71), channel_id=1, source_target_pairs={{0,8},{8,0},{16,24},{24,16},{32,40},{40,32},{48,56},{56,48},{64,72... | collective-permute-start | bytes 5505032 | tf_op jit(solution)/shard_map/cond/branch_0_fun/ppermute | solution.py:176
  42.3 3.4 %collective-permute-done = f32[256,1792]{1,0:T(8,128)S(1)} collective-permute-done((f32[256,1792]{1,0:T(8,128)S(1)}, f32[256,1792]{1,0:T(8,128)S(1)}, u32[]{:S(2)}, u32[]{:S(2)}) %collective-permute-start) | collective-permute-done | bytes 1835040 | tf_op jit(solution)/shard_map/cond/branch_0_fun/ppermute | solution.py:176
  45.7 1.6 fusion
  47.3 7.5 %all-to-all-start = ((bf16[16,2,8,1792]{3,2,1,0:T(8,128)(2,1)}), bf16[16,2,8,1792]{3,2,1,0:T(8,128)(2,1)S(1)}, u32[]{:S(2)}, u32[]{:S(2)}) async-start(bf16[16,2,8,1792]{3,2,1,0:T(8,128)(2,1)} %bitcast.141), calls=%async_computation | async-start | bytes 1835008 | tf_op jit(solution)/shard_map/cond/branch_0_fun/all_to_all | solution.py:23
  54.9 24.1 %all-to-all-done.got_ref = bf16[16,2,8,1792]{3,2,1,0:T(8,128)(2,1)S(1)} async-done(((bf16[16,2,8,1792]{3,2,1,0:T(8,128)(2,1)}), bf16[16,2,8,1792]{3,2,1,0:T(8,128)(2,1)S(1)}, u32[]{:S(2)}, u32[]{:S(2)}) %all-to-all-start) | async-done | bytes 917536 | tf_op jit(solution)/shard_map/cond/branch_0_fun/all_to_all | solution.py:23
  79.0 1.7 branch_0_fun.1
  80.7 28.1 %all_to_all.57 = bf16[16,2,8,1792]{3,2,1,0:T(8,128)(2,1)S(1)} all-to-all(bf16[16,2,8,1792]{3,2,1,0:T(8,128)(2,1)S(1)} %get-tuple-element.73), channel_id=1, replica_groups={{0,16,32,48,64,80,96,112,128,144,160,176,192,208,224,240},{8,24,40,56,7..., dimensions={0} | all-to-all | bytes 1835008 | tf_op jit(solution)/shard_map/cond/branch_0_fun/all_to_all | solution.py:23
  108.8 1.7 collective-permute-start.1
  110.6 0.7 fusion.9
  111.2 1.4 collective-permute-done.1
  112.7 0.7 fusion.72
  113.4 8.8 %all_to_all.58 = bf16[4,64,512]{2,1,0:T(8,128)(2,1)S(1)} all-to-all(bf16[4,64,512]{2,1,0:T(8,128)(2,1)S(1)} %bitcast.158), channel_id=1, replica_groups={{0,1,2,3},{4,5,6,7},{8,9,10,11},{12,13,14,15},{16,17,18,19},{20,21,22,2..., dimensions={0} | all-to-all | bytes 524288 | tf_op jit(solution)/shard_map/cond/branch_0_fun/all_to_all | solution.py:23
  122.3 4.2 %collective-permute-start.2 = (f32[64,512]{1,0:T(8,128)S(1)}, f32[64,512]{1,0:T(8,128)S(1)}, u32[]{:S(2)}, u32[]{:S(2)}) collective-permute-start(f32[64,512]{1,0:T(8,128)S(1)} %convert_reduce_fusion), channel_id=1, source_target_pairs={{0,4},{1,5},{2,6},{3,7},{4,0},{5,1},{6,2},{7,3},{8,12},{9,13},{10,... | collective-permute-start | bytes 393224 | tf_op jit(solution)/shard_map/cond/branch_0_fun/ppermute | solution.py:35
  126.5 2.2 %fusion.12 = f32[]{:T(128)} fusion(bf16[256,1792]{1,0:T(8,128)(2,1)S(1)} %collective-permute-done.1, bf16[256,1792]{1,0:T(8,128)(2,1)S(1)} %bitcast.164, bf16[256,512]{1,0:T(8,128)(2,1)S(1)} %bitcast.162, bf16[256,512]{1,0:T(8,128)(2,1)S(1)} %bitcast.157), kind=kOutput, calls=%fused_computation.10 | convolution fusion | flops 946077696 | bytes 2359300 | tf_op jit(solution)/shard_map/cond/branch_0_fun/dot_general | solution.py:196
  128.6 1.5 collective-permute-done.2
  130.4 0.7 broadcast_in_dim.209
  131.2 3.4 %all-to-all-start.11 = ((bf16[4,64,512]{2,1,0:T(8,128)(2,1)}), bf16[4,64,512]{2,1,0:T(8,128)(2,1)S(1)}, u32[]{:S(2)}, u32[]{:S(2)}) async-start(bf16[4,64,512]{2,1,0:T(8,128)(2,1)} %broadcast_in_dim.209), calls=%async_computation.11 | async-start | bytes 524288 | tf_op jit(solution)/shard_map/all_to_all | solution.py:23
  134.6 1.2 dynamic-slice_bitcast_fusion.7
  135.8 0.4 fusion.69
  136.2 3.8 %all-to-all-done.11 = bf16[4,64,512]{2,1,0:T(8,128)(2,1)S(1)} async-done(((bf16[4,64,512]{2,1,0:T(8,128)(2,1)}), bf16[4,64,512]{2,1,0:T(8,128)(2,1)S(1)}, u32[]{:S(2)}, u32[]{:S(2)}) %all-to-all-start.11) | async-done | bytes 262176 | tf_op jit(solution)/shard_map/all_to_all | solution.py:23
  140.1 0.9 fusion.68
  142.2 0.7 compare_select_fusion.1
  142.9 0.7 broadcast_in_dim.213
  143.6 12.6 %all-to-all-start.12 = ((f32[256,1,128]{2,1,0:T(1,128)}), f32[256,1,128]{2,1,0:T(1,128)S(1)}, u32[]{:S(2)}, u32[]{:S(2)}) async-start(f32[256,1,128]{2,1,0:T(1,128)} %broadcast_in_dim.213), calls=%async_computation.12 | async-start | bytes 262144 | tf_op jit(solution)/shard_map/all_to_all | solution.py:219
  156.3 12.7 %all-to-all-done.12 = f32[256,1,128]{2,1,0:T(1,128)S(1)} async-done(((f32[256,1,128]{2,1,0:T(1,128)}), f32[256,1,128]{2,1,0:T(1,128)S(1)}, u32[]{:S(2)}, u32[]{:S(2)}) %all-to-all-start.12) | async-done | bytes 131104 | tf_op jit(solution)/shard_map/all_to_all | solution.py:219
  169.0 0.6 fusion.70
  171.0 1.6 copy-done.2
  172.7 1.5 copy-done.3
  174.2 4.6 %shard_map.120 = (bf16[1792,512]{1,0:T(8,128)(2,1)}, bf16[1792,512]{1,0:T(8,128)(2,1)}) custom-call(f32[1,1]{1,0:T(1,128)} %bitcast.51.factor_ref, bf16[256,1792]{1,0:T(8,128)(2,1)S(1)} %pad_maximum_fusion.3.in_ref, bf16[256,512]{1,0:T(8,128)(2,1)S(1)} %bitcast.130, bf16[1792,512]{1,0:T(8,128)(2,1)S(1)} %bitcast.131, bf16[1792,512]{1,0:T(8,128)(2,1)S(1)} %bitcast.132), custom_call_target="tpu_custom_call" | custom-call | tf_op jit(solution)/shard_map/pallas_call | solution.py:98
  (30 shorter events, 0.5 us)
Async XLA Ops:
  0.6 1.5 copy-start
  0.6 9.2 %copy-start.27 = (s32[5]{0:T(128)S(1)}, s32[5]{0:T(128)}, u32[]{:S(2)}) copy-start(s32[5]{0:T(128)} %param.18) | copy-start | bytes 64
  0.7 24.6 %copy-start.26 = (f32[512]{0:T(512)S(1)}, f32[512]{0:T(512)}, u32[]{:S(2)}) copy-start(f32[512]{0:T(512)} %param.14) | copy-start | bytes 6148
  4.7 31.2 %copy-start.4 = (bf16[512,1,1792]{2,0,1:T(8,128)(2,1)S(1)}, bf16[512,1,1792]{2,0,1:T(8,128)(2,1)}, u32[]{:S(2)}) copy-start(bf16[512,1,1792]{2,0,1:T(8,128)(2,1)} %param.15) | copy-start | bytes 5505028
  4.7 31.2 %copy-start.19 = (f32[1,1792]{1,0:T(1,128)S(1)}, f32[1,1792]{1,0:T(1,128)}, u32[]{:S(2)}) copy-start(f32[1,1792]{1,0:T(1,128)} %param.16) | copy-start | bytes 21508
  4.7 10.7 %all-to-all-start.9 = ((bf16[4,64,512]{2,1,0:T(8,128)(2,1)}), bf16[4,64,512]{2,1,0:T(8,128)(2,1)S(1)}, u32[]{:S(2)}, u32[]{:S(2)}) async-start(bf16[4,64,512]{2,1,0:T(8,128)(2,1)} %bitcast.44), calls=%async_computation.9 | async-start | bytes 524288 | tf_op jit(solution)/shard_map/all_to_all | solution.py:23
  15.4 9.9 %collective-permute-start.9 = (f32[64,512]{1,0:T(8,128)S(1)}, f32[64,512]{1,0:T(8,128)S(1)}, u32[]{:S(2)}, u32[]{:S(2)}) collective-permute-start(f32[64,512]{1,0:T(8,128)S(1)} %convert_reduce_fusion.3), channel_id=1, source_target_pairs={{0,4},{1,5},{2,6},{3,7},{4,0},{5,1},{6,2},{7,3},{8,12},{9,13},{10,... | collective-permute-start | bytes 393224 | tf_op jit(solution)/shard_map/ppermute | solution.py:35
  26.9 8.9 %all-to-all-start.10 = ((bf16[4,64,512]{2,1,0:T(8,128)(2,1)}), bf16[4,64,512]{2,1,0:T(8,128)(2,1)S(1)}, u32[]{:S(2)}, u32[]{:S(2)}) async-start(bf16[4,64,512]{2,1,0:T(8,128)(2,1)} %broadcast_in_dim.208), calls=%async_computation.10 | async-start | bytes 524288 | tf_op jit(solution)/shard_map/all_to_all | solution.py:23
  35.9 0.5 copy-start.20
  37.8 7.9 %collective-permute-start = (f32[256,1792]{1,0:T(8,128)S(1)}, f32[256,1792]{1,0:T(8,128)S(1)}, u32[]{:S(2)}, u32[]{:S(2)}) collective-permute-start(f32[256,1792]{1,0:T(8,128)S(1)} %fusion.71), channel_id=1, source_target_pairs={{0,8},{8,0},{16,24},{24,16},{32,40},{40,32},{48,56},{56,48},{64,72... | collective-permute-start | bytes 5505032 | tf_op jit(solution)/shard_map/cond/branch_0_fun/ppermute | solution.py:176
  47.3 7.5 %copy-start.21 = (s32[16]{0:T(128)S(1)}, s32[16]{0:T(128)}, u32[]{:S(2)}) copy-start(s32[16]{0:T(128)} %copy-done.20) | copy-start | bytes 196 | tf_op jit(solution)/shard_map/conditional
  47.3 31.7 %all-to-all-start = ((bf16[16,2,8,1792]{3,2,1,0:T(8,128)(2,1)}), bf16[16,2,8,1792]{3,2,1,0:T(8,128)(2,1)S(1)}, u32[]{:S(2)}, u32[]{:S(2)}) async-start(bf16[16,2,8,1792]{3,2,1,0:T(8,128)(2,1)} %bitcast.141), calls=%async_computation | async-start | bytes 1835008 | tf_op jit(solution)/shard_map/cond/branch_0_fun/all_to_all | solution.py:23
  108.8 3.8 %collective-permute-start.1 = (bf16[256,1792]{1,0:T(8,128)(2,1)S(1)}, bf16[256,1792]{1,0:T(8,128)(2,1)S(1)}, u32[]{:S(2)}, u32[]{:S(2)}) collective-permute-start(bf16[256,1792]{1,0:T(8,128)(2,1)S(1)} %bitcast.163), channel_id=1, source_target_pairs={{0,8},{8,0},{16,24},{24,16},{32,40},{40,32},{48,56},{56,48},{64,72... | collective-permute-start | bytes 2752520 | tf_op jit(solution)/shard_map/cond/branch_0_fun/ppermute | solution.py:183
  122.3 7.9 %collective-permute-start.2 = (f32[64,512]{1,0:T(8,128)S(1)}, f32[64,512]{1,0:T(8,128)S(1)}, u32[]{:S(2)}, u32[]{:S(2)}) collective-permute-start(f32[64,512]{1,0:T(8,128)S(1)} %convert_reduce_fusion), channel_id=1, source_target_pairs={{0,4},{1,5},{2,6},{3,7},{4,0},{5,1},{6,2},{7,3},{8,12},{9,13},{10,... | collective-permute-start | bytes 393224 | tf_op jit(solution)/shard_map/cond/branch_0_fun/ppermute | solution.py:35
  131.2 8.9 %all-to-all-start.11 = ((bf16[4,64,512]{2,1,0:T(8,128)(2,1)}), bf16[4,64,512]{2,1,0:T(8,128)(2,1)S(1)}, u32[]{:S(2)}, u32[]{:S(2)}) async-start(bf16[4,64,512]{2,1,0:T(8,128)(2,1)} %broadcast_in_dim.209), calls=%async_computation.11 | async-start | bytes 524288 | tf_op jit(solution)/shard_map/all_to_all | solution.py:23
  143.6 25.4 %all-to-all-start.12 = ((f32[256,1,128]{2,1,0:T(1,128)}), f32[256,1,128]{2,1,0:T(1,128)S(1)}, u32[]{:S(2)}, u32[]{:S(2)}) async-start(f32[256,1,128]{2,1,0:T(1,128)} %broadcast_in_dim.213), calls=%async_computation.12 | async-start | bytes 262144 | tf_op jit(solution)/shard_map/all_to_all | solution.py:219
  171.0 7.7 %copy-start.1 = (bf16[1,1792,512]{2,1,0:T(8,128)(2,1)S(1)}, bf16[1,1792,512]{2,1,0:T(8,128)(2,1)}, u32[]{:S(2)}) copy-start(bf16[1,1792,512]{2,1,0:T(8,128)(2,1)} %param.13) | copy-start | bytes 5505028
  171.0 1.6 copy-start.2
  172.7 1.5 copy-start.3

commit v3 on v2

--- a/solution.py
+++ b/solution.py
@@ -15,24 +15,159 @@
 CHIPS = NX * NZ
 PLANE_SETS = [[chip * NCORE + c for chip in range(CHIPS)] for c in range(NCORE)]
 Y_SETS = [[h * NY + y for y in range(NY)] for h in range(NHI)]
-CORE_SWAP = [(i, i ^ 1) for i in range(NX * NZ * NCORE)]
+SAME_Y_SETS = [
+    [(i * NHI + h) * NY + y for i in range(CHIPS * NCORE) for h in range(NHI)] for y in range(NY)
+]
+CORE_SWAP = [(i, i ^ 1) for i in range(CHIPS * NCORE)]
 HI_SWAP = [(i, i ^ NY) for i in range(NHI * NY)]
+Y_SWAPS = [[(i, i ^ m) for i in range(NHI * NY)] for m in (1, 2)]
+TAIL = 16
 
 
 def swap_blocks(blocks, axis, sets):
     return lax.all_to_all(blocks, axis, 0, 0, axis_index_groups=sets)
 
 
-def gather_blocks(block, axis, sets):
-    copies = jnp.broadcast_to(block[None], (len(sets[0]), *block.shape))
-    return swap_blocks(copies, axis, sets)
-
-
-def sum_over_layers(partial):
-    rows, feats = partial.shape
-    parts = partial.astype(BF16).reshape(NY, rows // NY, feats)
-    mine = jnp.sum(swap_blocks(parts, "layer", Y_SETS).astype(F32), axis=0)
-    return mine + lax.ppermute(mine, "layer", HI_SWAP)
+def vmem_specs(count):
+    return [pl.BlockSpec(memory_space=pltpu.VMEM)] * count
+
+
+SMEM_SPEC = pl.BlockSpec(memory_space=pltpu.SMEM)
+SMALL = pltpu.CompilerParams(vmem_limit_bytes=24 * 2**20)
+LARGE = pltpu.CompilerParams(vmem_limit_bytes=56 * 2**20)
+
+
+def pre_kernel(in_ref, enc_ref, out_ref, acc):
+    step = pl.program_id(0)
+    part = jnp.dot(in_ref[...], enc_ref[...], preferred_element_type=F32)
+
+    @pl.when(step == 0)
+    def _():
+        acc[...] = part
+
+    @pl.when(step > 0)
+    def _():
+        acc[...] += part
+
+    @pl.when(step == pl.num_programs(0) - 1)
+    def _():
+        out_ref[...] = acc[...].astype(BF16)
+
+
+def partial_pre(layer_in, enc):
+    tokens, width = layer_in.shape
+    feats = enc.shape[1]
+    tile = 256
+    return pl.pallas_call(
+        pre_kernel,
+        grid=(width // tile,),
+        out_shape=jax.ShapeDtypeStruct((tokens, feats), BF16),
+        in_specs=[
+            pl.BlockSpec((tokens, tile), lambda i: (0, i)),
+            pl.BlockSpec((tile, feats), lambda i: (i, 0)),
+        ],
+        out_specs=pl.BlockSpec((tokens, feats), lambda i: (0, 0)),
+        scratch_shapes=[pltpu.VMEM((tokens, feats), F32)],
+        compiler_params=LARGE,
+    )(layer_in, enc)
+
+
+def feature_kernel(mine_ref, other_ref, bias_ref, gate_ref, out_ref):
+    pre = mine_ref[...] + other_ref[...] + bias_ref[...]
+    features = (pre * gate_ref[...]).astype(BF16)
+    for y in range(NY):
+        out_ref[y] = features
+
+
+def feature_copies(mine, other, bias, gate):
+    return pl.pallas_call(
+        feature_kernel,
+        out_shape=jax.ShapeDtypeStruct((NY, *mine.shape), BF16),
+        in_specs=vmem_specs(4),
+        out_specs=vmem_specs(1)[0],
+        compiler_params=SMALL,
+    )(mine, other, bias, gate)
+
+
+def in_thirds(value, lanes, first):
+    whole = jnp.full(lanes.shape, value, F32)
+    high = whole.astype(BF16).astype(F32)
+    middle = (whole - high).astype(BF16).astype(F32)
+    low = whole - high - middle
+    rest = jnp.where(lanes == first + 2, low, 0.0)
+    rest = jnp.where(lanes == first + 1, middle, rest)
+    return jnp.where(lanes == first, high, rest)
+
+
+def dpre_kernel(mine_ref, other_ref, gate_ref, gram_ref, loss_ref, dec_ref, out_ref):
+    dpre = ((mine_ref[...] + other_ref[...]) * gate_ref[...]).astype(BF16)
+    pairs = lax.dot_general(dpre, dpre, (((1,), (1,)), ((), ())), preferred_element_type=F32)
+    squares = jnp.sum(pairs * gram_ref[...]) + dec_ref[0, 0]
+    lanes = lax.broadcasted_iota(jnp.int32, (TAIL, dpre.shape[1]), 1)
+    tail = in_thirds(squares, lanes, 0) + in_thirds(loss_ref[0, 0], lanes, 3)
+    tokens = dpre.shape[0]
+    for y in range(NY):
+        out_ref[y, 0:tokens, :] = dpre
+        out_ref[y, tokens : tokens + TAIL, :] = tail.astype(BF16)
+
+
+def dpre_copies(mine, other, gate, gram, loss, dec_squares):
+    tokens, feats = mine.shape
+    return pl.pallas_call(
+        dpre_kernel,
+        out_shape=jax.ShapeDtypeStruct((NY, tokens + TAIL, feats), BF16),
+        in_specs=vmem_specs(4) + [SMEM_SPEC] * 2,
+        out_specs=vmem_specs(1)[0],
+        compiler_params=SMALL,
+    )(mine, other, gate, gram, loss, dec_squares)
+
+
+def row_kernel(got_ref, out_ref):
+    tokens = got_ref.shape[1] - TAIL
+    row = jnp.zeros((TAIL, got_ref.shape[2]), F32)
+    for y in range(NY):
+        row += got_ref[y, tokens : tokens + TAIL, :].astype(F32)
+    out_ref[...] = jnp.broadcast_to(row[0:1][None], out_ref.shape)
+
+
+def scalar_rows(got, count):
+    return pl.pallas_call(
+        row_kernel,
+        out_shape=jax.ShapeDtypeStruct((count, 1, got.shape[2]), F32),
+        in_specs=vmem_specs(1),
+        out_specs=vmem_specs(1)[0],
+        compiler_params=SMALL,
+    )(got)
+
+
+def grad_kernel(in_ref, got_ref, out_ref):
+    tokens = in_ref.shape[0]
+    dpre = jnp.concatenate([got_ref[y, 0:tokens, :] for y in range(NY)], axis=1)
+    out_ref[...] = lax.dot_general(
+        in_ref[...], dpre, (((0,), (0,)), ((), ())), preferred_element_type=F32
+    )
+
+
+def encoder_grad(layer_in, got):
+    tokens, width = layer_in.shape
+    feats = NY * got.shape[2]
+    tile = 256
+    return pl.pallas_call(
+        grad_kernel,
+        grid=(width // tile,),
+        out_shape=jax.ShapeDtypeStruct((width, feats), F32),
+        in_specs=[
+            pl.BlockSpec((tokens, tile), lambda i: (0, i)),
+            pl.BlockSpec(got.shape, lambda i: (0, 0, 0)),
+        ],
+        out_specs=pl.BlockSpec((tile, feats), lambda i: (i, 0)),
+        compiler_params=SMALL,
+        cost_estimate=pl.CostEstimate(
+            flops=2 * tokens * width * feats,
+            bytes_accessed=4 * width * feats,
+            transcendentals=0,
+        ),
+    )(layer_in, got)
 
 
 def owner_kernel(slots, groups, seg_ref, got_ref, rows_ref, bias_ref, out_ref, loss_ref, sums, errs):
@@ -79,36 +214,38 @@
     )(slot_seg, got, rows, bias)
 
 
-def update_kernel(factor_ref, in_ref, dpre_ref, first_ref, second_ref, new_first_ref, new_second_ref):
-    grad = lax.dot_general(
-        in_ref[...], dpre_ref[...], (((0,), (0,)), ((), ())), preferred_element_type=F32
-    )
-    clipped = factor_ref[0, 0] * grad
+def update_kernel(
+    limit, loss_scale, rows_ref, grad_ref, first_ref, second_ref,
+    new_first_ref, new_second_ref, loss_ref, norm_ref,
+):
+    totals = jnp.sum(rows_ref[...], axis=0)
+    lanes = lax.broadcasted_iota(jnp.int32, totals.shape, 1)
+    squares = jnp.sum(jnp.where(lanes < 3, totals, 0.0), axis=1, keepdims=True)
+    loss = jnp.sum(jnp.where(lanes < 3, 0.0, totals), axis=1, keepdims=True)
+    norm = jnp.sqrt(squares)
+    clipped = (limit / jnp.maximum(norm, limit)) * grad_ref[...]
     new_first_ref[...] = (0.9 * first_ref[...].astype(F32) + 0.1 * clipped).astype(BF16)
     new_second_ref[...] = (
         0.95 * second_ref[...].astype(F32) + 0.05 * clipped * clipped
     ).astype(BF16)
-
-
-def update(factor, layer_in, dpre, first, second):
-    tokens, width = layer_in.shape
-    feats = dpre.shape[1]
+    loss_ref[...] = loss * loss_scale
+    norm_ref[...] = norm
+
+
+def update(rows, grad, first, second, limit, loss_scale):
+    width, feats = grad.shape
     tile = 256
     tiles = pl.BlockSpec((tile, feats), lambda i: (i, 0))
-    return pl.pallas_call(
-        update_kernel,
+    one = pl.BlockSpec((1, 1), lambda i: (0, 0))
+    return pl.pallas_call(
+        functools.partial(update_kernel, limit, loss_scale),
         grid=(width // tile,),
-        out_shape=(jax.ShapeDtypeStruct((width, feats), BF16),) * 2,
-        in_specs=[
-            pl.BlockSpec(memory_space=pltpu.SMEM),
-            pl.BlockSpec((tokens, tile), lambda i: (0, i)),
-            pl.BlockSpec((tokens, feats), lambda i: (0, 0)),
-            tiles,
-            tiles,
-        ],
-        out_specs=(tiles, tiles),
-        compiler_params=pltpu.CompilerParams(vmem_limit_bytes=24 * 2**20),
-    )(factor, layer_in, dpre, first, second)
+        out_shape=(jax.ShapeDtypeStruct((width, feats), BF16),) * 2
+        + (jax.ShapeDtypeStruct((1, 1), F32),) * 2,
+        in_specs=[pl.BlockSpec(rows.shape, lambda i: (0, 0, 0)), tiles, tiles, tiles],
+        out_specs=(tiles, tiles, one, one),
+        compiler_params=LARGE,
+    )(rows, grad, first, second)
 
 
 def on_device(
@@ -135,9 +272,16 @@
     own_in = lax.dynamic_slice_in_dim(layer_in, own_start, half, 0)
     other_in = lax.dynamic_slice_in_dim(layer_in, other_start, half, 0)
     turned_in = jnp.concatenate([own_in, other_in], axis=0)
-    gate_mask = lax.dynamic_slice_in_dim(active, ypos * quarter, quarter, 0).astype(F32)
-    turned_start = (ypos * quarter + own_start) % tokens
-    turned_gate = lax.dynamic_slice_in_dim(active, turned_start, quarter, 0).astype(F32)
+    gate = active.astype(F32)
+    gate_rows = lax.dynamic_slice_in_dim(gate, ypos * quarter, quarter, 0)
+    gate_cols = lax.dynamic_slice_in_dim(gate, ypos * (feats_here // NY), feats_here // NY, 1)
+    turned_gate = jnp.concatenate(
+        [
+            lax.dynamic_slice_in_dim(gate_cols, own_start, half, 0),
+            lax.dynamic_slice_in_dim(gate_cols, other_start, half, 0),
+        ],
+        axis=0,
+    )
 
     latent_ids = lat * feats_here + lax.iota(jnp.int32, feats_here)
     seg = jnp.sum((bounds[:, None] <= latent_ids[None, :]).astype(jnp.int32), axis=0)
@@ -150,10 +294,11 @@
     slots_needed = jnp.max(chip_last - chip_first) + 1
     first_here = lax.dynamic_index_in_dim(chip_first, chip, 0, keepdims=False)
 
-    partial_pre = jnp.dot(layer_in, enc_local, preferred_element_type=F32)
-    pre_acts = sum_over_layers(partial_pre) + enc_bias
-    features_mine = (pre_acts * gate_mask).astype(BF16)
-    features = gather_blocks(features_mine, "layer", Y_SETS).reshape(tokens, feats_here)
+    pre_parts = partial_pre(layer_in, enc_local).reshape(NY, quarter, feats_here)
+    pre_mine = jnp.sum(swap_blocks(pre_parts, "layer", Y_SETS).astype(F32), axis=0)
+    pre_other = lax.ppermute(pre_mine, "layer", HI_SWAP)
+    copies = feature_copies(pre_mine, pre_other, enc_bias[None], gate_rows)
+    features = swap_blocks(copies, "layer", Y_SETS).reshape(tokens, feats_here)
 
     token_start = own_start + chip * per
     stream_rows = lax.dynamic_slice_in_dim(layer_in, token_start, per, 0).astype(F32)
@@ -176,7 +321,10 @@
         got = lax.ppermute(theirs, "lat", CORE_SWAP)
         ours = jnp.dot(own_rows, dec_local, preferred_element_type=F32)
         chip_sum = (ours + got).astype(BF16).reshape(CHIPS, slots, per, width)
+        chip_sum, gram = lax.optimization_barrier((chip_sum, own_gram))
         by_chip = swap_blocks(chip_sum, "lat", PLANE_SETS)
+        for swap in Y_SWAPS:
+            gram = gram + lax.ppermute(gram, "layer", swap)
         slot_seg = jnp.minimum(chip_first[:, None] + slot_ids[None, :], groups - 1)
         wanted, loss = owner_step(slot_seg, by_chip, stream_rows, dec_bias, groups)
         own_err = swap_blocks(wanted, "lat", PLANE_SETS).reshape(CHIPS * slots * per, width)
@@ -191,41 +339,36 @@
             ).reshape(half, feats_here)
 
         partial_dfeat = jnp.concatenate([back(own_err), back(other_err)], axis=0)
-        dfeat = sum_over_layers(partial_dfeat)
-        dpre_mine = (dfeat * turned_gate).astype(BF16)
+        parts = partial_dfeat.astype(BF16).reshape(tokens, NY, feats_here // NY).transpose(1, 0, 2)
+        mine = jnp.sum(swap_blocks(parts, "layer", Y_SETS).astype(F32), axis=0)
+        other = lax.ppermute(mine, "layer", HI_SWAP)
         grad_dec = lax.dot_general(
             jnp.concatenate([own_rows, other_rows], axis=0),
             jnp.concatenate([own_err, other_err], axis=0),
             (((0,), (0,)), ((), ())),
             preferred_element_type=F32,
         )
-        return dpre_mine, loss[0, 0], jnp.sum(grad_dec * grad_dec)
+        dec_squares = jnp.sum(grad_dec * grad_dec).reshape(1, 1)
+        return dpre_copies(mine, other, turned_gate, gram, loss, dec_squares)
 
     choices = sorted({min(2, groups), min(3, groups), groups})
     which = sum((slots_needed > c).astype(jnp.int32) for c in choices[:-1])
-    dpre_mine, loss_part, dec_squares = lax.switch(
+    copies = lax.switch(
         which,
         [lambda f, d, s=s: middle(s, f, d) for s in choices],
         features,
         dec_local,
     )
-
-    dpre = gather_blocks(dpre_mine, "layer", Y_SETS).reshape(tokens, feats_here)
-    dpre_gram = lax.dot_general(dpre, dpre, (((1,), (1,)), ((), ())), preferred_element_type=F32)
-    squares = jnp.sum(own_gram * dpre_gram) + dec_squares
-    lanes = lax.iota(jnp.int32, 128)
-    row = jnp.where(lanes == 0, squares, jnp.where(lanes == 1, loss_part, 0.0))
-    rows = jnp.broadcast_to(row[None], (lat_count * layer_count, 128))
-    totals = jnp.sum(lax.all_to_all(rows, ("lat", "layer"), 0, 0), axis=0)
-    norm_total, loss_total = totals[0], totals[1]
-    grad_norm = jnp.sqrt(norm_total)
+    got = swap_blocks(copies, "layer", Y_SETS)
+    rows = scalar_rows(got, len(SAME_Y_SETS[0]))
+    rows = lax.all_to_all(rows, ("lat", "layer"), 0, 0, axis_index_groups=SAME_Y_SETS)
+    grad_enc = encoder_grad(turned_in, got)
     limit = math.sqrt(2.0 * layer_count * width * feats_here * lat_count)
-    factor = limit / jnp.maximum(grad_norm, limit)
-    new_first, new_second = update(
-        factor.reshape(1, 1), turned_in, dpre, first_moment[0], second_moment[0]
-    )
-    loss_value = loss_total / (tokens * layer_count * width)
-    return (new_first[None], new_second[None], loss_value, grad_norm)
+    new_first, new_second, loss_value, grad_norm = update(
+        rows, grad_enc, first_moment[0], second_moment[0],
+        limit, 1.0 / (tokens * layer_count * width),
+    )
+    return (new_first[None], new_second[None], loss_value[0, 0], grad_norm[0, 0])
 
 
 def solution(mesh):

time: 182 us -> 185 us (1.016)
  Pallas kernels: 6.22 us -> 20.6 us
  between operations: 6.43 us -> 1.51 us
  waiting for transfers between devices: 57.2 us -> 53 us
  local copies, waits for them, and re-layouts: 9.77 us -> 5.78 us
  matrix products: 9.55 us -> 12.2 us
    pallas_call x1 -> x6, Pallas kernels: 4.57 us -> 18.9 us  [the longest x1 7.99 us: update(): pl.pallas_call(functools.partial(update_kernel, limit, loss_scale), grid=...]
    all_to_all x1, waiting for transfers between devices: 12.7 us -> 4.25 us  [on_device(): lax.all_to_all(rows, ('lat', 'layer'), 0, 0, axis_index_groups=SAME_Y_SETS)]
    ppermute x2 -> x4, waiting for transfers between devices: 1.54 us -> 7.71 us  [the longest x2 7.65 us: middle(): gram = gram + lax.ppermute(gram, 'layer', swap)]
    dot_general x2 -> x0, matrix products: 3.38 us -> none  [the longest x1 2.52 us: on_device(): partial_pre = jnp.dot(layer_in, enc_local, preferred_element_type=F32)]
    dot_general x2, matrix products: 1.34 us -> 3.73 us  [back(): lax.dot_general(err, dec_local, (((1,), (1,)), ((), ())), preferred_eleme...]
    broadcast_in_dim x3 -> x0, local copies, waits for them, and re-layouts: 2.17 us -> none  [the longest x2 1.45 us: gather_blocks(): copies = jnp.broadcast_to(block[None], (len(sets[0]), *block.shape))]
    dot_general x1, matrix products: 0.43 us -> 2.59 us  [on_device(): lax.dot_general(turned_in, turned_in, (((1,), (1,)), ((), ())), preferred...]
    unnamed x16 -> x18, local copies, waits for them, and re-layouts: 4.63 us -> 3.11 us
  transfers between devices with their start and end apart: 9 -> 11, of which waited for: 8 -> 8; matrix products, arithmetic and copies ran while one was open for 4% -> 9% of each run, Pallas kernels for 0% -> 1%
where the time goes in v3:
time: 185 us; the launch traced here: 184 us
  waiting for transfers between devices  53 us (29%)
  starting transfers between devices  48.5 us (26%)
  blocking collectives  37.3 us (20%)
  Pallas kernels  20.6 us (11%)
  matrix products  12.2 us (7%)
  local copies, waits for them, and re-layouts  5.78 us (3%)
  other arithmetic  4.81 us (3%)
    all_to_all x4, waiting for transfers between devices, swap_blocks(): return lax.all_to_all(blocks, axis, 0, 0, axis_index_groups=sets)  37.6 us
    all_to_all x2, blocking collectives, swap_blocks(): return lax.all_to_all(blocks, axis, 0, 0, axis_index_groups=sets)  37.3 us
    all_to_all x4, starting transfers between devices, swap_blocks(): return lax.all_to_all(blocks, axis, 0, 0, axis_index_groups=sets)  18.6 us
    all_to_all x1, starting transfers between devices, on_device(): lax.all_to_all(rows, ('lat', 'layer'), 0, 0, axis_index_groups=SAME_Y_SETS)  12.2 us
    pallas_call x1, Pallas kernels, update(): pl.pallas_call(functools.partial(update_kernel, limit, loss_scale), grid=...  7.99 us
    ppermute x2, waiting for transfers between devices, middle(): gram = gram + lax.ppermute(gram, 'layer', swap)  7.65 us
    ppermute x1, starting transfers between devices, on_device(): pre_other = lax.ppermute(pre_mine, 'layer', HI_SWAP)  7.04 us
    pallas_call x1, Pallas kernels, partial_pre(): pl.pallas_call(pre_kernel, grid=(width // tile,), out_shape=jax.ShapeDtyp...  6 us
  transfers between devices with their start and end apart: 11, of which 8 were waited for; matrix products, arithmetic and copies ran while one was open for 9% of the time, Pallas kernels for 1%

profile of v3, /device:TPU:1, one launch (start us, length us, event | category | flops | bytes accessed | tf_op | source)
XLA Modules:
  0.0 184.0 jit_solution(4695881648702829280)
XLA Ops:
  0.6 6.0 %shard_map.120 = bf16[256,512]{1,0:T(8,128)(2,1)} custom-call(bf16[256,1792]{1,0:T(8,128)(2,1)} %bitcast.113, bf16[1792,512]{1,0:T(8,128)(2,1)} %bitcast.124), custom_call_target="tpu_custom_call" | custom-call | tf_op jit(solution)/shard_map/pallas_call | solution.py:61
  6.6 5.1 %all-to-all-start.9 = ((bf16[4,64,512]{2,1,0:T(8,128)(2,1)}), bf16[4,64,512]{2,1,0:T(8,128)(2,1)S(1)}, u32[]{:S(2)}, u32[]{:S(2)}) async-start(bf16[4,64,512]{2,1,0:T(8,128)(2,1)} %bitcast.132), calls=%async_computation.9 | async-start | bytes 524288 | tf_op jit(solution)/shard_map/all_to_all | solution.py:28
  11.9 0.1 fusion.63
  12.0 0.6 pad_maximum_fusion.1
  12.7 0.1 convert_reduce_fusion.4
  12.8 1.0 dynamic-slice_bitcast_fusion.7
  13.8 3.5 %all-to-all-done.9 = bf16[4,64,512]{2,1,0:T(8,128)(2,1)S(1)} async-done(((bf16[4,64,512]{2,1,0:T(8,128)(2,1)}), bf16[4,64,512]{2,1,0:T(8,128)(2,1)S(1)}, u32[]{:S(2)}, u32[]{:S(2)}) %all-to-all-start.9) | async-done | bytes 262176 | tf_op jit(solution)/shard_map/all_to_all | solution.py:28
  17.4 7.0 %collective-permute-start.15 = (f32[64,512]{1,0:T(8,128)S(1)}, f32[64,512]{1,0:T(8,128)S(1)}, u32[]{:S(2)}, u32[]{:S(2)}) collective-permute-start(f32[64,512]{1,0:T(8,128)S(1)} %convert_reduce_fusion.3.mine_ref), channel_id=1, source_target_pairs={{0,4},{1,5},{2,6},{3,7},{4,0},{5,1},{6,2},{7,3},{8,12},{9,13},{10,... | collective-permute-start | bytes 393224 | tf_op jit(solution)/shard_map/ppermute | solution.py:299
  24.4 0.6 subtract_reduce_fusion
  25.7 0.6 dynamic_slice.45
  26.3 2.6 %fusion.62 = f32[256,256]{1,0:T(8,128)} fusion(bf16[128,1792]{1,0:T(8,128)(2,1)} %get-tuple-element.142, bf16[128,1792]{1,0:T(8,128)(2,1)} %get-tuple-element.141), kind=kOutput, calls=%fused_computation.89 | convolution fusion | flops 236716032 | bytes 1179648 | tf_op jit(solution)/shard_map/dot_general | solution.py:305
  28.9 0.7 shard_map.121
  29.6 3.4 %all-to-all-start.10 = ((bf16[4,64,512]{2,1,0:T(8,128)(2,1)}), bf16[4,64,512]{2,1,0:T(8,128)(2,1)S(1)}, u32[]{:S(2)}, u32[]{:S(2)}) async-start(bf16[4,64,512]{2,1,0:T(8,128)(2,1)} %shard_map.121), calls=%async_computation.10 | async-start | bytes 524288 | tf_op jit(solution)/shard_map/all_to_all | solution.py:28
  33.0 5.5 %all-to-all-done.10 = bf16[4,64,512]{2,1,0:T(8,128)(2,1)S(1)} async-done(((bf16[4,64,512]{2,1,0:T(8,128)(2,1)}), bf16[4,64,512]{2,1,0:T(8,128)(2,1)S(1)}, u32[]{:S(2)}, u32[]{:S(2)}) %all-to-all-start.10) | async-done | bytes 262176 | tf_op jit(solution)/shard_map/all_to_all | solution.py:28
  38.5 105.1 %conditional.1 = (bf16[4,272,128]{2,1,0:T(8,128)(2,1)S(1)}) conditional(s32[]{:T(128)} %clamp.11, (s32[]{:T(128)}, s32[512]{0:T(512)S(1)}, s32[16]{0:T(128)S(1)}, s32[]{:T(128)}, bf16[256,512]{1,0:T(8,128)(2,1)S(1)}, /*index=5*/bf16[512,1792]{1,0:T(8,128)(2,1)S(1)}, s32[]{:T(128)}, f32[256,256]{1,0:T(8,128)}, ...), branch_computations={%region_5.10_spmd, %region_10.15_spmd, %region_15.20_spmd} | conditional | flops 7064685568 | bytes 108283416 | solution.py:356
  38.5 0.6 broadcast_subtract_fusion
  39.3 0.6 fusion.64
  40.0 3.6 %collective-permute-start = (f32[256,1792]{1,0:T(8,128)S(1)}, f32[256,1792]{1,0:T(8,128)S(1)}, u32[]{:S(2)}, u32[]{:S(2)}) collective-permute-start(f32[256,1792]{1,0:T(8,128)S(1)} %fusion.64), channel_id=1, source_target_pairs={{0,8},{8,0},{16,24},{24,16},{32,40},{40,32},{48,56},{56,48},{64,72... | collective-permute-start | bytes 5505032 | tf_op jit(solution)/shard_map/cond/branch_0_fun/ppermute | solution.py:321
  43.6 3.4 %collective-permute-done = f32[256,1792]{1,0:T(8,128)S(1)} collective-permute-done((f32[256,1792]{1,0:T(8,128)S(1)}, f32[256,1792]{1,0:T(8,128)S(1)}, u32[]{:S(2)}, u32[]{:S(2)}) %collective-permute-start) | collective-permute-done | bytes 1835040 | tf_op jit(solution)/shard_map/cond/branch_0_fun/ppermute | solution.py:321
  47.0 1.6 fusion
  48.6 6.6 %all-to-all-start = ((bf16[16,2,8,1792]{3,2,1,0:T(8,128)(2,1)}), bf16[16,2,8,1792]{3,2,1,0:T(8,128)(2,1)S(1)}, u32[]{:S(2)}, u32[]{:S(2)}) async-start(bf16[16,2,8,1792]{3,2,1,0:T(8,128)(2,1)} %bitcast.114), calls=%async_computation | async-start | bytes 1835008 | tf_op jit(solution)/shard_map/cond/branch_0_fun/all_to_all | solution.py:28
  55.3 24.1 %all-to-all-done.got_ref = bf16[16,2,8,1792]{3,2,1,0:T(8,128)(2,1)S(1)} async-done(((bf16[16,2,8,1792]{3,2,1,0:T(8,128)(2,1)}), bf16[16,2,8,1792]{3,2,1,0:T(8,128)(2,1)S(1)}, u32[]{:S(2)}, u32[]{:S(2)}) %all-to-all-start) | async-done | bytes 917536 | tf_op jit(solution)/shard_map/cond/branch_0_fun/all_to_all | solution.py:28
  79.5 1.6 branch_0_fun.2
  81.1 28.2 %all_to_all.56 = bf16[16,2,8,1792]{3,2,1,0:T(8,128)(2,1)} all-to-all(bf16[16,2,8,1792]{3,2,1,0:T(8,128)(2,1)S(1)} %get-tuple-element.81), channel_id=1, replica_groups={{0,16,32,48,64,80,96,112,128,144,160,176,192,208,224,240},{8,24,40,56,7..., dimensions={0} | all-to-all | bytes 1835008 | tf_op jit(solution)/shard_map/cond/branch_0_fun/all_to_all | solution.py:28
  109.4 1.7 collective-permute-start.1
  111.1 0.3 collective-permute-start.3
  111.4 7.6 %collective-permute-done.3 = f32[256,256]{1,0:T(8,128)S(1)} collective-permute-done((f32[256,256]{1,0:T(8,128)S(1)}, f32[256,256]{1,0:T(8,128)S(1)}, u32[]{:S(2)}, u32[]{:S(2)}) %collective-permute-start.3) | collective-permute-done | bytes 262176 | tf_op jit(solution)/shard_map/cond/branch_0_fun/ppermute | solution.py:327
  119.1 0.9 collective-permute-start.4
  120.0 1.9 %fusion.9 = bf16[16,8,512]{2,1,0:T(8,128)(2,1)S(1)} fusion(bf16[16,2,8,1792]{3,2,1,0:T(8,128)(2,1)} %all_to_all.56, bf16[512,1792]{1,0:T(8,128)(2,1)S(1)} %get-tuple-element.75, pred[2,512]{1,0:T(4,128)(4,1)S(1)} %iota_compare_fusion), kind=kOutput, calls=%fused_computation.9 | convolution fusion | flops 469958656 | bytes 2884608 | tf_op jit(solution)/shard_map/cond/branch_0_fun/dot_general | solution.py:334
  121.9 1.8 %fusion.65 = f32[256,512]{1,0:T(8,128)S(1)} fusion(bf16[256,1792]{1,0:T(8,128)(2,1)} %collective-permute-done.1, bf16[512,1792]{1,0:T(8,128)(2,1)S(1)} %get-tuple-element.75), kind=kOutput, calls=%fused_computation.92 | convolution fusion | flops 469762048 | bytes 3276800 | tf_op jit(solution)/shard_map/cond/branch_0_fun/dot_general | solution.py:334
  123.9 0.2 maximum_bitcast_fusion
  124.1 0.7 copy.16
  124.8 3.4 %all-to-all-start.2 = ((bf16[4,256,128]{2,1,0:T(8,128)(2,1)}), bf16[4,256,128]{2,1,0:T(8,128)(2,1)S(1)}, u32[]{:S(2)}, u32[]{:S(2)}) async-start(bf16[4,256,128]{2,1,0:T(8,128)(2,1)} %copy.16), calls=%async_computation.2 | async-start | bytes 524288 | tf_op jit(solution)/shard_map/cond/branch_0_fun/all_to_all | solution.py:28
  128.2 1.0 add.113.gram_ref
  129.2 4.5 %all-to-all-done.2 = bf16[4,256,128]{2,1,0:T(8,128)(2,1)S(1)} async-done(((bf16[4,256,128]{2,1,0:T(8,128)(2,1)}), bf16[4,256,128]{2,1,0:T(8,128)(2,1)S(1)}, u32[]{:S(2)}, u32[]{:S(2)}) %all-to-all-start.2) | async-done | bytes 262176 | tf_op jit(solution)/shard_map/cond/branch_0_fun/all_to_all | solution.py:28
  133.8 4.2 %collective-permute-start.2 = (f32[256,128]{1,0:T(8,128)S(1)}, f32[256,128]{1,0:T(8,128)S(1)}, u32[]{:S(2)}, u32[]{:S(2)}) collective-permute-start(f32[256,128]{1,0:T(8,128)S(1)} %convert_reduce_fusion.mine_ref), channel_id=1, source_target_pairs={{0,4},{1,5},{2,6},{3,7},{4,0},{5,1},{6,2},{7,3},{8,12},{9,13},{10,... | collective-permute-start | bytes 393224 | tf_op jit(solution)/shard_map/cond/branch_0_fun/ppermute | solution.py:344
  138.0 3.6 %fusion.12 = f32[]{:T(128)} fusion(bf16[256,1792]{1,0:T(8,128)(2,1)} %collective-permute-done.1, bf16[256,1792]{1,0:T(8,128)(2,1)} %bitcast.7, bf16[256,512]{1,0:T(8,128)(2,1)S(1)} %bitcast.134, bf16[256,512]{1,0:T(8,128)(2,1)S(1)} %bitcast.131), kind=kOutput, calls=%fused_computation.10 | convolution fusion | flops 946077696 | bytes 2359300 | tf_op jit(solution)/shard_map/cond/branch_0_fun/dot_general | solution.py:345
  141.7 1.7 branch_0_fun.3
  143.6 0.7 copy-done.22
  144.3 9.0 %all_to_all.59.got_ref = bf16[4,272,128]{2,1,0:T(8,128)(2,1)S(1)} all-to-all(bf16[4,272,128]{2,1,0:T(8,128)(2,1)} %copy-done.22), channel_id=1, replica_groups={{0,1,2,3},{4,5,6,7},{8,9,10,11},{12,13,14,15},{16,17,18,19},{20,21,22,2..., dimensions={0} | all-to-all | bytes 557056 | tf_op jit(solution)/shard_map/all_to_all | solution.py:28
  153.4 0.6 shard_map.122
  154.0 12.2 %all-to-all-start.12 = ((f32[64,1,128]{2,1,0:T(1,128)}), f32[64,1,128]{2,1,0:T(1,128)S(1)}, u32[]{:S(2)}, u32[]{:S(2)}) async-start(f32[64,1,128]{2,1,0:T(1,128)} %shard_map.122), calls=%async_computation.12 | async-start | bytes 65536 | tf_op jit(solution)/shard_map/all_to_all | solution.py:364
  166.2 1.2 pad_maximum_fusion.in_ref
  167.4 1.9 %shard_map.123.grad_ref = f32[1792,512]{1,0:T(8,128)S(1)} custom-call(bf16[256,1792]{1,0:T(8,128)(2,1)S(1)} %pad_maximum_fusion.in_ref, bf16[4,272,128]{2,1,0:T(8,128)(2,1)S(1)} %all_to_all.59.got_ref), custom_call_target="tpu_custom_call" | custom-call | flops 469762048 | bytes 3670016 | tf_op jit(solution)/shard_map/pallas_call | solution.py:155
  169.3 1.8 copy-done
  171.1 4.3 %all-to-all-done.12.rows_ref = f32[64,1,128]{2,1,0:T(1,128)S(1)} async-done(((f32[64,1,128]{2,1,0:T(1,128)}), f32[64,1,128]{2,1,0:T(1,128)S(1)}, u32[]{:S(2)}, u32[]{:S(2)}) %all-to-all-start.12) | async-done | bytes 32800 | tf_op jit(solution)/shard_map/all_to_all | solution.py:364
  175.3 0.6 copy-done.27
  175.9 8.0 %shard_map.124 = (bf16[1792,512]{1,0:T(8,128)(2,1)}, bf16[1792,512]{1,0:T(8,128)(2,1)}, f32[1,1]{1,0:T(1,128)}, f32[1,1]{1,0:T(1,128)}) custom-call(f32[64,1,128]{2,1,0:T(1,128)} %copy-done.27, f32[1792,512]{1,0:T(8,128)} %copy-done, bf16[1792,512]{1,0:T(8,128)(2,1)} %bitcast.122, bf16[1792,512]{1,0:T(8,128)(2,1)} %bitcast.123), custom_call_target="tpu_custom_call" | custom-call | tf_op jit(solution)/shard_map/pallas_call | solution.py:240
  (43 shorter events, 0.8 us)
Async XLA Ops:
  0.6 11.1 %copy-start.25 = (s32[256,512]{1,0:T(8,128)S(1)}, s32[256,512]{1,0:T(8,128)}, u32[]{:S(2)}) copy-start(s32[256,512]{1,0:T(8,128)} %param.17) | copy-start | bytes 1572868
  6.6 6.0 %copy-start.33 = (s32[5]{0:T(128)S(1)}, s32[5]{0:T(128)}, u32[]{:S(2)}) copy-start(s32[5]{0:T(128)} %param.18) | copy-start | bytes 64
  6.6 6.2 %copy-start.5 = (bf16[256,1,1792]{2,0,1:T(8,128)(2,1)S(1)}, bf16[256,1,1792]{2,0,1:T(8,128)(2,1)}, u32[]{:S(2)}) copy-start(bf16[256,1,1792]{2,0,1:T(8,128)(2,1)} %param.12) | copy-start | bytes 2752516
  6.6 10.7 %all-to-all-start.9 = ((bf16[4,64,512]{2,1,0:T(8,128)(2,1)}), bf16[4,64,512]{2,1,0:T(8,128)(2,1)S(1)}, u32[]{:S(2)}, u32[]{:S(2)}) async-start(bf16[4,64,512]{2,1,0:T(8,128)(2,1)} %bitcast.132), calls=%async_computation.9 | async-start | bytes 524288 | tf_op jit(solution)/shard_map/all_to_all | solution.py:28
  13.8 15.0 %copy-start.1 = (f32[512]{0:T(512)S(1)}, f32[512]{0:T(512)}, u32[]{:S(2)}) copy-start(f32[512]{0:T(512)} %param.14) | copy-start | bytes 6148
  17.3 21.2 %copy-start.2 = (bf16[512,1,1792]{2,0,1:T(8,128)(2,1)S(1)}, bf16[512,1,1792]{2,0,1:T(8,128)(2,1)}, u32[]{:S(2)}) copy-start(bf16[512,1,1792]{2,0,1:T(8,128)(2,1)} %param.15) | copy-start | bytes 5505028
  17.4 21.2 %copy-start.28 = (f32[1,1792]{1,0:T(1,128)S(1)}, f32[1,1792]{1,0:T(1,128)}, u32[]{:S(2)}) copy-start(f32[1,1792]{1,0:T(1,128)} %param.16) | copy-start | bytes 21508
  17.4 11.5 %collective-permute-start.15 = (f32[64,512]{1,0:T(8,128)S(1)}, f32[64,512]{1,0:T(8,128)S(1)}, u32[]{:S(2)}, u32[]{:S(2)}) collective-permute-start(f32[64,512]{1,0:T(8,128)S(1)} %convert_reduce_fusion.3.mine_ref), channel_id=1, source_target_pairs={{0,4},{1,5},{2,6},{3,7},{4,0},{5,1},{6,2},{7,3},{8,12},{9,13},{10,... | collective-permute-start | bytes 393224 | tf_op jit(solution)/shard_map/ppermute | solution.py:299
  29.6 8.9 %all-to-all-start.10 = ((bf16[4,64,512]{2,1,0:T(8,128)(2,1)}), bf16[4,64,512]{2,1,0:T(8,128)(2,1)S(1)}, u32[]{:S(2)}, u32[]{:S(2)}) async-start(bf16[4,64,512]{2,1,0:T(8,128)(2,1)} %shard_map.121), calls=%async_computation.10 | async-start | bytes 524288 | tf_op jit(solution)/shard_map/all_to_all | solution.py:28
  39.3 0.7 copy-start.23
  40.0 7.0 %collective-permute-start = (f32[256,1792]{1,0:T(8,128)S(1)}, f32[256,1792]{1,0:T(8,128)S(1)}, u32[]{:S(2)}, u32[]{:S(2)}) collective-permute-start(f32[256,1792]{1,0:T(8,128)S(1)} %fusion.64), channel_id=1, source_target_pairs={{0,8},{8,0},{16,24},{24,16},{32,40},{40,32},{48,56},{56,48},{64,72... | collective-permute-start | bytes 5505032 | tf_op jit(solution)/shard_map/cond/branch_0_fun/ppermute | solution.py:321
  48.6 30.9 %all-to-all-start = ((bf16[16,2,8,1792]{3,2,1,0:T(8,128)(2,1)}), bf16[16,2,8,1792]{3,2,1,0:T(8,128)(2,1)S(1)}, u32[]{:S(2)}, u32[]{:S(2)}) async-start(bf16[16,2,8,1792]{3,2,1,0:T(8,128)(2,1)} %bitcast.114), calls=%async_computation | async-start | bytes 1835008 | tf_op jit(solution)/shard_map/cond/branch_0_fun/all_to_all | solution.py:28
  55.2 55.9 %copy-start.10 = (f32[256,256]{1,0:T(8,128)S(1)}, f32[256,256]{1,0:T(8,128)}, u32[]{:S(2)}) copy-start(f32[256,256]{1,0:T(8,128)} %get-tuple-element.83) | copy-start | bytes 786436 | tf_op jit(solution)/shard_map/cond
  109.4 12.6 %collective-permute-start.1 = (bf16[256,1792]{1,0:T(8,128)(2,1)}, bf16[256,1792]{1,0:T(8,128)(2,1)}, u32[]{:S(2)}, u32[]{:S(2)}) collective-permute-start(bf16[256,1792]{1,0:T(8,128)(2,1)} %bitcast.7), channel_id=1, source_target_pairs={{0,8},{8,0},{16,24},{24,16},{32,40},{40,32},{48,56},{56,48},{64,72... | collective-permute-start | bytes 2752520 | tf_op jit(solution)/shard_map/cond/branch_0_fun/ppermute | solution.py:331
  111.1 7.9 %collective-permute-start.3 = (f32[256,256]{1,0:T(8,128)S(1)}, f32[256,256]{1,0:T(8,128)S(1)}, u32[]{:S(2)}, u32[]{:S(2)}) collective-permute-start(f32[256,256]{1,0:T(8,128)S(1)} %copy-done.10), channel_id=1, source_target_pairs={{0,1},{1,0},{2,3},{3,2},{4,5},{5,4},{6,7},{7,6},{8,9},{9,8},{10,11... | collective-permute-start | bytes 786440 | tf_op jit(solution)/shard_map/cond/branch_0_fun/ppermute | solution.py:327
  119.1 9.2 %collective-permute-start.4 = (f32[256,256]{1,0:T(8,128)S(1)}, f32[256,256]{1,0:T(8,128)}, u32[]{:S(2)}, u32[]{:S(2)}) collective-permute-start(f32[256,256]{1,0:T(8,128)S(1)} %add.112), channel_id=1, source_target_pairs={{0,2},{1,3},{2,0},{3,1},{4,6},{5,7},{6,4},{7,5},{8,10},{9,11},{10,... | collective-permute-start | bytes 786440 | tf_op jit(solution)/shard_map/cond/branch_0_fun/ppermute | solution.py:327
  123.8 14.3 %copy-start.24 = (bf16[16,2,8,512]{3,2,1,0:T(8,128)(2,1)S(1)}, bf16[16,2,8,512]{3,2,1,0:T(8,128)(2,1)}, u32[]{:S(2)}) copy-start(bf16[16,2,8,512]{3,2,1,0:T(8,128)(2,1)} %copy-done.23) | copy-start | bytes 786436 | tf_op jit(solution)/shard_map/cond
  124.8 9.0 %all-to-all-start.2 = ((bf16[4,256,128]{2,1,0:T(8,128)(2,1)}), bf16[4,256,128]{2,1,0:T(8,128)(2,1)S(1)}, u32[]{:S(2)}, u32[]{:S(2)}) async-start(bf16[4,256,128]{2,1,0:T(8,128)(2,1)} %copy.16), calls=%async_computation.2 | async-start | bytes 524288 | tf_op jit(solution)/shard_map/cond/branch_0_fun/all_to_all | solution.py:28
  133.8 7.9 %copy-start.15 = (f32[256,128]{1,0:T(8,128)S(1)}, f32[256,128]{1,0:T(8,128)}, u32[]{:S(2)}) copy-start(f32[256,128]{1,0:T(8,128)} %get-tuple-element.82.gate_ref) | copy-start | bytes 393220 | tf_op jit(solution)/shard_map/cond
  133.8 7.9 %collective-permute-start.2 = (f32[256,128]{1,0:T(8,128)S(1)}, f32[256,128]{1,0:T(8,128)S(1)}, u32[]{:S(2)}, u32[]{:S(2)}) collective-permute-start(f32[256,128]{1,0:T(8,128)S(1)} %convert_reduce_fusion.mine_ref), channel_id=1, source_target_pairs={{0,4},{1,5},{2,6},{3,7},{4,0},{5,1},{6,2},{7,3},{8,12},{9,13},{10,... | collective-permute-start | bytes 393224 | tf_op jit(solution)/shard_map/cond/branch_0_fun/ppermute | solution.py:344
  143.6 0.7 copy-start.22
  154.0 21.3 %all-to-all-start.12 = ((f32[64,1,128]{2,1,0:T(1,128)}), f32[64,1,128]{2,1,0:T(1,128)S(1)}, u32[]{:S(2)}, u32[]{:S(2)}) async-start(f32[64,1,128]{2,1,0:T(1,128)} %shard_map.122), calls=%async_computation.12 | async-start | bytes 65536 | tf_op jit(solution)/shard_map/all_to_all | solution.py:364
  169.3 1.8 copy-start
  175.3 0.6 copy-start.27

commit v4 on v3

v4 whole, which is shorter than its diff:
```python
import functools
import math

import jax
import jax.numpy as jnp
from jax import lax
from jax.experimental import pallas as pl
from jax.experimental.pallas import tpu as pltpu
from jax.sharding import PartitionSpec as P

BF16 = jnp.bfloat16
F32 = jnp.float32

NX, NZ, NCORE, NHI, NY = 4, 4, 2, 2, 4
CHIPS = NX * NZ
PLANE_SETS = [[chip * NCORE + c for chip in range(CHIPS)] for c in range(NCORE)]
Y_SETS = [[h * NY + y for y in range(NY)] for h in range(NHI)]
CORE_SWAP = [(i, i ^ 1) for i in range(CHIPS * NCORE)]
HI_SWAP = [(i, i ^ NY) for i in range(NHI * NY)]
Y_SWAPS = [[(i, i ^ m) for i in range(NHI * NY)] for m in (1, 2)]
LANES = 128
UPDATE_STEPS = 7


def swap_blocks(blocks, axis, sets):
    return lax.all_to_all(blocks, axis, 0, 0, axis_index_groups=sets)


def vmem_specs(count):
    return [pl.BlockSpec(memory_space=pltpu.VMEM)] * count


SMEM_SPEC = pl.BlockSpec(memory_space=pltpu.SMEM)
SMALL = pltpu.CompilerParams(vmem_limit_bytes=24 * 2**20)
LARGE = pltpu.CompilerParams(vmem_limit_bytes=56 * 2**20)


def pre_kernel(in_ref, enc_ref, out_ref, acc):
    step = pl.program_id(0)
    part = jnp.dot(in_ref[...], enc_ref[...], preferred_element_type=F32)

    @pl.when(step == 0)
    def _():
        acc[...] = part

    @pl.when(step > 0)
    def _():
        acc[...] += part

    @pl.when(step == pl.num_programs(0) - 1)
    def _():
        out_ref[...] = acc[...].astype(BF16)


def partial_pre(layer_in, enc):
    tokens, width = layer_in.shape
    feats = enc.shape[1]
    tile = width // 2
    return pl.pallas_call(
        pre_kernel,
        grid=(width // tile,),
        out_shape=jax.ShapeDtypeStruct((tokens, feats), BF16),
        in_specs=[
            pl.BlockSpec((tokens, tile), lambda i: (0, i)),
            pl.BlockSpec((tile, feats), lambda i: (i, 0)),
        ],
        out_specs=pl.BlockSpec((tokens, feats), lambda i: (0, 0)),
        scratch_shapes=[pltpu.VMEM((tokens, feats), F32)],
        compiler_params=LARGE,
    )(layer_in, enc)


def feature_kernel(mine_ref, other_ref, bias_ref, gate_ref, out_ref):
    pre = mine_ref[...] + other_ref[...] + bias_ref[...]
    features = (pre * gate_ref[...]).astype(BF16)
    for y in range(NY):
        out_ref[y] = features


def feature_copies(mine, other, bias, gate):
    return pl.pallas_call(
        feature_kernel,
        out_shape=jax.ShapeDtypeStruct((NY, *mine.shape), BF16),
        in_specs=vmem_specs(4),
        out_specs=vmem_specs(1)[0],
        compiler_params=SMALL,
    )(mine, other, bias, gate)


def parts_kernel(own_ref, other_ref, out_ref):
    half, feats = own_ref.shape
    block = feats // NY
    for y in range(NY):
        out_ref[y, 0:half, :] = own_ref[:, y * block : (y + 1) * block]
        out_ref[y, half : 2 * half, :] = other_ref[:, y * block : (y + 1) * block]


def latent_parts(own, other):
    half, feats = own.shape
    return pl.pallas_call(
        parts_kernel,
        out_shape=jax.ShapeDtypeStruct((NY, NCORE * half, feats // NY), BF16),
        in_specs=vmem_specs(2),
        out_specs=vmem_specs(1)[0],
        compiler_params=SMALL,
    )(own, other)


def dpre_kernel(
    mine_ref, other_ref, gate_ref, gram_ref, loss_ref, dec_ref, out_ref, rows_ref
):
    dpre = ((mine_ref[...] + other_ref[...]) * gate_ref[...]).astype(BF16)
    out_ref[...] = dpre
    pairs = lax.dot_general(dpre, dpre, (((1,), (1,)), ((), ())), preferred_element_type=F32)
    squares = jnp.sum(pairs * gram_ref[...]) + dec_ref[0, 0]
    lanes = lax.broadcasted_iota(jnp.int32, rows_ref.shape, 2)
    rows_ref[...] = jnp.where(lanes == 0, squares, jnp.where(lanes == 1, loss_ref[0, 0], 0.0))


def dpre_and_rows(mine, other, gate, gram, loss, dec_squares, devices):
    return pl.pallas_call(
        dpre_kernel,
        out_shape=(
            jax.ShapeDtypeStruct(mine.shape, BF16),
            jax.ShapeDtypeStruct((devices, 1, LANES), F32),
        ),
        in_specs=vmem_specs(4) + [SMEM_SPEC] * 2,
        out_specs=vmem_specs(2),
        compiler_params=SMALL,
    )(mine, other, gate, gram, loss, dec_squares)


def owner_kernel(
    slots, groups, seg_ref, got_ref, rows_ref, bias_ref, gram_ref, out_ref, loss_ref, sums, errs
):
    sums[...] = jnp.zeros_like(sums)
    for c in range(CHIPS):
        for e in range(slots):
            s = seg_ref[c, e]
            sums[s] += got_ref[c, e].astype(F32)
    recon = jnp.zeros_like(rows_ref)
    loss = jnp.zeros_like(rows_ref)
    grad_err = []
    for k in range(groups):
        recon += sums[k]
        residual = recon + bias_ref[...] - rows_ref[...]
        loss += residual * residual
        grad_err.append((2.0 * residual).astype(BF16).astype(F32))
    total = jnp.zeros_like(rows_ref)
    for k in range(groups - 1, -1, -1):
        total += grad_err[k]
        errs[k] = total.astype(BF16)
    loss_ref[0, 0] = jnp.sum(loss)
    for c in range(CHIPS):
        for e in range(slots):
            out_ref[c, e] = errs[seg_ref[c, e]]


def owner_step(slot_seg, got, rows, bias, gram, groups):
    chips, slots, per, width = got.shape
    vmem = pl.BlockSpec(memory_space=pltpu.VMEM)
    smem = pl.BlockSpec(memory_space=pltpu.SMEM)
    return pl.pallas_call(
        functools.partial(owner_kernel, slots, groups),
        out_shape=(
            jax.ShapeDtypeStruct(got.shape, BF16),
            jax.ShapeDtypeStruct((1, 1), F32),
        ),
        in_specs=[smem, vmem, vmem, vmem, pl.BlockSpec(memory_space=pl.ANY)],
        out_specs=(vmem, smem),
        scratch_shapes=[
            pltpu.VMEM((groups, per, width), F32),
            pltpu.VMEM((groups, per, width), BF16),
        ],
        compiler_params=pltpu.CompilerParams(vmem_limit_bytes=24 * 2**20),
    )(slot_seg, got, rows, bias, gram)


def update_kernel(
    limit, loss_scale, ypos_ref, rows_ref, in_ref, near_ref, far_ref, first_hbm, second_hbm,
    new_first_hbm, new_second_hbm, loss_ref, norm_ref,
    dpre, first, second, new_first, new_second, sems,
):
    width = in_ref.shape[1]
    tile = width // UPDATE_STEPS
    block = near_ref.shape[2]

    def copies(i):
        here = pl.ds(i * tile, tile)
        pairs = (
            (first_hbm, first), (second_hbm, second),
            (new_first, new_first_hbm), (new_second, new_second_hbm),
        )
        return [
            pltpu.make_async_copy(src.at[here, :], dst.at[here, :], sems.at[n, i])
            for n, (src, dst) in enumerate(pairs)
        ]

    steps = [copies(i) for i in range(UPDATE_STEPS)]
    for step in steps:
        step[0].start()
        step[1].start()
    for at, ref in ((0, near_ref), (2, far_ref)):
        for b in range(2):
            owner = ypos_ref[0, 0] ^ (at + b)
            dpre[:, pl.ds(pl.multiple_of(owner * block, block), block)] = ref[b]
    totals = jnp.sum(rows_ref[...], axis=0)
    lanes = lax.broadcasted_iota(jnp.int32, totals.shape, 1)
    squares = jnp.sum(jnp.where(lanes == 0, totals, 0.0), axis=1, keepdims=True)
    loss = jnp.sum(jnp.where(lanes == 1, totals, 0.0), axis=1, keepdims=True)
    norm = jnp.sqrt(squares)
    factor = limit / jnp.maximum(norm, limit)
    loss_ref[...] = loss * loss_scale
    norm_ref[...] = norm
    for i, step in enumerate(steps):
        here = slice(i * tile, (i + 1) * tile)
        grad = lax.dot_general(
            in_ref[:, here], dpre[...], (((0,), (0,)), ((), ())), preferred_element_type=F32
        )
        clipped = factor * grad
        step[0].wait()
        new_first[here, :] = (0.9 * first[here, :].astype(F32) + 0.1 * clipped).astype(BF16)
        step[2].start()
        step[1].wait()
        new_second[here, :] = (
            0.95 * second[here, :].astype(F32) + 0.05 * clipped * clipped
        ).astype(BF16)
        step[3].start()
    for step in steps:
        step[2].wait()
        step[3].wait()


def update(ypos, rows, layer_in, near, far, first, second, limit, loss_scale):
    width, feats = first.shape
    tokens = layer_in.shape[0]
    hbm = pl.BlockSpec(memory_space=pl.ANY)
    whole = pltpu.VMEM((width, feats), BF16)
    return pl.pallas_call(
        functools.partial(update_kernel, limit, loss_scale),
        out_shape=(jax.ShapeDtypeStruct((width, feats), BF16),) * 2
        + (jax.ShapeDtypeStruct((1, 1), F32),) * 2,
        in_specs=[SMEM_SPEC] + vmem_specs(4) + [hbm] * 2,
        out_specs=[hbm] * 2 + vmem_specs(2),
        scratch_shapes=[
            pltpu.VMEM((tokens, feats), BF16), whole, whole, whole, whole,
            pltpu.SemaphoreType.DMA((4, UPDATE_STEPS)),
        ],
        compiler_params=SMALL,
    )(ypos, rows, layer_in, near, far, first, second)


def on_device(
    streams, enc_weight, enc_bias, dec_weight, dec_bias, active, bounds, first_moment, second_moment
):
    lat_count = lax.axis_size("lat")
    layer_count = lax.axis_size("layer")
    lat = lax.axis_index("lat")
    layer = lax.axis_index("layer")
    tokens = streams.shape[0]
    width = streams.shape[2]
    feats_here = enc_weight.shape[2]
    groups = bounds.shape[0]
    core, chip = lat % NCORE, lat // NCORE
    ypos = layer % NY
    half = tokens // NCORE
    per = half // CHIPS
    quarter = tokens // NY
    layer_in = streams[:, 0, :]
    enc_local = enc_weight[0]
    dec_local = dec_weight[:, 0, :]

    own_start, other_start = core * half, (1 - core) * half
    own_in = lax.dynamic_slice_in_dim(layer_in, own_start, half, 0)
    other_in = lax.dynamic_slice_in_dim(layer_in, other_start, half, 0)
    turned_in = jnp.concatenate([own_in, other_in], axis=0)
    gate = active.astype(F32)
    gate_rows = lax.dynamic_slice_in_dim(gate, ypos * quarter, quarter, 0)
    gate_cols = lax.dynamic_slice_in_dim(gate, ypos * (feats_here // NY), feats_here // NY, 1)
    turned_gate = jnp.concatenate(
        [
            lax.dynamic_slice_in_dim(gate_cols, own_start, half, 0),
            lax.dynamic_slice_in_dim(gate_cols, other_start, half, 0),
        ],
        axis=0,
    )

    latent_ids = lat * feats_here + lax.iota(jnp.int32, feats_here)
    seg = jnp.sum((bounds[:, None] <= latent_ids[None, :]).astype(jnp.int32), axis=0)
    chip_feats = NCORE * feats_here
    chip_starts = lax.iota(jnp.int32, CHIPS) * chip_feats
    chip_first = jnp.sum((bounds[None, :] <= chip_starts[:, None]).astype(jnp.int32), axis=1)
    chip_last = jnp.sum(
        (bounds[None, :] <= chip_starts[:, None] + (chip_feats - 1)).astype(jnp.int32), axis=1
    )
    slots_needed = jnp.max(chip_last - chip_first) + 1
    first_here = lax.dynamic_index_in_dim(chip_first, chip, 0, keepdims=False)
    slot_here = lax.optimization_barrier(seg - first_here)

    pre_parts = partial_pre(layer_in, enc_local).reshape(NY, quarter, feats_here)
    pre_mine = jnp.sum(swap_blocks(pre_parts, "layer", Y_SETS).astype(F32), axis=0)
    pre_other = lax.ppermute(pre_mine, "layer", HI_SWAP)
    copies = feature_copies(pre_mine, pre_other, enc_bias[None], gate_rows)
    features = swap_blocks(copies, "layer", Y_SETS).reshape(tokens, feats_here)

    token_start = own_start + chip * per
    stream_rows = lax.dynamic_slice_in_dim(layer_in, token_start, per, 0).astype(F32)
    def middle(slots, features, dec_local):
        slot_ids = lax.iota(jnp.int32, slots)
        slot_mask = slot_here[None, :] == slot_ids[:, None]

        def by_slot(rows):
            spread = rows.reshape(CHIPS, 1, per, feats_here)
            kept = jnp.where(slot_mask[None, :, None, :], spread, jnp.zeros((), BF16))
            return kept.reshape(CHIPS * slots * per, feats_here)

        own_rows = by_slot(lax.dynamic_slice_in_dim(features, own_start, half, 0))
        other_rows = by_slot(lax.dynamic_slice_in_dim(features, other_start, half, 0))
        theirs = jnp.dot(other_rows, dec_local, preferred_element_type=F32).astype(BF16)
        got = lax.ppermute(theirs, "lat", CORE_SWAP).astype(F32)
        ours = jnp.dot(own_rows, dec_local, preferred_element_type=F32)
        chip_sum = (ours + got).astype(BF16).reshape(CHIPS, slots, per, width)
        chip_sum, turned = lax.optimization_barrier((chip_sum, turned_in))
        by_chip = swap_blocks(chip_sum, "lat", PLANE_SETS)
        gram = lax.dot_general(
            turned, turned, (((1,), (1,)), ((), ())), preferred_element_type=F32
        )
        for swap in Y_SWAPS:
            gram = gram + lax.ppermute(gram, "layer", swap)
        slot_seg = jnp.minimum(chip_first[:, None] + slot_ids[None, :], groups - 1)
        wanted, loss = owner_step(slot_seg, by_chip, stream_rows, dec_bias, gram, groups)
        own_err = swap_blocks(wanted, "lat", PLANE_SETS).reshape(CHIPS * slots * per, width)
        other_err = lax.ppermute(own_err, "lat", CORE_SWAP)


        def back(err):
            out = lax.dot_general(
                err, dec_local, (((1,), (1,)), ((), ())), preferred_element_type=F32
            ).reshape(CHIPS, slots, per, feats_here)
            kept = jnp.where(slot_mask[None, :, None, :], out, 0.0)
            return jnp.sum(kept, axis=1).astype(BF16).reshape(half, feats_here)

        parts = latent_parts(back(own_err), back(other_err))
        pairs = [
            lax.dot_general(r, r, (((1,), (1,)), ((), ())), preferred_element_type=F32)
            for r in (
                jnp.concatenate([own_rows, other_rows], axis=0),
                jnp.concatenate([own_err, other_err], axis=0),
            )
        ]
        dec_squares = jnp.sum(pairs[0] * pairs[1]).reshape(1, 1)
        return parts, gram, loss, dec_squares

    choices = sorted({min(2, groups), min(3, groups), groups})
    which = sum((slots_needed > c).astype(jnp.int32) for c in choices[:-1])
    parts, gram, loss, dec_squares = lax.switch(
        which, [functools.partial(middle, s) for s in choices], features, dec_local
    )
    mine = jnp.sum(swap_blocks(parts, "layer", Y_SETS).astype(F32), axis=0)
    other = lax.ppermute(mine, "layer", HI_SWAP)
    dpre, rows = dpre_and_rows(
        mine, other, turned_gate, gram, loss, dec_squares, lat_count * layer_count
    )
    rows = lax.all_to_all(rows, ("lat", "layer"), 0, 0)
    near = jnp.stack([dpre, lax.ppermute(dpre, "layer", Y_SWAPS[0])])
    far = lax.ppermute(near, "layer", Y_SWAPS[1])
    limit = math.sqrt(2.0 * layer_count * width * feats_here * lat_count)
    new_first, new_second, loss_value, grad_norm = update(
        ypos.reshape(1, 1), rows, turned_in, near, far, first_moment[0], second_moment[0],
        limit, 1.0 / (tokens * layer_count * width),
    )
    return (new_first[None], new_second[None], loss_value[0, 0], grad_norm[0, 0])


def solution(mesh):
    in_specs = (
        P(None, "layer", None),
        P("layer", None, "lat"),
        P("lat"),
        P("lat", "layer", None),
        P("layer", None),
        P(None, "lat"),
        P(),
        P("layer", None, "lat"),
        P("layer", None, "lat"),
    )
    out_specs = (P("layer", None, "lat"), P("layer", None, "lat"), P(), P())
    return jax.shard_map(
        on_device, mesh=mesh, in_specs=in_specs, out_specs=out_specs, check_vma=False
    )
```

time: 185 us -> 166 us (0.90)
  blocking collectives: 37.3 us -> 28.3 us
  Pallas kernels: 20.6 us -> 14.7 us
  matrix products: 12.2 us -> 6.34 us
  starting transfers between devices: 48.5 us -> 54.3 us
  local copies, waits for them, and re-layouts: 5.78 us -> 3.65 us
    all_to_all x4, waiting for transfers between devices: 37.6 us -> 22.5 us  [swap_blocks(): return lax.all_to_all(blocks, axis, 0, 0, axis_index_groups=sets)]
    all_to_all x2 -> x1, blocking collectives: 37.3 us -> 28.3 us  [swap_blocks(): return lax.all_to_all(blocks, axis, 0, 0, axis_index_groups=sets)]
    ppermute x2, waiting for transfers between devices: 7.65 us -> 13.7 us  [middle(): gram = gram + lax.ppermute(gram, 'layer', swap)]
    ppermute x2 -> x4, starting transfers between devices: 7.78 us -> 12.2 us  [the longest x1 4.72 us: middle(): got = lax.ppermute(theirs, 'lat', CORE_SWAP).astype(F32)]
    ppermute x2 -> x4, waiting for transfers between devices: 3.47 us -> 7.71 us  [the longest x1 3 us: on_device(): far = lax.ppermute(near, 'layer', Y_SWAPS[1])]
    dot_general x3 -> x4, matrix products: 6.84 us -> 3.42 us  [the longest x2 2.35 us: middle(): lax.dot_general(r, r, (((1,), (1,)), ((), ())), preferred_element_type=F32)]
    pallas_call x4 -> x3, Pallas kernels: 12.2 us -> 9.2 us  [the longest x1 5.09 us: update(): pl.pallas_call(functools.partial(update_kernel, limit, loss_scale), out_s...]
    pallas_call x1, Pallas kernels: 6 us -> 3.1 us  [partial_pre(): pl.pallas_call(pre_kernel, grid=(width // tile,), out_shape=jax.ShapeDtyp...]
  transfers between devices with their start and end apart: 11 -> 13, of which waited for: 8 -> 11; matrix products, arithmetic and copies ran while one was open for 9% -> 5% of each run, Pallas kernels for 1% -> 0%
where the time goes in v4:
time: 166 us; the launch traced here: 165 us
  starting transfers between devices  54.3 us (33%)
  waiting for transfers between devices  51.6 us (31%)
  blocking collectives  28.3 us (17%)
  Pallas kernels  14.7 us (9%)
  matrix products  6.34 us (4%)
  other arithmetic  4.44 us (3%)
  local copies, waits for them, and re-layouts  3.65 us (2%)
  between operations  1.68 us (1%)
    all_to_all x1, blocking collectives, swap_blocks(): return lax.all_to_all(blocks, axis, 0, 0, axis_index_groups=sets)  28.3 us
    all_to_all x4, waiting for transfers between devices, swap_blocks(): return lax.all_to_all(blocks, axis, 0, 0, axis_index_groups=sets)  22.5 us
    all_to_all x4, starting transfers between devices, swap_blocks(): return lax.all_to_all(blocks, axis, 0, 0, axis_index_groups=sets)  19.3 us
    ppermute x2, waiting for transfers between devices, middle(): gram = gram + lax.ppermute(gram, 'layer', swap)  13.7 us
    all_to_all x1, starting transfers between devices, on_device(): rows = lax.all_to_all(rows, ('lat', 'layer'), 0, 0)  12.6 us
    ppermute x1, starting transfers between devices, on_device(): pre_other = lax.ppermute(pre_mine, 'layer', HI_SWAP)  7.02 us
    all_to_all x1, waiting for transfers between devices, on_device(): rows = lax.all_to_all(rows, ('lat', 'layer'), 0, 0)  6.78 us
    pallas_call x1, Pallas kernels, update(): pl.pallas_call(functools.partial(update_kernel, limit, loss_scale), out_s...  5.09 us
  transfers between devices with their start and end apart: 13, of which 11 were waited for; matrix products, arithmetic and copies ran while one was open for 5% of the time, Pallas kernels for 0%

profile of v4, /device:TPU:1, one launch (start us, length us, event | category | flops | bytes accessed | tf_op | source)
XLA Modules:
  0.0 165.2 jit_solution(1374858312351811209)
XLA Ops:
  0.7 3.1 %shard_map.120 = bf16[256,512]{1,0:T(8,128)(2,1)} custom-call(bf16[256,1792]{1,0:T(8,128)(2,1)} %bitcast.141, bf16[1792,512]{1,0:T(8,128)(2,1)} %bitcast.147), custom_call_target="tpu_custom_call" | custom-call | tf_op jit(solution)/shard_map/pallas_call | solution.py:59
  3.7 5.0 %all-to-all-start.6 = ((bf16[4,64,512]{2,1,0:T(8,128)(2,1)}), bf16[4,64,512]{2,1,0:T(8,128)(2,1)S(1)}, u32[]{:S(2)}, u32[]{:S(2)}) async-start(bf16[4,64,512]{2,1,0:T(8,128)(2,1)} %bitcast.154), calls=%async_computation.6 | async-start | bytes 524288 | tf_op jit(solution)/shard_map/all_to_all | solution.py:26
  8.8 0.1 convert_reduce_fusion.2
  9.0 0.6 dynamic_slice.45
  9.7 0.8 broadcast_subtract_fusion
  10.5 3.8 %all-to-all-done.6 = bf16[4,64,512]{2,1,0:T(8,128)(2,1)S(1)} async-done(((bf16[4,64,512]{2,1,0:T(8,128)(2,1)}), bf16[4,64,512]{2,1,0:T(8,128)(2,1)S(1)}, u32[]{:S(2)}, u32[]{:S(2)}) %all-to-all-start.6) | async-done | bytes 262176 | tf_op jit(solution)/shard_map/all_to_all | solution.py:26
  14.3 7.0 %collective-permute-start.12 = (f32[64,512]{1,0:T(8,128)S(1)}, f32[64,512]{1,0:T(8,128)S(1)}, u32[]{:S(2)}, u32[]{:S(2)}) collective-permute-start(f32[64,512]{1,0:T(8,128)S(1)} %convert_reduce_fusion.1.mine_ref), channel_id=1, source_target_pairs={{0,4},{1,5},{2,6},{3,7},{4,0},{5,1},{6,2},{7,3},{8,12},{9,13},{10,... | collective-permute-start | bytes 393224 | tf_op jit(solution)/shard_map/ppermute | solution.py:302
  21.4 0.6 subtract_reduce_fusion
  22.6 1.1 convert_element_type.105
  23.8 0.8 shard_map.121
  24.6 3.4 %all-to-all-start.7 = ((bf16[4,64,512]{2,1,0:T(8,128)(2,1)}), bf16[4,64,512]{2,1,0:T(8,128)(2,1)S(1)}, u32[]{:S(2)}, u32[]{:S(2)}) async-start(bf16[4,64,512]{2,1,0:T(8,128)(2,1)} %shard_map.121), calls=%async_computation.7 | async-start | bytes 524288 | tf_op jit(solution)/shard_map/all_to_all | solution.py:26
  28.0 1.4 bitcast_convert_fusion
  29.4 4.1 %all-to-all-done.7 = bf16[4,64,512]{2,1,0:T(8,128)(2,1)S(1)} async-done(((bf16[4,64,512]{2,1,0:T(8,128)(2,1)}), bf16[4,64,512]{2,1,0:T(8,128)(2,1)S(1)}, u32[]{:S(2)}, u32[]{:S(2)}) %all-to-all-start.7) | async-done | bytes 262176 | tf_op jit(solution)/shard_map/all_to_all | solution.py:26
  33.5 78.3 %conditional.1 = (bf16[4,256,128]{2,1,0:T(8,128)(2,1)}, f32[256,256]{1,0:T(8,128)}, f32[1,1]{1,0:T(1,128)}, f32[1,1]{1,0:T(1,128)}) conditional(s32[]{:T(128)} %clamp.11, (s32[512]{0:T(512)S(1)}, s32[16]{0:T(128)}, s32[]{:T(128)}, bf16[256,512]{1,0:T(8,128)(2,1)S(1)}, bf16[512,1792]{1,0:T(8,128)(2,1)S(1)}, /*index=5*/s32[]{:T(128)}, ...), branch_computations={%region_5.9_spmd, %region_9.13_spmd, %region_13.17_spmd} | conditional | flops 12503877632 | bytes 105231552 | solution.py:356
  33.7 0.6 convolution_convert_fusion
  34.4 0.3 copy-done.27
  34.6 4.7 %collective-permute-start = (bf16[256,1792]{1,0:T(8,128)(2,1)S(1)}, bf16[256,1792]{1,0:T(8,128)(2,1)S(1)}, u32[]{:S(2)}, u32[]{:S(2)}) collective-permute-start(bf16[256,1792]{1,0:T(8,128)(2,1)S(1)} %convolution_convert_fusion), channel_id=1, source_target_pairs={{0,8},{8,0},{16,24},{24,16},{32,40},{40,32},{48,56},{56,48},{64,72... | collective-permute-start | bytes 2752520 | tf_op jit(solution)/shard_map/cond/branch_0_fun/ppermute | solution.py:320
  39.4 2.1 %collective-permute-done = bf16[256,1792]{1,0:T(8,128)(2,1)S(1)} collective-permute-done((bf16[256,1792]{1,0:T(8,128)(2,1)S(1)}, bf16[256,1792]{1,0:T(8,128)(2,1)S(1)}, u32[]{:S(2)}, u32[]{:S(2)}) %collective-permute-start) | collective-permute-done | bytes 917536 | tf_op jit(solution)/shard_map/cond/branch_0_fun/ppermute | solution.py:320
  41.5 1.6 add_convert_fusion
  43.0 7.4 %all-to-all-start = ((bf16[16,2,8,1792]{3,2,1,0:T(8,128)(2,1)}), bf16[16,2,8,1792]{3,2,1,0:T(8,128)(2,1)S(1)}, u32[]{:S(2)}, u32[]{:S(2)}) async-start(bf16[16,2,8,1792]{3,2,1,0:T(8,128)(2,1)} %bitcast.142), calls=%async_computation | async-start | bytes 1835008 | tf_op jit(solution)/shard_map/cond/branch_0_fun/all_to_all | solution.py:26
  50.4 0.4 fusion.61
  50.9 0.4 collective-permute-start.1
  51.2 6.9 %collective-permute-done.1 = f32[256,256]{1,0:T(8,128)S(1)} collective-permute-done((f32[256,256]{1,0:T(8,128)S(1)}, f32[256,256]{1,0:T(8,128)S(1)}, u32[]{:S(2)}, u32[]{:S(2)}) %collective-permute-start.1) | collective-permute-done | bytes 262176 | tf_op jit(solution)/shard_map/cond/branch_0_fun/ppermute | solution.py:329
  58.2 1.0 collective-permute-start.2
  59.3 6.8 %collective-permute-done.2 = f32[256,256]{1,0:T(8,128)S(1)} collective-permute-done((f32[256,256]{1,0:T(8,128)S(1)}, f32[256,256]{1,0:T(8,128)S(1)}, u32[]{:S(2)}, u32[]{:S(2)}) %collective-permute-start.2) | collective-permute-done | bytes 262176 | tf_op jit(solution)/shard_map/cond/branch_0_fun/ppermute | solution.py:329
  66.1 8.5 %all-to-all-done.got_ref = bf16[16,2,8,1792]{3,2,1,0:T(8,128)(2,1)S(1)} async-done(((bf16[16,2,8,1792]{3,2,1,0:T(8,128)(2,1)}), bf16[16,2,8,1792]{3,2,1,0:T(8,128)(2,1)S(1)}, u32[]{:S(2)}, u32[]{:S(2)}) %all-to-all-start) | async-done | bytes 917536 | tf_op jit(solution)/shard_map/cond/branch_0_fun/all_to_all | solution.py:26
  74.6 1.6 branch_0_fun.2
  76.3 28.3 %all_to_all.44 = bf16[16,2,8,1792]{3,2,1,0:T(8,128)(2,1)S(1)} all-to-all(bf16[16,2,8,1792]{3,2,1,0:T(8,128)(2,1)S(1)} %get-tuple-element.65), channel_id=1, replica_groups={{0,16,32,48,64,80,96,112,128,144,160,176,192,208,224,240},{8,24,40,56,7..., dimensions={0} | all-to-all | bytes 1835008 | tf_op jit(solution)/shard_map/cond/branch_0_fun/all_to_all | solution.py:26
  104.6 1.7 %collective-permute-start.3 = (bf16[256,1792]{1,0:T(8,128)(2,1)S(1)}, bf16[256,1792]{1,0:T(8,128)(2,1)S(1)}, u32[]{:S(2)}, u32[]{:S(2)}) collective-permute-start(bf16[256,1792]{1,0:T(8,128)(2,1)S(1)} %bitcast.157), channel_id=1, source_target_pairs={{0,8},{8,0},{16,24},{24,16},{32,40},{40,32},{48,56},{56,48},{64,72... | collective-permute-start | bytes 2752520 | tf_op jit(solution)/shard_map/cond/branch_0_fun/ppermute | solution.py:333
  106.3 0.5 fusion.14
  106.8 0.7 fusion.9
  107.5 0.9 collective-permute-done.3
  108.4 0.7 fusion.62
  109.2 0.7 branch_0_fun.3
  109.9 1.9 %multiply_reduce_fusion = f32[]{:T(128)} fusion(f32[512,512]{1,0:T(8,128)S(1)} %fusion.14, bf16[256,1792]{1,0:T(8,128)(2,1)S(1)} %collective-permute-done.3, bf16[256,1792]{1,0:T(8,128)(2,1)S(1)} %bitcast.158), kind=kOutput, calls=%fused_computation.10 | convolution fusion | flops 943718400 | bytes 2883588 | tf_op jit(solution)/shard_map/cond/branch_0_fun/dot_general | solution.py:345
  111.8 3.5 %all-to-all-start.8 = ((bf16[4,256,128]{2,1,0:T(8,128)(2,1)}), bf16[4,256,128]{2,1,0:T(8,128)(2,1)S(1)}, u32[]{:S(2)}, u32[]{:S(2)}) async-start(bf16[4,256,128]{2,1,0:T(8,128)(2,1)} %get-tuple-element.107), calls=%async_computation.8 | async-start | bytes 524288 | tf_op jit(solution)/shard_map/all_to_all | solution.py:26
  115.4 6.1 %all-to-all-done.8 = bf16[4,256,128]{2,1,0:T(8,128)(2,1)S(1)} async-done(((bf16[4,256,128]{2,1,0:T(8,128)(2,1)}), bf16[4,256,128]{2,1,0:T(8,128)(2,1)S(1)}, u32[]{:S(2)}, u32[]{:S(2)}) %all-to-all-start.8) | async-done | bytes 262176 | tf_op jit(solution)/shard_map/all_to_all | solution.py:26
  121.5 4.2 %collective-permute-start.13 = (f32[256,128]{1,0:T(8,128)S(1)}, f32[256,128]{1,0:T(8,128)S(1)}, u32[]{:S(2)}, u32[]{:S(2)}) collective-permute-start(f32[256,128]{1,0:T(8,128)S(1)} %convert_reduce_fusion.mine_ref), channel_id=1, source_target_pairs={{0,4},{1,5},{2,6},{3,7},{4,0},{5,1},{6,2},{7,3},{8,12},{9,13},{10,... | collective-permute-start | bytes 393224 | tf_op jit(solution)/shard_map/ppermute | solution.py:360
  125.7 1.1 fusion.60
  126.8 2.6 %collective-permute-done.13.other_ref = f32[256,128]{1,0:T(8,128)S(1)} collective-permute-done((f32[256,128]{1,0:T(8,128)S(1)}, f32[256,128]{1,0:T(8,128)S(1)}, u32[]{:S(2)}, u32[]{:S(2)}) %collective-permute-start.13) | collective-permute-done | bytes 131104 | tf_op jit(solution)/shard_map/ppermute | solution.py:360
  129.4 3.4 %shard_map.122 = (bf16[256,128]{1,0:T(8,128)(2,1)S(1)}, f32[256,1,128]{2,1,0:T(1,128)}) custom-call(f32[256,128]{1,0:T(8,128)S(1)} %convert_reduce_fusion.mine_ref, f32[256,128]{1,0:T(8,128)S(1)} %collective-permute-done.13.other_ref, f32[256,128]{1,0:T(8,128)S(1)} %pad_maximum_fusion.1.gate_ref, f32[256,256]{1,0:T(8,128)} %get-tuple-element.108.gram_ref, ...), custom_call_target="tpu_custom_call" | custom-call | tf_op jit(solution)/shard_map/pallas_call | solution.py:121
  132.7 0.3 collective-permute-start.14
  133.0 12.6 %all-to-all-start.9 = ((f32[256,1,128]{2,1,0:T(1,128)}), f32[256,1,128]{2,1,0:T(1,128)S(1)}, u32[]{:S(2)}, u32[]{:S(2)}) async-start(f32[256,1,128]{2,1,0:T(1,128)} %get-tuple-element.111), calls=%async_computation.9 | async-start | bytes 262144 | tf_op jit(solution)/shard_map/all_to_all | solution.py:364
  145.7 3.0 %collective-permute-start.15 = (bf16[2,256,128]{2,1,0:T(8,128)(2,1)S(1)}, bf16[2,256,128]{2,1,0:T(8,128)(2,1)S(1)}, u32[]{:S(2)}, u32[]{:S(2)}) collective-permute-start(bf16[2,256,128]{2,1,0:T(8,128)(2,1)S(1)} %pad_maximum_fusion.2.near_ref), channel_id=1, source_target_pairs={{0,2},{1,3},{2,0},{3,1},{4,6},{5,7},{6,4},{7,5},{8,10},{9,11},{10,... | collective-permute-start | bytes 393224 | tf_op jit(solution)/shard_map/ppermute | solution.py:366
  148.7 3.0 %collective-permute-done.15.far_ref = bf16[2,256,128]{2,1,0:T(8,128)(2,1)S(1)} collective-permute-done((bf16[2,256,128]{2,1,0:T(8,128)(2,1)S(1)}, bf16[2,256,128]{2,1,0:T(8,128)(2,1)S(1)}, u32[]{:S(2)}, u32[]{:S(2)}) %collective-permute-start.15) | collective-permute-done | bytes 131104 | tf_op jit(solution)/shard_map/ppermute | solution.py:366
  151.7 6.8 %all-to-all-done.9.rows_ref = f32[256,1,128]{2,1,0:T(1,128)S(1)} async-done(((f32[256,1,128]{2,1,0:T(1,128)}), f32[256,1,128]{2,1,0:T(1,128)S(1)}, u32[]{:S(2)}, u32[]{:S(2)}) %all-to-all-start.9) | async-done | bytes 131104 | tf_op jit(solution)/shard_map/all_to_all | solution.py:364
  158.5 1.5 copy-done.1
  160.0 5.1 %shard_map.123 = (bf16[1792,512]{1,0:T(8,128)(2,1)}, bf16[1792,512]{1,0:T(8,128)(2,1)}, f32[1,1]{1,0:T(1,128)}, f32[1,1]{1,0:T(1,128)}) custom-call(s32[1,1]{1,0:T(1,128)} %bitcast.36.ypos_ref, f32[256,1,128]{2,1,0:T(1,128)S(1)} %all-to-all-done.9.rows_ref, bf16[256,1792]{1,0:T(8,128)(2,1)S(1)} %pad_maximum_fusion.in_ref, ...), custom_call_target="tpu_custom_call" | custom-call | tf_op jit(solution)/shard_map/pallas_call | solution.py:239
  (53 shorter events, 0.8 us)
Async XLA Ops:
  0.6 8.9 %copy-start.13 = (bf16[256,1,1792]{2,0,1:T(8,128)(2,1)S(1)}, bf16[256,1,1792]{2,0,1:T(8,128)(2,1)}, u32[]{:S(2)}) copy-start(bf16[256,1,1792]{2,0,1:T(8,128)(2,1)} %param.12) | copy-start | bytes 2752516
  0.6 8.1 %copy-start.33 = (s32[5]{0:T(128)S(1)}, s32[5]{0:T(128)}, u32[]{:S(2)}) copy-start(s32[5]{0:T(128)} %param.18) | copy-start | bytes 64
  3.7 10.5 %all-to-all-start.6 = ((bf16[4,64,512]{2,1,0:T(8,128)(2,1)}), bf16[4,64,512]{2,1,0:T(8,128)(2,1)S(1)}, u32[]{:S(2)}, u32[]{:S(2)}) async-start(bf16[4,64,512]{2,1,0:T(8,128)(2,1)} %bitcast.154), calls=%async_computation.6 | async-start | bytes 524288 | tf_op jit(solution)/shard_map/all_to_all | solution.py:26
  9.0 12.4 %copy-start.29 = (s32[16]{0:T(128)}, s32[16]{0:T(128)S(1)}, u32[]{:S(2)}) copy-start(s32[16]{0:T(128)S(1)} %get-tuple-element.117) | copy-start | bytes 196
  9.6 14.2 %copy-start.2 = (f32[512]{0:T(512)S(1)}, f32[512]{0:T(512)}, u32[]{:S(2)}) copy-start(f32[512]{0:T(512)} %param.14) | copy-start | bytes 6148
  9.7 23.8 %copy-start.3 = (bf16[512,1,1792]{2,0,1:T(8,128)(2,1)S(1)}, bf16[512,1,1792]{2,0,1:T(8,128)(2,1)}, u32[]{:S(2)}) copy-start(bf16[512,1,1792]{2,0,1:T(8,128)(2,1)} %param.15) | copy-start | bytes 5505028
  9.7 23.8 %copy-start.26 = (f32[1,1792]{1,0:T(1,128)S(1)}, f32[1,1792]{1,0:T(1,128)}, u32[]{:S(2)}) copy-start(f32[1,1792]{1,0:T(1,128)} %param.16) | copy-start | bytes 21508
  14.3 9.5 %collective-permute-start.12 = (f32[64,512]{1,0:T(8,128)S(1)}, f32[64,512]{1,0:T(8,128)S(1)}, u32[]{:S(2)}, u32[]{:S(2)}) collective-permute-start(f32[64,512]{1,0:T(8,128)S(1)} %convert_reduce_fusion.1.mine_ref), channel_id=1, source_target_pairs={{0,4},{1,5},{2,6},{3,7},{4,0},{5,1},{6,2},{7,3},{8,12},{9,13},{10,... | collective-permute-start | bytes 393224 | tf_op jit(solution)/shard_map/ppermute | solution.py:302
  23.7 9.8 %copy-start.14 = (f32[256,512]{1,0:T(8,128)}, f32[256,512]{1,0:T(8,128)S(1)}, u32[]{:S(2)}) copy-start(f32[256,512]{1,0:T(8,128)S(1)} %convert_element_type.105) | copy-start | bytes 1572868
  24.6 8.9 %all-to-all-start.7 = ((bf16[4,64,512]{2,1,0:T(8,128)(2,1)}), bf16[4,64,512]{2,1,0:T(8,128)(2,1)S(1)}, u32[]{:S(2)}, u32[]{:S(2)}) async-start(bf16[4,64,512]{2,1,0:T(8,128)(2,1)} %shard_map.121), calls=%async_computation.7 | async-start | bytes 524288 | tf_op jit(solution)/shard_map/all_to_all | solution.py:26
  33.5 7.9 %copy-start.4 = (bf16[512,1792]{1,0:T(8,128)(2,1)}, bf16[512,1792]{1,0:T(8,128)(2,1)S(1)}, u32[]{:S(2)}) copy-start(bf16[512,1792]{1,0:T(8,128)(2,1)S(1)} %get-tuple-element.58) | copy-start | bytes 5505028 | tf_op jit(solution)/shard_map/cond
  33.6 1.1 copy-start.27
  33.7 9.3 %copy-start.15 = (bf16[16,2,8,512]{3,2,1,0:T(8,128)(2,1)}, bf16[16,2,8,512]{3,2,1,0:T(8,128)(2,1)S(1)}, u32[]{:S(2)}) copy-start(bf16[16,2,8,512]{3,2,1,0:T(8,128)(2,1)S(1)} %get-tuple-element.122) | copy-start | bytes 786436 | tf_op jit(solution)/shard_map/cond
  34.6 6.8 %collective-permute-start = (bf16[256,1792]{1,0:T(8,128)(2,1)S(1)}, bf16[256,1792]{1,0:T(8,128)(2,1)S(1)}, u32[]{:S(2)}, u32[]{:S(2)}) collective-permute-start(bf16[256,1792]{1,0:T(8,128)(2,1)S(1)} %convolution_convert_fusion), channel_id=1, source_target_pairs={{0,8},{8,0},{16,24},{24,16},{32,40},{40,32},{48,56},{56,48},{64,72... | collective-permute-start | bytes 2752520 | tf_op jit(solution)/shard_map/cond/branch_0_fun/ppermute | solution.py:320
  43.0 31.6 %all-to-all-start = ((bf16[16,2,8,1792]{3,2,1,0:T(8,128)(2,1)}), bf16[16,2,8,1792]{3,2,1,0:T(8,128)(2,1)S(1)}, u32[]{:S(2)}, u32[]{:S(2)}) async-start(bf16[16,2,8,1792]{3,2,1,0:T(8,128)(2,1)} %bitcast.142), calls=%async_computation | async-start | bytes 1835008 | tf_op jit(solution)/shard_map/cond/branch_0_fun/all_to_all | solution.py:26
  50.4 8.8 %copy-start.30 = (s32[16]{0:T(128)S(1)}, s32[16]{0:T(128)}, u32[]{:S(2)}) copy-start(s32[16]{0:T(128)} %get-tuple-element.55) | copy-start | bytes 196 | tf_op jit(solution)/shard_map/cond
  50.4 24.2 %copy-start.17 = (f32[8,1792]{1,0:T(8,128)S(1)}, f32[8,1792]{1,0:T(8,128)}, u32[]{:S(2)}) copy-start(f32[8,1792]{1,0:T(8,128)} %get-tuple-element.62.rows_ref) | copy-start | bytes 172036 | tf_op jit(solution)/shard_map/cond
  50.9 7.3 %collective-permute-start.1 = (f32[256,256]{1,0:T(8,128)S(1)}, f32[256,256]{1,0:T(8,128)S(1)}, u32[]{:S(2)}, u32[]{:S(2)}) collective-permute-start(f32[256,256]{1,0:T(8,128)S(1)} %fusion.61), channel_id=1, source_target_pairs={{0,1},{1,0},{2,3},{3,2},{4,5},{5,4},{6,7},{7,6},{8,9},{9,8},{10,11... | collective-permute-start | bytes 786440 | tf_op jit(solution)/shard_map/cond/branch_0_fun/ppermute | solution.py:329
  58.2 7.9 %collective-permute-start.2 = (f32[256,256]{1,0:T(8,128)S(1)}, f32[256,256]{1,0:T(8,128)S(1)}, u32[]{:S(2)}, u32[]{:S(2)}) collective-permute-start(f32[256,256]{1,0:T(8,128)S(1)} %add.112), channel_id=1, source_target_pairs={{0,2},{1,3},{2,0},{3,1},{4,6},{5,7},{6,4},{7,5},{8,10},{9,11},{10,... | collective-permute-start | bytes 786440 | tf_op jit(solution)/shard_map/cond/branch_0_fun/ppermute | solution.py:329
  59.3 47.0 %copy-start.16 = (bf16[16,2,8,512]{3,2,1,0:T(8,128)(2,1)S(1)}, bf16[16,2,8,512]{3,2,1,0:T(8,128)(2,1)}, u32[]{:S(2)}) copy-start(bf16[16,2,8,512]{3,2,1,0:T(8,128)(2,1)} %copy-done.15) | copy-start | bytes 786436 | tf_op jit(solution)/shard_map/cond
  66.1 40.7 %copy-start.10 = (f32[256,256]{1,0:T(8,128)}, f32[256,256]{1,0:T(8,128)S(1)}, u32[]{:S(2)}) copy-start(f32[256,256]{1,0:T(8,128)S(1)} %add.113.gram_ref) | copy-start | bytes 786436 | tf_op jit(solution)/shard_map/cond
  76.3 30.5 %copy-start.5 = (bf16[512,1792]{1,0:T(8,128)(2,1)S(1)}, bf16[512,1792]{1,0:T(8,128)(2,1)}, u32[]{:S(2)}) copy-start(bf16[512,1792]{1,0:T(8,128)(2,1)} %copy-done.4) | copy-start | bytes 5505028 | tf_op jit(solution)/shard_map/cond
  76.3 30.5 %copy-start.28 = (pred[2,512]{1,0:T(4,128)(4,1)S(1)}, pred[2,512]{1,0:T(4,128)(4,1)}, u32[]{:S(2)}) copy-start(pred[2,512]{1,0:T(4,128)(4,1)} %copy-done.27) | copy-start | bytes 3076 | tf_op jit(solution)/shard_map/cond
  104.6 3.8 %collective-permute-start.3 = (bf16[256,1792]{1,0:T(8,128)(2,1)S(1)}, bf16[256,1792]{1,0:T(8,128)(2,1)S(1)}, u32[]{:S(2)}, u32[]{:S(2)}) collective-permute-start(bf16[256,1792]{1,0:T(8,128)(2,1)S(1)} %bitcast.157), channel_id=1, source_target_pairs={{0,8},{8,0},{16,24},{24,16},{32,40},{40,32},{48,56},{56,48},{64,72... | collective-permute-start | bytes 2752520 | tf_op jit(solution)/shard_map/cond/branch_0_fun/ppermute | solution.py:333
  111.8 46.7 %copy-start = (bf16[1,1792,512]{2,1,0:T(8,128)(2,1)S(1)}, bf16[1,1792,512]{2,1,0:T(8,128)(2,1)}, u32[]{:S(2)}) copy-start(bf16[1,1792,512]{2,1,0:T(8,128)(2,1)} %param.19) | copy-start | bytes 5505028
  111.8 9.6 %all-to-all-start.8 = ((bf16[4,256,128]{2,1,0:T(8,128)(2,1)}), bf16[4,256,128]{2,1,0:T(8,128)(2,1)S(1)}, u32[]{:S(2)}, u32[]{:S(2)}) async-start(bf16[4,256,128]{2,1,0:T(8,128)(2,1)} %get-tuple-element.107), calls=%async_computation.8 | async-start | bytes 524288 | tf_op jit(solution)/shard_map/all_to_all | solution.py:26
  121.5 7.9 %collective-permute-start.13 = (f32[256,128]{1,0:T(8,128)S(1)}, f32[256,128]{1,0:T(8,128)S(1)}, u32[]{:S(2)}, u32[]{:S(2)}) collective-permute-start(f32[256,128]{1,0:T(8,128)S(1)} %convert_reduce_fusion.mine_ref), channel_id=1, source_target_pairs={{0,4},{1,5},{2,6},{3,7},{4,0},{5,1},{6,2},{7,3},{8,12},{9,13},{10,... | collective-permute-start | bytes 393224 | tf_op jit(solution)/shard_map/ppermute | solution.py:360
  132.7 12.9 %collective-permute-start.14 = (bf16[256,128]{1,0:T(8,128)(2,1)S(1)}, bf16[256,128]{1,0:T(8,128)(2,1)S(1)}, u32[]{:S(2)}, u32[]{:S(2)}) collective-permute-start(bf16[256,128]{1,0:T(8,128)(2,1)S(1)} %get-tuple-element.112), channel_id=1, source_target_pairs={{0,1},{1,0},{2,3},{3,2},{4,5},{5,4},{6,7},{7,6},{8,9},{9,8},{10,11... | collective-permute-start | bytes 196616 | tf_op jit(solution)/shard_map/ppermute | solution.py:365
  133.0 25.4 %all-to-all-start.9 = ((f32[256,1,128]{2,1,0:T(1,128)}), f32[256,1,128]{2,1,0:T(1,128)S(1)}, u32[]{:S(2)}, u32[]{:S(2)}) async-start(f32[256,1,128]{2,1,0:T(1,128)} %get-tuple-element.111), calls=%async_computation.9 | async-start | bytes 262144 | tf_op jit(solution)/shard_map/all_to_all | solution.py:364
  145.7 6.0 %collective-permute-start.15 = (bf16[2,256,128]{2,1,0:T(8,128)(2,1)S(1)}, bf16[2,256,128]{2,1,0:T(8,128)(2,1)S(1)}, u32[]{:S(2)}, u32[]{:S(2)}) collective-permute-start(bf16[2,256,128]{2,1,0:T(8,128)(2,1)S(1)} %pad_maximum_fusion.2.near_ref), channel_id=1, source_target_pairs={{0,2},{1,3},{2,0},{3,1},{4,6},{5,7},{6,4},{7,5},{8,10},{9,11},{10,... | collective-permute-start | bytes 393224 | tf_op jit(solution)/shard_map/ppermute | solution.py:366
  158.5 1.5 copy-start.1

commit v5 on v4

--- a/solution.py
+++ b/solution.py
@@ -31,7 +31,7 @@
 
 
 SMEM_SPEC = pl.BlockSpec(memory_space=pltpu.SMEM)
-SMALL = pltpu.CompilerParams(vmem_limit_bytes=24 * 2**20)
+SMALL = pltpu.CompilerParams(vmem_limit_bytes=10 * 2**20)
 LARGE = pltpu.CompilerParams(vmem_limit_bytes=56 * 2**20)
 
 
@@ -107,32 +107,41 @@
 
 
 def dpre_kernel(
-    mine_ref, other_ref, gate_ref, gram_ref, loss_ref, dec_ref, out_ref, rows_ref
+    mine_ref, other_ref, gate_ref, scalars_ref, gram_hbm, out_ref, rows_ref, gram, sem
 ):
+    copy = pltpu.make_async_copy(gram_hbm, gram, sem)
+    copy.start()
     dpre = ((mine_ref[...] + other_ref[...]) * gate_ref[...]).astype(BF16)
     out_ref[...] = dpre
     pairs = lax.dot_general(dpre, dpre, (((1,), (1,)), ((), ())), preferred_element_type=F32)
-    squares = jnp.sum(pairs * gram_ref[...]) + dec_ref[0, 0]
-    lanes = lax.broadcasted_iota(jnp.int32, rows_ref.shape, 2)
-    rows_ref[...] = jnp.where(lanes == 0, squares, jnp.where(lanes == 1, loss_ref[0, 0], 0.0))
-
-
-def dpre_and_rows(mine, other, gate, gram, loss, dec_squares, devices):
+    copy.wait()
+    squares = jnp.sum(pairs * gram[...])
+    lanes = lax.broadcasted_iota(jnp.int32, (1, LANES), 1)
+    row = scalars_ref[0:1, :] + jnp.where(lanes == 0, squares, 0.0)
+    rows_ref[...] = jnp.broadcast_to(row[None], rows_ref.shape)
+
+
+def dpre_and_rows(mine, other, gate, scalars, gram, devices):
     return pl.pallas_call(
         dpre_kernel,
         out_shape=(
             jax.ShapeDtypeStruct(mine.shape, BF16),
             jax.ShapeDtypeStruct((devices, 1, LANES), F32),
         ),
-        in_specs=vmem_specs(4) + [SMEM_SPEC] * 2,
+        in_specs=vmem_specs(4) + [pl.BlockSpec(memory_space=pl.ANY)],
         out_specs=vmem_specs(2),
+        scratch_shapes=[pltpu.VMEM(gram.shape, F32), pltpu.SemaphoreType.DMA],
         compiler_params=SMALL,
-    )(mine, other, gate, gram, loss, dec_squares)
+    )(mine, other, gate, scalars, gram)
 
 
 def owner_kernel(
-    slots, groups, seg_ref, got_ref, rows_ref, bias_ref, gram_ref, out_ref, loss_ref, sums, errs
+    slots, groups, seg_ref, got_ref, rows_ref, bias_ref, near_ref, far_ref,
+    out_ref, loss_ref, gram_hbm, sums, errs, gram, sem,
 ):
+    gram[...] = near_ref[...] + far_ref[...]
+    copy = pltpu.make_async_copy(gram, gram_hbm, sem)
+    copy.start()
     sums[...] = jnp.zeros_like(sums)
     for c in range(CHIPS):
         for e in range(slots):
@@ -154,9 +163,10 @@
     for c in range(CHIPS):
         for e in range(slots):
             out_ref[c, e] = errs[seg_ref[c, e]]
-
-
-def owner_step(slot_seg, got, rows, bias, gram, groups):
+    copy.wait()
+
+
+def owner_step(slot_seg, got, rows, bias, near_gram, far_gram, groups):
     chips, slots, per, width = got.shape
     vmem = pl.BlockSpec(memory_space=pltpu.VMEM)
     smem = pl.BlockSpec(memory_space=pltpu.SMEM)
@@ -165,41 +175,28 @@
         out_shape=(
             jax.ShapeDtypeStruct(got.shape, BF16),
             jax.ShapeDtypeStruct((1, 1), F32),
+            jax.ShapeDtypeStruct(near_gram.shape, F32),
         ),
-        in_specs=[smem, vmem, vmem, vmem, pl.BlockSpec(memory_space=pl.ANY)],
-        out_specs=(vmem, smem),
+        in_specs=[smem, vmem, vmem, vmem, vmem, vmem],
+        out_specs=(vmem, smem, pl.BlockSpec(memory_space=pl.ANY)),
         scratch_shapes=[
             pltpu.VMEM((groups, per, width), F32),
             pltpu.VMEM((groups, per, width), BF16),
+            pltpu.VMEM(near_gram.shape, F32),
+            pltpu.SemaphoreType.DMA,
         ],
-        compiler_params=pltpu.CompilerParams(vmem_limit_bytes=24 * 2**20),
-    )(slot_seg, got, rows, bias, gram)
+        compiler_params=SMALL,
+    )(slot_seg, got, rows, bias, near_gram, far_gram)
 
 
 def update_kernel(
-    limit, loss_scale, ypos_ref, rows_ref, in_ref, near_ref, far_ref, first_hbm, second_hbm,
+    limit, loss_scale, ypos_ref, rows_ref, in_ref, near_ref, far_ref, first, second,
     new_first_hbm, new_second_hbm, loss_ref, norm_ref,
-    dpre, first, second, new_first, new_second, sems,
+    dpre, new_first, new_second, sems,
 ):
     width = in_ref.shape[1]
     tile = width // UPDATE_STEPS
     block = near_ref.shape[2]
-
-    def copies(i):
-        here = pl.ds(i * tile, tile)
-        pairs = (
-            (first_hbm, first), (second_hbm, second),
-            (new_first, new_first_hbm), (new_second, new_second_hbm),
-        )
-        return [
-            pltpu.make_async_copy(src.at[here, :], dst.at[here, :], sems.at[n, i])
-            for n, (src, dst) in enumerate(pairs)
-        ]
-
-    steps = [copies(i) for i in range(UPDATE_STEPS)]
-    for step in steps:
-        step[0].start()
-        step[1].start()
     for at, ref in ((0, near_ref), (2, far_ref)):
         for b in range(2):
             owner = ypos_ref[0, 0] ^ (at + b)
@@ -212,23 +209,26 @@
     factor = limit / jnp.maximum(norm, limit)
     loss_ref[...] = loss * loss_scale
     norm_ref[...] = norm
-    for i, step in enumerate(steps):
+    copies = []
+    for i in range(UPDATE_STEPS):
         here = slice(i * tile, (i + 1) * tile)
+        rows = pl.ds(i * tile, tile)
         grad = lax.dot_general(
             in_ref[:, here], dpre[...], (((0,), (0,)), ((), ())), preferred_element_type=F32
         )
         clipped = factor * grad
-        step[0].wait()
         new_first[here, :] = (0.9 * first[here, :].astype(F32) + 0.1 * clipped).astype(BF16)
-        step[2].start()
-        step[1].wait()
         new_second[here, :] = (
             0.95 * second[here, :].astype(F32) + 0.05 * clipped * clipped
         ).astype(BF16)
-        step[3].start()
-    for step in steps:
-        step[2].wait()
-        step[3].wait()
+        for n, (src, dst) in enumerate(
+            ((new_first, new_first_hbm), (new_second, new_second_hbm))
+        ):
+            copy = pltpu.make_async_copy(src.at[rows, :], dst.at[rows, :], sems.at[n, i])
+            copy.start()
+            copies.append(copy)
+    for copy in copies:
+        copy.wait()
 
 
 def update(ypos, rows, layer_in, near, far, first, second, limit, loss_scale):
@@ -240,13 +240,13 @@
         functools.partial(update_kernel, limit, loss_scale),
         out_shape=(jax.ShapeDtypeStruct((width, feats), BF16),) * 2
         + (jax.ShapeDtypeStruct((1, 1), F32),) * 2,
-        in_specs=[SMEM_SPEC] + vmem_specs(4) + [hbm] * 2,
+        in_specs=[SMEM_SPEC] + vmem_specs(6),
         out_specs=[hbm] * 2 + vmem_specs(2),
         scratch_shapes=[
-            pltpu.VMEM((tokens, feats), BF16), whole, whole, whole, whole,
-            pltpu.SemaphoreType.DMA((4, UPDATE_STEPS)),
+            pltpu.VMEM((tokens, feats), BF16), whole, whole,
+            pltpu.SemaphoreType.DMA((2, UPDATE_STEPS)),
         ],
-        compiler_params=SMALL,
+        compiler_params=pltpu.CompilerParams(vmem_limit_bytes=13 * 2**20),
     )(ypos, rows, layer_in, near, far, first, second)
 
 
@@ -325,10 +325,12 @@
         gram = lax.dot_general(
             turned, turned, (((1,), (1,)), ((), ())), preferred_element_type=F32
         )
-        for swap in Y_SWAPS:
-            gram = gram + lax.ppermute(gram, "layer", swap)
+        gram = gram + lax.ppermute(gram, "layer", Y_SWAPS[0])
+        far_gram = lax.ppermute(gram, "layer", Y_SWAPS[1])
         slot_seg = jnp.minimum(chip_first[:, None] + slot_ids[None, :], groups - 1)
-        wanted, loss = owner_step(slot_seg, by_chip, stream_rows, dec_bias, gram, groups)
+        wanted, loss, gram = owner_step(
+            slot_seg, by_chip, stream_rows, dec_bias, gram, far_gram, groups
+        )
         own_err = swap_blocks(wanted, "lat", PLANE_SETS).reshape(CHIPS * slots * per, width)
         other_err = lax.ppermute(own_err, "lat", CORE_SWAP)
 
@@ -358,8 +360,10 @@
     )
     mine = jnp.sum(swap_blocks(parts, "layer", Y_SETS).astype(F32), axis=0)
     other = lax.ppermute(mine, "layer", HI_SWAP)
+    lanes = lax.broadcasted_iota(jnp.int32, (8, LANES), 1)
+    scalars = jnp.where(lanes == 0, dec_squares, jnp.where(lanes == 1, loss, 0.0))
     dpre, rows = dpre_and_rows(
-        mine, other, turned_gate, gram, loss, dec_squares, lat_count * layer_count
+        mine, other, turned_gate, scalars, gram, lat_count * layer_count
     )
     rows = lax.all_to_all(rows, ("lat", "layer"), 0, 0)
     near = jnp.stack([dpre, lax.ppermute(dpre, "layer", Y_SWAPS[0])])

time: 166 us -> 164 us (0.988)
  Pallas kernels: 14.7 us -> 12.3 us
  waiting for transfers between devices: 51.6 us -> 49.8 us
    all_to_all x4, waiting for transfers between devices: 22.5 us -> 19.1 us  [swap_blocks(): return lax.all_to_all(blocks, axis, 0, 0, axis_index_groups=sets)]
    pallas_call x1, Pallas kernels: 3.35 us -> 1.13 us  [dpre_and_rows(): pl.pallas_call(dpre_kernel, out_shape=(jax.ShapeDtypeStruct(mine.shape, B...]
  transfers between devices with their start and end apart: 13 -> 13, of which waited for: 11 -> 12; matrix products, arithmetic and copies ran while one was open for 5% -> 6% of each run, Pallas kernels for 0% -> 0%
where the time goes in v5:
time: 164 us; the launch traced here: 163 us
  starting transfers between devices  54.7 us (33%)
  waiting for transfers between devices  49.8 us (30%)
  blocking collectives  28.3 us (17%)
  Pallas kernels  12.3 us (8%)
  matrix products  7.8 us (5%)
  other arithmetic  4.8 us (3%)
  local copies, waits for them, and re-layouts  3.37 us (2%)
  between operations  1.71 us (1%)
    all_to_all x1, blocking collectives, swap_blocks(): return lax.all_to_all(blocks, axis, 0, 0, axis_index_groups=sets)  28.3 us
    all_to_all x4, starting transfers between devices, swap_blocks(): return lax.all_to_all(blocks, axis, 0, 0, axis_index_groups=sets)  19.4 us
    all_to_all x4, waiting for transfers between devices, swap_blocks(): return lax.all_to_all(blocks, axis, 0, 0, axis_index_groups=sets)  19.1 us
    all_to_all x1, starting transfers between devices, on_device(): rows = lax.all_to_all(rows, ('lat', 'layer'), 0, 0)  12.7 us
    ppermute x1, starting transfers between devices, on_device(): pre_other = lax.ppermute(pre_mine, 'layer', HI_SWAP)  7.02 us
    ppermute x1, waiting for transfers between devices, middle(): gram = gram + lax.ppermute(gram, 'layer', Y_SWAPS[0])  6.91 us
    ppermute x1, waiting for transfers between devices, middle(): far_gram = lax.ppermute(gram, 'layer', Y_SWAPS[1])  6.79 us
    all_to_all x1, waiting for transfers between devices, on_device(): rows = lax.all_to_all(rows, ('lat', 'layer'), 0, 0)  6.78 us
  transfers between devices with their start and end apart: 13, of which 12 were waited for; matrix products, arithmetic and copies ran while one was open for 6% of the time, Pallas kernels for 0%

profile of v5, /device:TPU:1, one launch (start us, length us, event | category | flops | bytes accessed | tf_op | source)
XLA Modules:
  0.0 162.9 jit_solution(5277455897144666066)
XLA Ops:
  0.6 3.1 %shard_map.120 = bf16[256,512]{1,0:T(8,128)(2,1)} custom-call(bf16[256,1792]{1,0:T(8,128)(2,1)} %bitcast.139, bf16[1792,512]{1,0:T(8,128)(2,1)} %bitcast.145), custom_call_target="tpu_custom_call" | custom-call | tf_op jit(solution)/shard_map/pallas_call | solution.py:59
  3.7 5.1 %all-to-all-start.6 = ((bf16[4,64,512]{2,1,0:T(8,128)(2,1)}), bf16[4,64,512]{2,1,0:T(8,128)(2,1)S(1)}, u32[]{:S(2)}, u32[]{:S(2)}) async-start(bf16[4,64,512]{2,1,0:T(8,128)(2,1)} %bitcast.152), calls=%async_computation.6 | async-start | bytes 524288 | tf_op jit(solution)/shard_map/all_to_all | solution.py:26
  9.3 0.6 dynamic_slice.45
  9.9 1.0 pad_maximum_fusion.in_ref
  10.9 1.1 fusion.60
  12.0 0.7 broadcast_subtract_fusion
  12.7 1.8 %all-to-all-done.6 = bf16[4,64,512]{2,1,0:T(8,128)(2,1)S(1)} async-done(((bf16[4,64,512]{2,1,0:T(8,128)(2,1)}), bf16[4,64,512]{2,1,0:T(8,128)(2,1)S(1)}, u32[]{:S(2)}, u32[]{:S(2)}) %all-to-all-start.6) | async-done | bytes 262176 | tf_op jit(solution)/shard_map/all_to_all | solution.py:26
  14.5 7.0 %collective-permute-start.12 = (f32[64,512]{1,0:T(8,128)S(1)}, f32[64,512]{1,0:T(8,128)S(1)}, u32[]{:S(2)}, u32[]{:S(2)}) collective-permute-start(f32[64,512]{1,0:T(8,128)S(1)} %convert_reduce_fusion.1.mine_ref), channel_id=1, source_target_pairs={{0,4},{1,5},{2,6},{3,7},{4,0},{5,1},{6,2},{7,3},{8,12},{9,13},{10,... | collective-permute-start | bytes 393224 | tf_op jit(solution)/shard_map/ppermute | solution.py:302
  21.5 0.6 subtract_reduce_fusion
  22.8 1.1 collective-permute-done.12.other_ref
  23.9 0.7 shard_map.121
  24.7 3.4 %all-to-all-start.7 = ((bf16[4,64,512]{2,1,0:T(8,128)(2,1)}), bf16[4,64,512]{2,1,0:T(8,128)(2,1)S(1)}, u32[]{:S(2)}, u32[]{:S(2)}) async-start(bf16[4,64,512]{2,1,0:T(8,128)(2,1)} %shard_map.121), calls=%async_computation.7 | async-start | bytes 524288 | tf_op jit(solution)/shard_map/all_to_all | solution.py:26
  28.1 0.8 bitcast_convert_fusion
  28.8 4.7 %all-to-all-done.7 = bf16[4,64,512]{2,1,0:T(8,128)(2,1)S(1)} async-done(((bf16[4,64,512]{2,1,0:T(8,128)(2,1)}), bf16[4,64,512]{2,1,0:T(8,128)(2,1)S(1)}, u32[]{:S(2)}, u32[]{:S(2)}) %all-to-all-start.7) | async-done | bytes 262176 | tf_op jit(solution)/shard_map/all_to_all | solution.py:26
  33.6 78.2 %conditional.1 = (bf16[4,256,128]{2,1,0:T(8,128)(2,1)}, f32[256,256]{1,0:T(8,128)S(1)}, f32[1,1]{1,0:T(1,128)}, f32[]{:T(128)}) conditional(s32[]{:T(128)} %clamp.11, (s32[512]{0:T(512)S(1)}, s32[16]{0:T(128)S(1)}, s32[]{:T(128)}, bf16[256,512]{1,0:T(8,128)(2,1)S(1)}, bf16[512,1792]{1,0:T(8,128)(2,1)S(1)}, /*index=5*/s32[]{:T(128)}, ...), branch_computations={%region_5.9_spmd, %region_9.13_spmd, %region_13.17_spmd} | conditional | flops 12503812096 | bytes 103166816 | solution.py:358
  33.8 0.6 convolution_convert_fusion
  34.4 4.9 %collective-permute-start = (bf16[256,1792]{1,0:T(8,128)(2,1)S(1)}, bf16[256,1792]{1,0:T(8,128)(2,1)S(1)}, u32[]{:S(2)}, u32[]{:S(2)}) collective-permute-start(bf16[256,1792]{1,0:T(8,128)(2,1)S(1)} %convolution_convert_fusion), channel_id=1, source_target_pairs={{0,8},{8,0},{16,24},{24,16},{32,40},{40,32},{48,56},{56,48},{64,72... | collective-permute-start | bytes 2752520 | tf_op jit(solution)/shard_map/cond/branch_0_fun/ppermute | solution.py:320
  39.3 2.1 %collective-permute-done = bf16[256,1792]{1,0:T(8,128)(2,1)S(1)} collective-permute-done((bf16[256,1792]{1,0:T(8,128)(2,1)S(1)}, bf16[256,1792]{1,0:T(8,128)(2,1)S(1)}, u32[]{:S(2)}, u32[]{:S(2)}) %collective-permute-start) | collective-permute-done | bytes 917536 | tf_op jit(solution)/shard_map/cond/branch_0_fun/ppermute | solution.py:320
  41.4 1.6 add_convert_fusion
  43.0 7.4 %all-to-all-start = ((bf16[16,2,8,1792]{3,2,1,0:T(8,128)(2,1)}), bf16[16,2,8,1792]{3,2,1,0:T(8,128)(2,1)S(1)}, u32[]{:S(2)}, u32[]{:S(2)}) async-start(bf16[16,2,8,1792]{3,2,1,0:T(8,128)(2,1)} %bitcast.140), calls=%async_computation | async-start | bytes 1835008 | tf_op jit(solution)/shard_map/cond/branch_0_fun/all_to_all | solution.py:26
  50.3 1.9 %fusion.61 = f32[256,256]{1,0:T(8,128)S(1)} fusion(bf16[256,1792]{1,0:T(8,128)(2,1)} %get-tuple-element.68), kind=kOutput, calls=%fused_computation.99 | convolution fusion | flops 234881024 | bytes 1179648 | tf_op jit(solution)/shard_map/cond/branch_0_fun/dot_general | solution.py:325
  52.2 0.4 collective-permute-start.1
  52.6 6.9 %collective-permute-done.1 = f32[256,256]{1,0:T(8,128)S(1)} collective-permute-done((f32[256,256]{1,0:T(8,128)S(1)}, f32[256,256]{1,0:T(8,128)S(1)}, u32[]{:S(2)}, u32[]{:S(2)}) %collective-permute-start.1) | collective-permute-done | bytes 262176 | tf_op jit(solution)/shard_map/cond/branch_0_fun/ppermute | solution.py:328
  59.5 1.0 collective-permute-start.2
  60.6 6.8 %collective-permute-done.2.far_ref = f32[256,256]{1,0:T(8,128)S(1)} collective-permute-done((f32[256,256]{1,0:T(8,128)S(1)}, f32[256,256]{1,0:T(8,128)S(1)}, u32[]{:S(2)}, u32[]{:S(2)}) %collective-permute-start.2) | collective-permute-done | bytes 262176 | tf_op jit(solution)/shard_map/cond/branch_0_fun/ppermute | solution.py:329
  67.4 7.1 %all-to-all-done.got_ref = bf16[16,2,8,1792]{3,2,1,0:T(8,128)(2,1)S(1)} async-done(((bf16[16,2,8,1792]{3,2,1,0:T(8,128)(2,1)}), bf16[16,2,8,1792]{3,2,1,0:T(8,128)(2,1)S(1)}, u32[]{:S(2)}, u32[]{:S(2)}) %all-to-all-start) | async-done | bytes 917536 | tf_op jit(solution)/shard_map/cond/branch_0_fun/all_to_all | solution.py:26
  74.5 1.7 %branch_0_fun.2 = (bf16[16,2,8,1792]{3,2,1,0:T(8,128)(2,1)S(1)}, f32[1,1]{1,0:T(1,128)}, f32[256,256]{1,0:T(8,128)S(1)}) custom-call(s32[16,2]{1,0:T(8,128)S(1)} %add_minimum_fusion.seg_ref, bf16[16,2,8,1792]{3,2,1,0:T(8,128)(2,1)S(1)} %all-to-all-done.got_ref, f32[8,1792]{1,0:T(8,128)S(1)} %get-tuple-element.66.rows_ref, ...), custom_call_target="tpu_custom_call" | custom-call | tf_op jit(solution)/shard_map/cond/branch_0_fun/pallas_call | solution.py:173
  76.3 28.3 %all_to_all.44 = bf16[16,2,8,1792]{3,2,1,0:T(8,128)(2,1)S(1)} all-to-all(bf16[16,2,8,1792]{3,2,1,0:T(8,128)(2,1)S(1)} %get-tuple-element.69), channel_id=1, replica_groups={{0,16,32,48,64,80,96,112,128,144,160,176,192,208,224,240},{8,24,40,56,7..., dimensions={0} | all-to-all | bytes 1835008 | tf_op jit(solution)/shard_map/cond/branch_0_fun/all_to_all | solution.py:26
  104.6 1.7 %collective-permute-start.3 = (bf16[256,1792]{1,0:T(8,128)(2,1)S(1)}, bf16[256,1792]{1,0:T(8,128)(2,1)S(1)}, u32[]{:S(2)}, u32[]{:S(2)}) collective-permute-start(bf16[256,1792]{1,0:T(8,128)(2,1)S(1)} %bitcast.155), channel_id=1, source_target_pairs={{0,8},{8,0},{16,24},{24,16},{32,40},{40,32},{48,56},{56,48},{64,72... | collective-permute-start | bytes 2752520 | tf_op jit(solution)/shard_map/cond/branch_0_fun/ppermute | solution.py:335
  106.3 0.5 fusion.14
  106.8 0.7 fusion.9
  107.5 0.9 collective-permute-done.3
  108.4 0.7 fusion.62
  109.1 0.8 branch_0_fun.3
  109.9 1.9 %multiply_reduce_fusion = f32[]{:T(128)} fusion(f32[512,512]{1,0:T(8,128)S(1)} %fusion.14, bf16[256,1792]{1,0:T(8,128)(2,1)S(1)} %collective-permute-done.3, bf16[256,1792]{1,0:T(8,128)(2,1)S(1)} %bitcast.156), kind=kOutput, calls=%fused_computation.10 | convolution fusion | flops 943718400 | bytes 2883588 | tf_op jit(solution)/shard_map/cond/branch_0_fun/dot_general | solution.py:347
  111.7 3.5 %all-to-all-start.8 = ((bf16[4,256,128]{2,1,0:T(8,128)(2,1)}), bf16[4,256,128]{2,1,0:T(8,128)(2,1)S(1)}, u32[]{:S(2)}, u32[]{:S(2)}) async-start(bf16[4,256,128]{2,1,0:T(8,128)(2,1)} %get-tuple-element.114), calls=%async_computation.8 | async-start | bytes 524288 | tf_op jit(solution)/shard_map/all_to_all | solution.py:26
  115.3 0.6 compare_select_fusion
  115.9 5.5 %all-to-all-done.8 = bf16[4,256,128]{2,1,0:T(8,128)(2,1)S(1)} async-done(((bf16[4,256,128]{2,1,0:T(8,128)(2,1)}), bf16[4,256,128]{2,1,0:T(8,128)(2,1)S(1)}, u32[]{:S(2)}, u32[]{:S(2)}) %all-to-all-start.8) | async-done | bytes 262176 | tf_op jit(solution)/shard_map/all_to_all | solution.py:26
  121.4 4.3 %collective-permute-start.13 = (f32[256,128]{1,0:T(8,128)S(1)}, f32[256,128]{1,0:T(8,128)S(1)}, u32[]{:S(2)}, u32[]{:S(2)}) collective-permute-start(f32[256,128]{1,0:T(8,128)S(1)} %convert_reduce_fusion.mine_ref), channel_id=1, source_target_pairs={{0,4},{1,5},{2,6},{3,7},{4,0},{5,1},{6,2},{7,3},{8,12},{9,13},{10,... | collective-permute-start | bytes 393224 | tf_op jit(solution)/shard_map/ppermute | solution.py:362
  125.7 0.6 broadcast_select_fusion.6.scalars_ref
  126.3 3.0 %collective-permute-done.13.other_ref = f32[256,128]{1,0:T(8,128)S(1)} collective-permute-done((f32[256,128]{1,0:T(8,128)S(1)}, f32[256,128]{1,0:T(8,128)S(1)}, u32[]{:S(2)}, u32[]{:S(2)}) %collective-permute-start.13) | collective-permute-done | bytes 131104 | tf_op jit(solution)/shard_map/ppermute | solution.py:362
  129.3 1.1 shard_map.122
  130.8 12.7 %all-to-all-start.9 = ((f32[256,1,128]{2,1,0:T(1,128)}), f32[256,1,128]{2,1,0:T(1,128)S(1)}, u32[]{:S(2)}, u32[]{:S(2)}) async-start(f32[256,1,128]{2,1,0:T(1,128)} %get-tuple-element.118), calls=%async_computation.9 | async-start | bytes 262144 | tf_op jit(solution)/shard_map/all_to_all | solution.py:368
  143.5 3.0 %collective-permute-start.15 = (bf16[2,256,128]{2,1,0:T(8,128)(2,1)S(1)}, bf16[2,256,128]{2,1,0:T(8,128)(2,1)S(1)}, u32[]{:S(2)}, u32[]{:S(2)}) collective-permute-start(bf16[2,256,128]{2,1,0:T(8,128)(2,1)S(1)} %pad_maximum_fusion.2.near_ref), channel_id=1, source_target_pairs={{0,2},{1,3},{2,0},{3,1},{4,6},{5,7},{6,4},{7,5},{8,10},{9,11},{10,... | collective-permute-start | bytes 393224 | tf_op jit(solution)/shard_map/ppermute | solution.py:370
  146.5 3.0 %collective-permute-done.15.far_ref = bf16[2,256,128]{2,1,0:T(8,128)(2,1)S(1)} collective-permute-done((bf16[2,256,128]{2,1,0:T(8,128)(2,1)S(1)}, bf16[2,256,128]{2,1,0:T(8,128)(2,1)S(1)}, u32[]{:S(2)}, u32[]{:S(2)}) %collective-permute-start.15) | collective-permute-done | bytes 131104 | tf_op jit(solution)/shard_map/ppermute | solution.py:370
  149.5 6.8 %all-to-all-done.9.rows_ref = f32[256,1,128]{2,1,0:T(1,128)S(1)} async-done(((f32[256,1,128]{2,1,0:T(1,128)}), f32[256,1,128]{2,1,0:T(1,128)S(1)}, u32[]{:S(2)}, u32[]{:S(2)}) %all-to-all-start.9) | async-done | bytes 131104 | tf_op jit(solution)/shard_map/all_to_all | solution.py:368
  156.3 1.5 copy-done.1
  157.8 4.9 %shard_map.123 = (bf16[1792,512]{1,0:T(8,128)(2,1)}, bf16[1792,512]{1,0:T(8,128)(2,1)}, f32[1,1]{1,0:T(1,128)}, f32[1,1]{1,0:T(1,128)}) custom-call(s32[1,1]{1,0:T(1,128)} %bitcast.33.ypos_ref, f32[256,1,128]{2,1,0:T(1,128)S(1)} %all-to-all-done.9.rows_ref, bf16[256,1792]{1,0:T(8,128)(2,1)} %pad_maximum_fusion.in_ref, ...), custom_call_target="tpu_custom_call" | custom-call | tf_op jit(solution)/shard_map/pallas_call | solution.py:239
  (41 shorter events, 1.1 us)
Async XLA Ops:
  0.6 8.3 %copy-start.10 = (bf16[256,1,1792]{2,0,1:T(8,128)(2,1)S(1)}, bf16[256,1,1792]{2,0,1:T(8,128)(2,1)}, u32[]{:S(2)}) copy-start(bf16[256,1,1792]{2,0,1:T(8,128)(2,1)} %param.12) | copy-start | bytes 2752516
  3.7 5.3 %copy-start.16 = (s32[256,512]{1,0:T(8,128)S(1)}, s32[256,512]{1,0:T(8,128)}, u32[]{:S(2)}) copy-start(s32[256,512]{1,0:T(8,128)} %param.17) | copy-start | bytes 1572868
  3.7 5.4 %copy-start.22 = (s32[5]{0:T(128)S(1)}, s32[5]{0:T(128)}, u32[]{:S(2)}) copy-start(s32[5]{0:T(128)} %param.18) | copy-start | bytes 64
  3.7 10.7 %all-to-all-start.6 = ((bf16[4,64,512]{2,1,0:T(8,128)(2,1)}), bf16[4,64,512]{2,1,0:T(8,128)(2,1)S(1)}, u32[]{:S(2)}, u32[]{:S(2)}) async-start(bf16[4,64,512]{2,1,0:T(8,128)(2,1)} %bitcast.152), calls=%async_computation.6 | async-start | bytes 524288 | tf_op jit(solution)/shard_map/all_to_all | solution.py:26
  9.0 14.9 %copy-start.2 = (f32[512]{0:T(512)S(1)}, f32[512]{0:T(512)}, u32[]{:S(2)}) copy-start(f32[512]{0:T(512)} %param.14) | copy-start | bytes 6148
  9.1 0.8 copy-start.11
  9.9 23.7 %copy-start.3 = (bf16[512,1,1792]{2,0,1:T(8,128)(2,1)S(1)}, bf16[512,1,1792]{2,0,1:T(8,128)(2,1)}, u32[]{:S(2)}) copy-start(bf16[512,1,1792]{2,0,1:T(8,128)(2,1)} %param.15) | copy-start | bytes 5505028
  9.9 23.7 %copy-start.21 = (f32[1,1792]{1,0:T(1,128)S(1)}, f32[1,1792]{1,0:T(1,128)}, u32[]{:S(2)}) copy-start(f32[1,1792]{1,0:T(1,128)} %param.16) | copy-start | bytes 21508
  14.5 9.5 %collective-permute-start.12 = (f32[64,512]{1,0:T(8,128)S(1)}, f32[64,512]{1,0:T(8,128)S(1)}, u32[]{:S(2)}, u32[]{:S(2)}) collective-permute-start(f32[64,512]{1,0:T(8,128)S(1)} %convert_reduce_fusion.1.mine_ref), channel_id=1, source_target_pairs={{0,4},{1,5},{2,6},{3,7},{4,0},{5,1},{6,2},{7,3},{8,12},{9,13},{10,... | collective-permute-start | bytes 393224 | tf_op jit(solution)/shard_map/ppermute | solution.py:302
  24.7 8.9 %all-to-all-start.7 = ((bf16[4,64,512]{2,1,0:T(8,128)(2,1)}), bf16[4,64,512]{2,1,0:T(8,128)(2,1)S(1)}, u32[]{:S(2)}, u32[]{:S(2)}) async-start(bf16[4,64,512]{2,1,0:T(8,128)(2,1)} %shard_map.121), calls=%async_computation.7 | async-start | bytes 524288 | tf_op jit(solution)/shard_map/all_to_all | solution.py:26
  33.6 7.8 %copy-start.4 = (bf16[512,1792]{1,0:T(8,128)(2,1)}, bf16[512,1792]{1,0:T(8,128)(2,1)S(1)}, u32[]{:S(2)}) copy-start(bf16[512,1792]{1,0:T(8,128)(2,1)S(1)} %get-tuple-element.62) | copy-start | bytes 5505028 | tf_op jit(solution)/shard_map/cond
  34.4 7.0 %collective-permute-start = (bf16[256,1792]{1,0:T(8,128)(2,1)S(1)}, bf16[256,1792]{1,0:T(8,128)(2,1)S(1)}, u32[]{:S(2)}, u32[]{:S(2)}) collective-permute-start(bf16[256,1792]{1,0:T(8,128)(2,1)S(1)} %convolution_convert_fusion), channel_id=1, source_target_pairs={{0,8},{8,0},{16,24},{24,16},{32,40},{40,32},{48,56},{56,48},{64,72... | collective-permute-start | bytes 2752520 | tf_op jit(solution)/shard_map/cond/branch_0_fun/ppermute | solution.py:320
  43.0 31.6 %all-to-all-start = ((bf16[16,2,8,1792]{3,2,1,0:T(8,128)(2,1)}), bf16[16,2,8,1792]{3,2,1,0:T(8,128)(2,1)S(1)}, u32[]{:S(2)}, u32[]{:S(2)}) async-start(bf16[16,2,8,1792]{3,2,1,0:T(8,128)(2,1)} %bitcast.140), calls=%async_computation | async-start | bytes 1835008 | tf_op jit(solution)/shard_map/cond/branch_0_fun/all_to_all | solution.py:26
  52.2 7.3 %collective-permute-start.1 = (f32[256,256]{1,0:T(8,128)S(1)}, f32[256,256]{1,0:T(8,128)S(1)}, u32[]{:S(2)}, u32[]{:S(2)}) collective-permute-start(f32[256,256]{1,0:T(8,128)S(1)} %fusion.61), channel_id=1, source_target_pairs={{0,1},{1,0},{2,3},{3,2},{4,5},{5,4},{6,7},{7,6},{8,9},{9,8},{10,11... | collective-permute-start | bytes 786440 | tf_op jit(solution)/shard_map/cond/branch_0_fun/ppermute | solution.py:328
  59.5 7.9 %collective-permute-start.2 = (f32[256,256]{1,0:T(8,128)S(1)}, f32[256,256]{1,0:T(8,128)S(1)}, u32[]{:S(2)}, u32[]{:S(2)}) collective-permute-start(f32[256,256]{1,0:T(8,128)S(1)} %add.106.near_ref), channel_id=1, source_target_pairs={{0,2},{1,3},{2,0},{3,1},{4,6},{5,7},{6,4},{7,5},{8,10},{9,11},{10,... | collective-permute-start | bytes 786440 | tf_op jit(solution)/shard_map/cond/branch_0_fun/ppermute | solution.py:329
  76.3 30.5 %copy-start.5 = (bf16[512,1792]{1,0:T(8,128)(2,1)S(1)}, bf16[512,1792]{1,0:T(8,128)(2,1)}, u32[]{:S(2)}) copy-start(bf16[512,1792]{1,0:T(8,128)(2,1)} %copy-done.4) | copy-start | bytes 5505028 | tf_op jit(solution)/shard_map/cond
  104.6 3.8 %collective-permute-start.3 = (bf16[256,1792]{1,0:T(8,128)(2,1)S(1)}, bf16[256,1792]{1,0:T(8,128)(2,1)S(1)}, u32[]{:S(2)}, u32[]{:S(2)}) collective-permute-start(bf16[256,1792]{1,0:T(8,128)(2,1)S(1)} %bitcast.155), channel_id=1, source_target_pairs={{0,8},{8,0},{16,24},{24,16},{32,40},{40,32},{48,56},{56,48},{64,72... | collective-permute-start | bytes 2752520 | tf_op jit(solution)/shard_map/cond/branch_0_fun/ppermute | solution.py:335
  111.7 44.6 %copy-start = (bf16[1,1792,512]{2,1,0:T(8,128)(2,1)S(1)}, bf16[1,1792,512]{2,1,0:T(8,128)(2,1)}, u32[]{:S(2)}) copy-start(bf16[1,1792,512]{2,1,0:T(8,128)(2,1)} %param.19) | copy-start | bytes 5505028
  111.7 9.6 %all-to-all-start.8 = ((bf16[4,256,128]{2,1,0:T(8,128)(2,1)}), bf16[4,256,128]{2,1,0:T(8,128)(2,1)S(1)}, u32[]{:S(2)}, u32[]{:S(2)}) async-start(bf16[4,256,128]{2,1,0:T(8,128)(2,1)} %get-tuple-element.114), calls=%async_computation.8 | async-start | bytes 524288 | tf_op jit(solution)/shard_map/all_to_all | solution.py:26
  121.4 7.9 %collective-permute-start.13 = (f32[256,128]{1,0:T(8,128)S(1)}, f32[256,128]{1,0:T(8,128)S(1)}, u32[]{:S(2)}, u32[]{:S(2)}) collective-permute-start(f32[256,128]{1,0:T(8,128)S(1)} %convert_reduce_fusion.mine_ref), channel_id=1, source_target_pairs={{0,4},{1,5},{2,6},{3,7},{4,0},{5,1},{6,2},{7,3},{8,12},{9,13},{10,... | collective-permute-start | bytes 393224 | tf_op jit(solution)/shard_map/ppermute | solution.py:362
  130.5 13.1 %collective-permute-start.14 = (bf16[256,128]{1,0:T(8,128)(2,1)S(1)}, bf16[256,128]{1,0:T(8,128)(2,1)S(1)}, u32[]{:S(2)}, u32[]{:S(2)}) collective-permute-start(bf16[256,128]{1,0:T(8,128)(2,1)S(1)} %get-tuple-element.119), channel_id=1, source_target_pairs={{0,1},{1,0},{2,3},{3,2},{4,5},{5,4},{6,7},{7,6},{8,9},{9,8},{10,11... | collective-permute-start | bytes 196616 | tf_op jit(solution)/shard_map/ppermute | solution.py:369
  130.8 25.5 %all-to-all-start.9 = ((f32[256,1,128]{2,1,0:T(1,128)}), f32[256,1,128]{2,1,0:T(1,128)S(1)}, u32[]{:S(2)}, u32[]{:S(2)}) async-start(f32[256,1,128]{2,1,0:T(1,128)} %get-tuple-element.118), calls=%async_computation.9 | async-start | bytes 262144 | tf_op jit(solution)/shard_map/all_to_all | solution.py:368
  143.5 6.0 %collective-permute-start.15 = (bf16[2,256,128]{2,1,0:T(8,128)(2,1)S(1)}, bf16[2,256,128]{2,1,0:T(8,128)(2,1)S(1)}, u32[]{:S(2)}, u32[]{:S(2)}) collective-permute-start(bf16[2,256,128]{2,1,0:T(8,128)(2,1)S(1)} %pad_maximum_fusion.2.near_ref), channel_id=1, source_target_pairs={{0,2},{1,3},{2,0},{3,1},{4,6},{5,7},{6,4},{7,5},{8,10},{9,11},{10,... | collective-permute-start | bytes 393224 | tf_op jit(solution)/shard_map/ppermute | solution.py:370
  156.3 1.5 copy-start.1
